TPU v7x, 32 devices: a whole 2x2x4 slice. The times are simulated.
32 devices in a mesh: section: 2 (over x), dp: 4 (over z), tensor: 4 (over y, core).
Axes of the slice: x: 2, y: 2, z: 4, core: 2. Of those that a mesh axis runs over, the one named last changes fastest.
Arguments:
- block_input: bfloat16 [3840, 2048], P('dp'), may hold values from -6 to 6
- out_grad: bfloat16 [3840, 2048], P('dp'), may hold values from -6 to 6
- seq_lengths: int32 [4, 4], P('dp'), may hold values from 0 to 960, as said below
- attn_gains: bfloat16 [2, 2048], P('section'), may hold values from 0.099609375 to 1.8984375
- attn_weights: bfloat16 [2, 2, 2048, 2048], P('section', None, None, 'tensor')
- ffn_gain: bfloat16 [2048], replicated, may hold values from 0.099609375 to 1.8984375
- gate_weight: bfloat16 [2048, 5504], P(None, ('section', 'tensor')), may hold values from -0.125 to 0.125
- up_weight: bfloat16 [2048, 5504], P(None, ('section', 'tensor')), may hold values from -0.125 to 0.125
- down_weight: bfloat16 [5504, 2048], P(('section', 'tensor')), may hold values from -0.078125 to 0.078125
Outputs:
- block_output: bfloat16 [3840, 2048], P('dp', ('section', 'tensor'))
- input_grad: bfloat16 [3840, 2048], P('dp', ('section', 'tensor'))
- attn_gains_grad: float32 [2, 2048], P('section')
- attn_weights_grad: float32 [2, 2, 2048, 2048], P('section', None, None, 'tensor')
- ffn_gain_grad: float32 [2048], replicated
- gate_weight_grad: float32 [2048, 5504], P(None, ('section', 'tensor'))
- up_weight_grad: float32 [2048, 5504], P(None, ('section', 'tensor'))
- down_weight_grad: float32 [5504, 2048], P(('section', 'tensor'))
- activation_rms: float32 [2], replicated
Inputs may be any that keep to these rules, and one draw needn't show every extreme that they name: `seq_lengths`: row g lists the lengths of group g's sequences, packed in order from the group's first token slot: 1 to 4 positive entries first, zeros after, summing to at most 960; slots past the sum are padding. Some row holds one sequence of 960.
All inputs are finite; a program needn't handle non-finite values.
Results may differ from a plain program's by a relative error of at most 0.017.
Values may be sent and summed in bfloat16 or wider, within the bound.
No kernel may reach another device: no remote copies, remote signals or barrier semaphores. Data moves between devices by JAX's collectives and lax.ppermute only.
A program may use at most 256 MiB of HBM per device.

v0:
```python
import jax
import jax.numpy as jnp
from jax import lax
from jax.sharding import PartitionSpec as P

HEAD_SIZE = 128


epsilon = 1e-06
negative = -1e30


def spread(value, axis, source):
    kept = jnp.where(lax.axis_index(axis) == source, value, 0).astype(value.dtype)
    return lax.psum(kept, axis)


def passed_along(value, axis, steps):
    count = lax.axis_size(axis)
    initial, last = (max(0, -steps), min(count, count - steps))
    return lax.ppermute(value, axis, [(source, source + steps) for source in range(initial, last)])


def segment_ids(length_row, tok_count):
    seq_ends = jnp.cumsum(length_row)
    places = jnp.arange(tok_count, dtype=jnp.int32)
    return jnp.sum((places[:, None] >= seq_ends[None, :]).astype(jnp.int32), axis=1)


def norm_back(source, inverse, gain_vec, grad_in):
    scaled = grad_in * gain_vec
    inner_mean = jnp.mean(scaled * source, axis=-1, keepdims=True)
    return inverse * scaled - source * inverse**3 * inner_mean


def contract_rows(left_mat, right_mat):
    return lax.dot_general(
        left_mat, right_mat, (((0,), (0,)), ((), ())), preferred_element_type=jnp.float32
    )


def contract_cols(left_mat, right_mat):
    return lax.dot_general(
        left_mat, right_mat, (((1,), (1,)), ((), ())), preferred_element_type=jnp.float32
    )


def block_size(tok_count):
    size_rows = tok_count
    while size_rows > 1024 and size_rows % 2 == 0:
        size_rows = size_rows // 2
    return size_rows


def masked_scores(q_block, k_heads, seg_ids):
    score_scale = q_block.shape[2] ** (-0.5)
    scores = (
        jnp.einsum("qhd,khd->hqk", q_block, k_heads, preferred_element_type=jnp.float32)
        * score_scale
    )
    places = jnp.arange(seg_ids.shape[0], dtype=jnp.int32)
    allowed = (seg_ids[:, None] == seg_ids[None, :]) & (places[None, :] <= places[:, None])
    return jnp.where(allowed[None], scores, negative)


def attend_forward(queries, keys, values, seg_ids, head_dim):
    tok_count = queries.shape[0]
    heads_local = queries.shape[1] // head_dim
    q_heads = queries.reshape(tok_count, heads_local, head_dim)
    k_heads = keys.reshape(tok_count, heads_local, head_dim)
    v_heads = values.reshape(tok_count, heads_local, head_dim)
    block_rows = block_size(tok_count)
    scores = masked_scores(q_heads, k_heads, seg_ids)
    maximum = jnp.max(scores, axis=-1, keepdims=True)
    exponent = jnp.exp(scores - maximum)
    row_total = jnp.sum(exponent, axis=-1, keepdims=True)
    probs_low = (exponent / row_total).astype(jnp.bfloat16)
    block_out = jnp.einsum("hqk,khd->qhd", probs_low, v_heads, preferred_element_type=jnp.float32)
    outputs = [block_out.astype(jnp.bfloat16).reshape(block_rows, heads_local * head_dim)]
    lse_parts = [(maximum + jnp.log(row_total))[..., 0]]
    return (jnp.concatenate(outputs, axis=0), jnp.concatenate(lse_parts, axis=1))


def attend_backward(queries, keys, values, grad_out, seg_ids, log_total, head_dim):
    tok_count = queries.shape[0]
    heads_local = queries.shape[1] // head_dim
    score_scale = head_dim ** (-0.5)
    q_heads = queries.reshape(tok_count, heads_local, head_dim)
    k_heads = keys.reshape(tok_count, heads_local, head_dim)
    v_heads = values.reshape(tok_count, heads_local, head_dim)
    g_heads = grad_out.reshape(tok_count, heads_local, head_dim)
    block_rows = block_size(tok_count)
    grad_keys = jnp.zeros((tok_count, heads_local, head_dim), jnp.float32)
    grad_values = jnp.zeros((tok_count, heads_local, head_dim), jnp.float32)
    scores = masked_scores(q_heads, k_heads, seg_ids)
    prob_rows = jnp.exp(scores - log_total[:, 0:block_rows, None])
    probs_low = prob_rows.astype(jnp.bfloat16)
    grad_probs = jnp.einsum("qhd,khd->hqk", g_heads, v_heads, preferred_element_type=jnp.float32)
    inner_sum = jnp.sum(prob_rows * grad_probs, axis=-1, keepdims=True)
    grad_scores = (prob_rows * (grad_probs - inner_sum)).astype(jnp.bfloat16)
    block_q = (
        jnp.einsum("hqk,khd->qhd", grad_scores, k_heads, preferred_element_type=jnp.float32)
        * score_scale
    )
    grad_queries = [block_q]
    grad_keys = (
        grad_keys
        + jnp.einsum("hqk,qhd->khd", grad_scores, q_heads, preferred_element_type=jnp.float32)
        * score_scale
    )
    grad_values = grad_values + jnp.einsum(
        "hqk,qhd->khd", probs_low, g_heads, preferred_element_type=jnp.float32
    )
    flat_width = heads_local * head_dim
    query_grad = (
        jnp.concatenate(grad_queries, axis=0).reshape(tok_count, flat_width).astype(jnp.bfloat16)
    )
    kv_grad = jnp.stack(
        [grad_keys.reshape(tok_count, flat_width), grad_values.reshape(tok_count, flat_width)]
    ).astype(jnp.bfloat16)
    return (query_grad, kv_grad)


def shards(
    block_input,
    out_grad,
    seq_lengths,
    attn_gains,
    attn_weights,
    ffn_gain,
    gate_weight,
    up_weight,
    down_weight,
):
    tok_count, model_width = block_input.shape
    head_dim = HEAD_SIZE
    section_pos = lax.axis_index("section")
    is_first = section_pos == 0
    group_count = lax.axis_size("section") * lax.axis_size("tensor")
    share_part = 1.0 / group_count
    column_pos = section_pos * lax.axis_size("tensor") + lax.axis_index("tensor")
    columns = model_width // group_count
    col_start = column_pos * columns
    seg_ids = segment_ids(seq_lengths[0], tok_count)
    is_valid = (seg_ids < seq_lengths.shape[1]).astype(jnp.float32)[:, None]
    inputs_f = block_input.astype(jnp.float32)
    inverse = lax.rsqrt(jnp.mean(inputs_f * inputs_f, axis=-1, keepdims=True) + epsilon)
    gain_row = attn_gains[0].astype(jnp.float32)
    normed = (inputs_f * inverse * gain_row).astype(jnp.bfloat16)
    w_first = attn_weights[0, 0]
    w_second = attn_weights[0, 1]
    projected = jnp.dot(normed, w_first, preferred_element_type=jnp.float32).astype(jnp.bfloat16)
    second_proj = lax.cond(
        is_first,
        lambda: jnp.dot(normed, w_second, preferred_element_type=jnp.float32).astype(jnp.bfloat16),
        lambda: jnp.zeros_like(projected),
    )
    shared_kv = spread(jnp.stack([projected, second_proj]), "section", 0)
    heads_local = projected.shape[1] // head_dim
    attn_out, log_total = lax.cond(
        is_first,
        lambda: (jnp.zeros_like(projected), jnp.zeros((heads_local, tok_count), jnp.float32)),
        lambda: attend_forward(projected, shared_kv[0], shared_kv[1], seg_ids, head_dim),
    )
    partial_branch = lax.cond(
        is_first,
        lambda: jnp.zeros((tok_count, model_width), jnp.float32),
        lambda: contract_cols(attn_out, w_second),
    )
    gain_ffn = ffn_gain.astype(jnp.float32)
    branch = lax.psum(partial_branch, ("section", "tensor"))
    residual = inputs_f + branch
    resid_inv = lax.rsqrt(jnp.mean(residual * residual, axis=-1, keepdims=True) + epsilon)
    hidden_in = (residual * resid_inv * gain_ffn).astype(jnp.bfloat16)
    branch_cols = lax.dynamic_slice_in_dim(branch, col_start, columns, 1)
    resid_before = residual * share_part
    resid_after = 0.0
    gate_act = jnp.dot(hidden_in, gate_weight, preferred_element_type=jnp.float32)
    up_act = jnp.dot(hidden_in, up_weight, preferred_element_type=jnp.float32)
    gate_sig = jax.nn.sigmoid(gate_act)
    silu_val = gate_act * gate_sig
    hidden = (silu_val * up_act).astype(jnp.bfloat16)
    ffn_part = jnp.dot(hidden, down_weight, preferred_element_type=jnp.float32)
    output_sum = (
        lax.psum_scatter(
            (ffn_part + resid_before).astype(jnp.bfloat16),
            ("section", "tensor"),
            scatter_dimension=1,
            tiled=True,
        ).astype(jnp.float32)
        + resid_after
    )
    block_output = output_sum.astype(jnp.bfloat16)
    output_sq = jnp.sum(output_sum * output_sum * is_valid)
    branch_sq = jnp.sum(branch_cols * branch_cols * is_valid)
    count_term = jnp.where(column_pos == 0, jnp.sum(seq_lengths).astype(jnp.float32), 0.0)
    grad_hidden = contract_cols(out_grad, down_weight)
    grad_up = (grad_hidden * silu_val).astype(jnp.bfloat16)
    grad_gate = (grad_hidden * up_act * gate_sig * (1.0 + gate_act * (1.0 - gate_sig))).astype(
        jnp.bfloat16
    )
    down_grad = contract_rows(hidden, out_grad)
    gate_grad = contract_rows(hidden_in, grad_gate)
    up_grad = contract_rows(hidden_in, grad_up)
    grad_hidden_in = contract_cols(grad_gate, gate_weight) + contract_cols(grad_up, up_weight)
    ffn_gain_term = jnp.sum(grad_hidden_in * residual * resid_inv, axis=0)
    resid_part = norm_back(residual, resid_inv, gain_ffn, grad_hidden_in)
    grad_residual = out_grad.astype(jnp.float32) + lax.psum(resid_part, ("section", "tensor"))
    grad_branch_low = grad_residual.astype(jnp.bfloat16)
    grad_before = grad_residual * share_part
    grad_after = 0.0

    def cross_backward():
        grad_attn_out = jnp.dot(
            grad_branch_low, w_second, preferred_element_type=jnp.float32
        ).astype(jnp.bfloat16)
        return attend_backward(
            projected, shared_kv[0], shared_kv[1], grad_attn_out, seg_ids, log_total, head_dim
        )

    query_grad, kv_grad = lax.cond(
        is_first, lambda: (jnp.zeros_like(projected), jnp.zeros_like(shared_kv)), cross_backward
    )
    returned = passed_along(kv_grad, "section", -1)
    first_grad = jnp.where(is_first, returned[0], query_grad)
    left_second = jnp.where(is_first, normed, grad_branch_low)
    right_second = jnp.where(is_first, returned[1], attn_out)
    w_first_grad = contract_rows(normed, first_grad)
    w_second_grad = contract_rows(left_second, right_second)
    grad_normed = contract_cols(first_grad, w_first)
    grad_normed = grad_normed + lax.cond(
        is_first,
        lambda: contract_cols(returned[1], w_second),
        lambda: jnp.zeros((tok_count, model_width), jnp.float32),
    )
    attn_gain_term = jnp.sum(grad_normed * inputs_f * inverse, axis=0)
    input_part = norm_back(inputs_f, inverse, gain_row, grad_normed) + grad_before
    input_sum = (
        lax.psum_scatter(
            input_part.astype(jnp.bfloat16), ("section", "tensor"), scatter_dimension=1, tiled=True
        ).astype(jnp.float32)
        + grad_after
    )
    input_grad = input_sum.astype(jnp.bfloat16)
    attn_weight_grad = jnp.stack([w_first_grad, w_second_grad])[None]
    attn_weight_grad, gate_grad, up_grad, down_grad = (
        lax.psum(attn_weight_grad.astype(jnp.bfloat16), "dp").astype(jnp.float32),
        lax.psum(gate_grad.astype(jnp.bfloat16), "dp").astype(jnp.float32),
        lax.psum(up_grad.astype(jnp.bfloat16), "dp").astype(jnp.float32),
        lax.psum(down_grad.astype(jnp.bfloat16), "dp").astype(jnp.float32),
    )
    section_rows = jnp.where(
        jnp.arange(2, dtype=jnp.int32)[:, None] == section_pos, attn_gain_term[None, :], 0.0
    )
    gain_terms = jnp.concatenate([section_rows, ffn_gain_term[None, :]], axis=0)
    stat_terms = jnp.stack([output_sq, branch_sq, count_term])
    summed_gains, summed_stats = lax.psum((gain_terms, stat_terms), ("section", "dp", "tensor"))
    attn_gain_grad = lax.dynamic_slice_in_dim(summed_gains, section_pos, 1, 0)
    ffn_gain_grad = summed_gains[2]
    activation_rms = jnp.sqrt(summed_stats[:2] / (summed_stats[2] * model_width))
    return (
        block_output,
        input_grad,
        attn_gain_grad,
        attn_weight_grad,
        ffn_gain_grad,
        gate_grad,
        up_grad,
        down_grad,
        activation_rms,
    )


def solution(mesh):
    placed = (
        P("dp", None),
        P("dp", None),
        P("dp", None),
        P("section", None),
        P("section", None, None, "tensor"),
        P(),
        P(None, ("section", "tensor")),
        P(None, ("section", "tensor")),
        P(("section", "tensor"), None),
    )
    return jax.shard_map(
        shards,
        mesh=mesh,
        in_specs=placed,
        out_specs=(
            P("dp", ("section", "tensor")),
            P("dp", ("section", "tensor")),
            P("section", None),
            P("section", None, None, "tensor"),
            P(),
            P(None, ("section", "tensor")),
            P(None, ("section", "tensor")),
            P(("section", "tensor"), None),
            P(),
        ),
        check_vma=False,
    )
```

profile of v0, /device:TPU:0, one launch (start us, length us, event | category | flops | bytes accessed | tf_op | source)
XLA Modules:
  0.0 1044.3 jit_solution(1023561082317554751)
XLA Ops:
  7.3 3.1 fusion.41
  11.0 3.0 slice_bitcast_fusion
  14.0 1.0 fusion.43
  15.0 1.2 copy-done.22
  16.2 3.2 fusion.68
  19.4 4.7 conditional.5
  19.4 4.7 fusion
  24.1 3.0 maximum_select_fusion
  27.5 61.7 %all-reduce.7.cloned.1.call-done = bf16[2,960,512]{2,1,0:T(8,128)(2,1)} async-done(((bf16[2,960,512]{2,1,0:T(8,128)(2,1)}), bf16[2,960,512]{2,1,0:T(8,128)(2,1)}) %all-reduce.7.cloned.1.call-update) | async-done | bytes 1966096 | tf_op jit(solution)/shard_map/psum | solution.py:15
  89.2 7.8 conditional.6
  95.9 1.0 broadcast.142
  96.9 4.2 conditional.7
  96.9 4.2 broadcast.144
  101.8 156.8 %all-reduce.9.cloned.1.call-done = f32[960,2048]{1,0:T(8,128)} async-done(((f32[960,2048]{1,0:T(8,128)}), f32[960,2048]{1,0:T(8,128)}) %all-reduce.9.cloned.1.call-update) | async-done | bytes 7864336 | tf_op jit(solution)/shard_map/psum | solution.py:171
  258.7 5.4 multiply_reduce_fusion.3
  264.1 0.7 multiply_convert_fusion.3
  264.9 7.2 fusion.81
  272.1 4.7 fusion.82
  276.8 7.2 multiply_convert_fusion.4
  284.0 5.5 fusion.83
  289.5 7.5 multiply_reduce_fusion.1
  297.0 3.9 multiply_subtract_fusion
  301.0 7.3 add_convert_fusion
  308.4 114.1 %all-reduce.11.cloned.1.call-done = f32[960,2048]{1,0:T(8,128)} async-done(((f32[960,2048]{1,0:T(8,128)}), f32[960,2048]{1,0:T(8,128)}) %all-reduce.11.cloned.1.call-update) | async-done | bytes 7864336 | tf_op jit(solution)/shard_map/psum | solution.py:208
  422.5 7.8 fusion.51
  430.4 8.1 conditional.8
  438.5 1.6 collective-permute-start
  440.1 7.9 convolution_convert_fusion.2
  448.0 4.5 convolution_convert_fusion.3
  452.6 4.4 convolution_convert_fusion.4
  457.0 87.8 %collective-permute-done = bf16[2,960,512]{2,1,0:T(8,128)(2,1)S(1)} collective-permute-done((bf16[2,960,512]{2,1,0:T(8,128)(2,1)S(1)}, bf16[2,960,512]{2,1,0:T(8,128)(2,1)S(1)}, u32[]{:S(2)}, u32[]{:S(2)}) %collective-permute-start) | collective-permute-done | bytes 1966112 | tf_op jit(solution)/shard_map/ppermute | solution.py:21
  544.8 2.5 fusion.59
  547.6 2.7 fusion.60
  550.3 2.4 pad_maximum_fusion.1
  552.8 1.5 copy-done.21
  554.3 7.0 conditional.9
  554.5 6.8 fusion.38
  561.4 8.6 fusion.50
  570.0 7.0 fusion.47
  579.0 2.3 multiply_reduce_fusion.5
  581.3 1.4 pad_maximum_fusion.3
  582.8 44.2 %all-reduce = (f32[3,2048]{1,0:T(4,128)S(1)}, f32[3]{0:T(128)S(1)}) all-reduce(f32[3,2048]{1,0:T(4,128)S(1)} %pad_maximum_fusion.2, f32[3]{0:T(128)S(1)} %pad_maximum_fusion.3), channel_id=1, replica_groups=mesh['section'=2,'dp'=4,'tensor'=4] {'section','dp','tensor'}, use_global_device_ids=true, to_apply=%region_26.27 | all-reduce | flops 6147 | bytes 49176 | tf_op jit(solution)/shard_map/psum | solution.py:257
  629.4 354.8 %all-reduce.13.cloned.1.call-done = (bf16[1,2,2048,512]{3,2,1,0:T(8,128)(2,1)}, bf16[2048,688]{0,1:T(8,128)(2,1)}, bf16[2048,688]{0,1:T(8,128)(2,1)}, bf16[688,2048]{1,0:T(8,128)(2,1)}) async-done(((bf16[1,2,2048,512]{3,2,1,0:T(8,128)(2,1)}, bf16[2048,688]{0,1:T(8,128)(2,1)}, bf16[2048,688]{0,1:T(8,128)(2,1)}, bf16[688,2048]{1,0:T(8,128)(2,1)}), (bf16[1,2,2048,512]{3,2,1,0:T(8,128)(2,1)}, ...) | async-done | bytes 12648464 | tf_op jit(solution)/shard_map/psum | solution.py:247
  984.1 6.9 convert_element_type.141
  991.1 3.3 convert_element_type.143
  994.4 3.4 convert_element_type.145
  997.8 3.2 convert_element_type.147
  1001.1 35.9 %reduce-scatter.5.cloned.1.call-done = bf16[960,256]{1,0:T(8,128)(2,1)} async-done(((bf16[960,2048]{1,0:T(8,128)(2,1)}), bf16[960,256]{1,0:T(8,128)(2,1)}) %reduce-scatter.5.cloned.1.call-update) | async-done | bytes 491536 | tf_op jit(solution)/shard_map/reduce_scatter | solution.py:239
  (104 shorter events, 5.6 us)
Async XLA Ops:
  7.2 269.6 %copy-start = (bf16[688,2048]{1,0:T(8,128)(2,1)S(1)}, bf16[688,2048]{1,0:T(8,128)(2,1)}, u32[]{:S(2)}) copy-start(bf16[688,2048]{1,0:T(8,128)(2,1)} %param.27) | copy-start | bytes 8454148
  7.2 3.8 copy-start.30
  7.2 82.0 %all-reduce.7.cloned.1.call-start = ((), (), s32[]{:S(2)}) async-start(), calls=%async_computation.2 | async-start | bytes 3932160 | tf_op jit(solution)/shard_map/psum | solution.py:15
  7.3 6.8 copy-start.3
  11.0 4.0 copy-start.27
  11.0 4.0 copy-start.25
  14.0 2.2 copy-start.22
  16.2 3.2 copy-start.10
  24.1 3.1 copy-start.34
  27.1 231.5 %all-reduce.9.cloned.1.call-start = ((), (), s32[]{:S(2)}) async-start(), calls=%async_computation.3 | async-start | bytes 15728640 | tf_op jit(solution)/shard_map/psum | solution.py:171
  101.2 0.7 copy-start.31
  101.2 321.4 %all-reduce.11.cloned.1.call-start = ((), (), s32[]{:S(2)}) async-start(), calls=%async_computation.5 | async-start | bytes 15728640 | tf_op jit(solution)/shard_map/psum | solution.py:208
  264.1 32.9 %copy-start.2 = (f32[960,2048]{1,0:T(8,128)}, f32[960,2048]{1,0:T(8,128)S(1)}, u32[]{:S(2)}) copy-start(f32[960,2048]{1,0:T(8,128)S(1)} %get-tuple-element.85) | copy-start | bytes 23592964
  264.9 7.2 copy-start.12
  264.9 7.2 copy-start.20
  272.1 4.7 copy-start.5
  276.8 7.2 copy-start.32
  284.0 5.5 copy-start.36
  284.0 5.5 copy-start.16
  300.9 278.0 %reduce-scatter.3.cloned.1.call-start = ((), (), s32[]{:S(2)}) async-start(), calls=%async_computation.4 | async-start | bytes 4423680 | tf_op jit(solution)/shard_map/reduce_scatter | solution.py:185
  308.3 675.8 %all-reduce.13.cloned.1.call-start = ((), (), s32[]{:S(2)}) async-start(), calls=%async_computation.7 | async-start | bytes 25296896 | tf_op jit(solution)/shard_map/psum | solution.py:247
  308.4 122.0 %copy-start.9 = (bf16[2,960,512]{2,1,0:T(8,128)(2,1)S(1)}, bf16[2,960,512]{2,1,0:T(8,128)(2,1)}, u32[]{:S(2)}) copy-start(bf16[2,960,512]{2,1,0:T(8,128)(2,1)} %all-reduce.7.cloned.1.call-done) | copy-start | bytes 5898244
  438.5 9.5 copy-start.23
  438.5 9.5 copy-start.13
  438.5 9.5 copy-start.37
  438.5 106.3 %collective-permute-start = (bf16[2,960,512]{2,1,0:T(8,128)(2,1)S(1)}, bf16[2,960,512]{2,1,0:T(8,128)(2,1)S(1)}, u32[]{:S(2)}, u32[]{:S(2)}) collective-permute-start(bf16[2,960,512]{2,1,0:T(8,128)(2,1)S(1)} %get-tuple-element.70), channel_id=1, source_target_pairs={{16,0},{17,1},{18,2},{19,3},{20,4},{21,5},{22,6},{23,7},{24,8},{25... | collective-permute-start | bytes 5898248 | tf_op jit(solution)/shard_map/ppermute | solution.py:21
  448.0 4.5 copy-start.6
  448.0 4.5 copy-start.38
  452.6 92.3 %copy-start.11 = (bf16[960,2048]{1,0:T(8,128)(2,1)S(1)}, bf16[960,2048]{1,0:T(8,128)(2,1)}, u32[]{:S(2)}) copy-start(bf16[960,2048]{1,0:T(8,128)(2,1)} %copy-done.10) | copy-start | bytes 11796484
  452.6 92.3 %copy-start.24 = (bf16[960,512]{1,0:T(8,128)(2,1)S(1)}, bf16[960,512]{1,0:T(8,128)(2,1)}, u32[]{:S(2)}) copy-start(bf16[960,512]{1,0:T(8,128)(2,1)} %copy-done.23) | copy-start | bytes 2949124
  544.8 2.5 copy-start.33
  544.8 2.8 copy-start.15
  552.7 1.6 copy-start.21
  552.7 484.3 %reduce-scatter.5.cloned.1.call-start = ((), (), s32[]{:S(2)}) async-start(), calls=%async_computation.6 | async-start | bytes 4423680 | tf_op jit(solution)/shard_map/reduce_scatter | solution.py:239
  554.3 7.1 copy-start.26
  554.3 7.1 copy-start.28
  561.3 8.7 copy-start.4
  561.3 8.7 copy-start.7
  561.4 8.7 copy-start.29
  577.0 0.7 copy-start.35
  984.1 6.9 copy-start.19
  991.1 3.3 copy-start.18
  994.4 3.5 copy-start.17
  997.8 39.2 %copy-start.1 = (bf16[688,2048]{1,0:T(8,128)(2,1)S(1)}, bf16[688,2048]{1,0:T(8,128)(2,1)}, u32[]{:S(2)}) copy-start(bf16[688,2048]{1,0:T(8,128)(2,1)} %param.27) | copy-start | bytes 8454148
Sparse Core Ops, SparseCore 0:
  27.3 61.8 all-reduce.6
  101.3 157.3 all-reduce.8
  301.1 121.4 all-reduce.10
  426.9 50.1 reduce-scatter.2
  552.8 431.2 all-reduce.12
  988.1 48.8 reduce-scatter.4
where the time goes:
time: 1050 us; the launch traced here: 1040 us
  waiting for transfers between devices  811 us (77%)
  matrix products  84.6 us (8%)
  other arithmetic  57.1 us (5%)
  blocking collectives  44.2 us (4%)
  between operations  16.3 us (2%)
  loops' own time  14.9 us (1%)
  local copies, waits for them, and re-layouts  14.1 us (1%)
    psum x1, waiting for transfers between devices, shards(): lax.psum(attn_weight_grad.astype(jnp.bfloat16), 'dp').astype(jnp.float32)  355 us
    psum x1, waiting for transfers between devices, shards(): branch = lax.psum(partial_branch, ('section', 'tensor'))  157 us
    psum x1, waiting for transfers between devices, shards(): lax.psum(resid_part, ('section', 'tensor'))  114 us
    ppermute x1, waiting for transfers between devices, passed_along(): lax.ppermute(value, axis, [(source, source + steps) for source in range(i...  87.8 us
    psum x1, waiting for transfers between devices, spread(): return lax.psum(kept, axis)  61.7 us
    psum x1, blocking collectives, shards(): lax.psum((gain_terms, stat_terms), ('section', 'dp', 'tensor'))  44.2 us
    reduce_scatter x1, waiting for transfers between devices, shards(): lax.psum_scatter(input_part.astype(jnp.bfloat16), ('section', 'tensor'),...  35.9 us
    dot_general x5, matrix products, contract_cols(): lax.dot_general(left_mat, right_mat, (((1,), (1,)), ((), ())), preferred_...  35.6 us
  transfers between devices with their start and end apart: 7, of which 6 were waited for; matrix products, arithmetic and copies ran while one was open for 8% of the time, Pallas kernels for 0%

commit v1 on v0

v1 whole, which is shorter than its diff:
```python
import jax
import jax.numpy as jnp
from jax import lax
from jax.sharding import PartitionSpec as P

HEAD_SIZE = 128
epsilon = 1e-06
negative = -1e30
bf16 = jnp.bfloat16
f32 = jnp.float32

SWAP_SECTION = [(0, 1), (1, 0)]
SWAP_LOW = [(i, i ^ 1) for i in range(4)]
SWAP_HIGH = [(i, i ^ 2) for i in range(4)]
SWAP_BOTH = [(i, i ^ 6) for i in range(8)]


def place():
    section, tensor = lax.axis_index("section"), lax.axis_index("tensor")
    return section, tensor // 2, tensor % 2


def pick(blocks, index):
    return lax.dynamic_index_in_dim(blocks, index, 0, keepdims=False)


def swap_low(value):
    return lax.ppermute(value, "tensor", SWAP_LOW)


def swap_high(value):
    return lax.ppermute(value, "tensor", SWAP_HIGH)


def swap_section(value):
    return lax.ppermute(value, "section", SWAP_SECTION)


def swap_both(value):
    return lax.ppermute(value, ("section", "tensor"), SWAP_BOTH)


def scatter_sum(blocks):
    section, high, low = place()
    pairs = blocks.reshape((4, 2) + blocks.shape[1:])
    kept = lax.dynamic_index_in_dim(pairs, low, 1, keepdims=False)
    sent = lax.dynamic_index_in_dim(pairs, 1 - low, 1, keepdims=False)
    half = (kept.astype(f32) + swap_low(sent).astype(f32)).astype(bf16)

    def toward(a, b):
        return pick(half, (section ^ a) * 2 + (high ^ b))

    from_both = swap_both(toward(1, 1))
    from_section = swap_section(toward(1, 0))
    from_high = swap_high(toward(0, 1))
    return (
        toward(0, 0).astype(f32)
        + from_section.astype(f32)
        + from_high.astype(f32)
        + from_both.astype(f32)
    )


def gather_plane(block):
    section, high, low = place()
    found = [
        (swap_both(block), 1, 1),
        (swap_section(block), 1, 0),
        (swap_high(block), 0, 1),
        (block, 0, 0),
    ]
    rows = block.shape[0]
    whole = jnp.zeros((8 * rows, block.shape[1]), block.dtype)
    for value, a, b in found:
        other = swap_low(value)
        chip = ((section ^ a) * 2 + (high ^ b)) * 2
        whole = lax.dynamic_update_slice(whole, value, ((chip + low) * rows, 0))
        whole = lax.dynamic_update_slice(whole, other, ((chip + 1 - low) * rows, 0))
    return whole


def segment_ids(length_row, tok_count):
    slots = length_row.shape[0]
    upto = jnp.arange(slots)[None, :] <= jnp.arange(slots)[:, None]
    seq_ends = jnp.sum(jnp.where(upto, length_row[None, :], 0), axis=1)
    places = jnp.arange(tok_count, dtype=jnp.int32)
    return jnp.sum((places[:, None] >= seq_ends[None, :]).astype(jnp.int32), axis=1)


def norm_back(source, inverse, gain_vec, grad_in):
    scaled = grad_in * gain_vec
    inner_mean = jnp.mean(scaled * source, axis=-1, keepdims=True)
    return inverse * scaled - source * inverse**3 * inner_mean


def dot(left, right, left_dim, right_dim):
    return lax.dot_general(
        left, right, (((left_dim,), (right_dim,)), ((), ())), preferred_element_type=f32
    )


def heads_of(value):
    return value.reshape(value.shape[0], value.shape[1] // HEAD_SIZE, HEAD_SIZE)


def masked_scores(q_heads, k_heads, seg_ids):
    scores = jnp.einsum("qhd,khd->hqk", q_heads, k_heads, preferred_element_type=f32)
    places = jnp.arange(seg_ids.shape[0], dtype=jnp.int32)
    allowed = (seg_ids[:, None] == seg_ids[None, :]) & (places[None, :] <= places[:, None])
    return jnp.where(allowed[None], scores * HEAD_SIZE ** (-0.5), negative)


def attend_forward(queries, keys, values, seg_ids):
    scores = masked_scores(heads_of(queries), heads_of(keys), seg_ids)
    maximum = jnp.max(scores, axis=-1, keepdims=True)
    exponent = jnp.exp(scores - maximum)
    row_total = jnp.sum(exponent, axis=-1, keepdims=True)
    probs_low = (exponent / row_total).astype(bf16)
    mixed = jnp.einsum("hqk,khd->qhd", probs_low, heads_of(values), preferred_element_type=f32)
    return mixed.astype(bf16).reshape(queries.shape), maximum + jnp.log(row_total)


def attend_backward(queries, keys, values, grad_out, seg_ids, log_total):
    q_heads, k_heads, v_heads, g_heads = (heads_of(v) for v in (queries, keys, values, grad_out))
    probs = jnp.exp(masked_scores(q_heads, k_heads, seg_ids) - log_total)
    grad_probs = jnp.einsum("qhd,khd->hqk", g_heads, v_heads, preferred_element_type=f32)
    inner_sum = jnp.sum(probs * grad_probs, axis=-1, keepdims=True)
    grad_scores = (probs * (grad_probs - inner_sum)).astype(bf16)
    scale = HEAD_SIZE ** (-0.5)
    grad_q = jnp.einsum("hqk,khd->qhd", grad_scores, k_heads, preferred_element_type=f32) * scale
    grad_k = jnp.einsum("hqk,qhd->khd", grad_scores, q_heads, preferred_element_type=f32) * scale
    grad_v = jnp.einsum("hqk,qhd->khd", probs.astype(bf16), g_heads, preferred_element_type=f32)
    return tuple(v.astype(bf16).reshape(queries.shape) for v in (grad_q, grad_k, grad_v))


def sum_groups(*grads):
    return [g.astype(f32) for g in lax.psum(tuple(g.astype(bf16) for g in grads), "dp")]


def shards(
    block_input,
    out_grad,
    seq_lengths,
    attn_gains,
    attn_weights,
    ffn_gain,
    gate_weight,
    up_weight,
    down_weight,
):
    tok_count, width = block_input.shape
    section = lax.axis_index("section")
    is_first = section == 0
    plane = lax.axis_size("section") * lax.axis_size("tensor")
    plane_pos = section * lax.axis_size("tensor") + lax.axis_index("tensor")
    rows, columns = tok_count // plane, width // plane
    row_start = plane_pos * rows

    def own_rows(value):
        return lax.dynamic_slice_in_dim(value, row_start, rows, 0)

    seg_ids = segment_ids(seq_lengths[0], tok_count)
    is_valid = (seg_ids < seq_lengths.shape[1]).astype(f32)[:, None]
    inputs_f = block_input.astype(f32)
    inverse = lax.rsqrt(jnp.mean(inputs_f * inputs_f, axis=-1, keepdims=True) + epsilon)
    gain_row = attn_gains[0].astype(f32)
    normed = (inputs_f * inverse * gain_row).astype(bf16)
    w_first, w_second = attn_weights[0, 0], attn_weights[0, 1]
    half = w_first.shape[1] // 2

    first_proj = dot(normed, w_first, 1, 0).astype(bf16)
    second_proj = dot(normed, w_second, 1, 0).astype(bf16)

    def half_of(value, which):
        return lax.dynamic_slice_in_dim(value, which * half, half, 1)

    first_own, first_met = half_of(first_proj, section), swap_section(half_of(first_proj, 1 - section))
    second_met = lax.ppermute(second_proj[:, half:], "section", [(0, 1)])
    out_weight_met = lax.ppermute(w_second[:, :half], "section", [(1, 0)])
    queries = jnp.where(is_first, first_met, first_own)
    keys = jnp.where(is_first, first_own, first_met)
    values = jnp.where(is_first, second_proj[:, :half], second_met)
    out_weight = jnp.where(is_first, out_weight_met, w_second[:, half:])

    attn_out, log_total = attend_forward(queries, keys, values, seg_ids)
    branch_part = dot(attn_out, out_weight, 1, 1).astype(bf16)
    branch = scatter_sum(branch_part.reshape(plane, rows, width))
    residual = own_rows(block_input).astype(f32) + branch
    resid_inv = lax.rsqrt(jnp.mean(residual * residual, axis=-1, keepdims=True) + epsilon)
    gain_ffn = ffn_gain.astype(f32)
    hidden_in = gather_plane((residual * resid_inv * gain_ffn).astype(bf16))
    branch_sq = jnp.sum(branch * branch * own_rows(is_valid))

    gate_act = dot(hidden_in, gate_weight, 1, 0)
    up_act = dot(hidden_in, up_weight, 1, 0)
    gate_sig = jax.nn.sigmoid(gate_act)
    silu_val = gate_act * gate_sig
    hidden = (silu_val * up_act).astype(bf16)
    grad_hidden = dot(out_grad, down_weight, 1, 1)
    grad_up = (grad_hidden * silu_val).astype(bf16)
    grad_gate = (grad_hidden * up_act * gate_sig * (1.0 + gate_act * (1.0 - gate_sig))).astype(bf16)
    grad_hidden_part = (dot(grad_gate, gate_weight, 1, 1) + dot(grad_up, up_weight, 1, 1)).astype(bf16)
    grad_hidden_in = scatter_sum(grad_hidden_part.reshape(plane, rows, width))
    ffn_gain_term = jnp.sum(grad_hidden_in * residual * resid_inv, axis=0)
    grad_residual = own_rows(out_grad).astype(f32) + norm_back(residual, resid_inv, gain_ffn, grad_hidden_in)
    grad_branch_low = gather_plane(grad_residual.astype(bf16))

    def add_own(part, own):
        mixed = (own_rows(part).astype(f32) + own).astype(bf16)
        return lax.dynamic_update_slice_in_dim(part, mixed, row_start, 0)

    def by_columns(part):
        return part.reshape(tok_count, plane, columns).transpose(1, 0, 2)

    ffn_part = add_own(dot(hidden, down_weight, 1, 0).astype(bf16), residual)
    output_sum = scatter_sum(by_columns(ffn_part))
    block_output = output_sum.astype(bf16)
    output_sq = jnp.sum(output_sum * output_sum * is_valid)

    down_grad, gate_grad, up_grad = sum_groups(
        dot(hidden, out_grad, 0, 0), dot(hidden_in, grad_gate, 0, 0), dot(hidden_in, grad_up, 0, 0)
    )

    grad_attn_out = dot(grad_branch_low, out_weight, 1, 0).astype(bf16)
    grad_q, grad_k, grad_v = attend_backward(queries, keys, values, grad_attn_out, seg_ids, log_total)
    first_back = swap_section(jnp.where(is_first, grad_q, grad_k))
    second_back = swap_section(jnp.where(is_first, attn_out, grad_v))

    def joined(own, met):
        return jnp.concatenate([jnp.where(is_first, own, met), jnp.where(is_first, met, own)], axis=1)

    first_grad = joined(jnp.where(is_first, grad_k, grad_q), first_back)
    second_right = joined(jnp.where(is_first, grad_v, attn_out), second_back)
    second_left = jnp.where(is_first, normed, grad_branch_low)
    value_grad = jnp.where(is_first, second_right, jnp.zeros_like(second_right))
    grad_normed = dot(first_grad, w_first, 1, 1) + dot(value_grad, w_second, 1, 1)
    attn_gain_term = jnp.sum(grad_normed * inputs_f * inverse, axis=0)
    input_part = add_own(norm_back(inputs_f, inverse, gain_row, grad_normed).astype(bf16), grad_residual)
    input_grad = scatter_sum(by_columns(input_part)).astype(bf16)

    first_sum, second_sum, down_grad = lax.optimization_barrier(
        (dot(normed, first_grad, 0, 0), dot(second_left, second_right, 0, 0), down_grad)
    )
    attn_weight_grad = jnp.stack(sum_groups(first_sum, second_sum))[None]

    count_term = jnp.where(plane_pos == 0, jnp.sum(seq_lengths).astype(f32), 0.0)
    section_rows = jnp.where(
        jnp.arange(2, dtype=jnp.int32)[:, None] == section, attn_gain_term[None, :], 0.0
    )
    gain_terms = jnp.concatenate([section_rows, ffn_gain_term[None, :]], axis=0)
    stat_terms = jnp.stack([output_sq, branch_sq, count_term])
    gains, stats = lax.psum((gain_terms, stat_terms), ("section", "dp", "tensor"))
    attn_gain_grad = lax.dynamic_slice_in_dim(gains, section, 1, 0)
    activation_rms = jnp.sqrt(stats[:2] / (stats[2] * width))
    return (
        block_output,
        input_grad,
        attn_gain_grad,
        attn_weight_grad,
        gains[2],
        gate_grad,
        up_grad,
        down_grad,
        activation_rms,
    )


def solution(mesh):
    both = ("section", "tensor")
    in_specs = (
        P("dp", None),
        P("dp", None),
        P("dp", None),
        P("section", None),
        P("section", None, None, "tensor"),
        P(),
        P(None, both),
        P(None, both),
        P(both, None),
    )
    out_specs = (
        P("dp", both),
        P("dp", both),
        P("section", None),
        P("section", None, None, "tensor"),
        P(),
        P(None, both),
        P(None, both),
        P(both, None),
        P(),
    )
    return jax.shard_map(
        shards, mesh=mesh, in_specs=in_specs, out_specs=out_specs, check_vma=False
    )
```

time: 1050 us -> 689 us (0.66)
  waiting for transfers between devices: 811 us -> 410 us
  starting transfers between devices: 1.8 us -> 34.2 us
  local copies, waits for them, and re-layouts: 14.1 us -> 31.2 us
  loops' own time: 14.9 us -> 0 us
    psum x4 -> x2, waiting for transfers between devices: 687 us -> 279 us  [sum_groups(): lax.psum(tuple((g.astype(bf16) for g in grads)), 'dp')]
    ppermute x1 -> x35, waiting for transfers between devices: 87.8 us -> 130 us  [the longest x9 42.7 us: swap_section(): return lax.ppermute(value, 'section', SWAP_SECTION)]
    reduce_scatter x2 -> x0, waiting for transfers between devices: 36 us -> none  [the longest x1 35.9 us: shards(): lax.psum_scatter(input_part.astype(jnp.bfloat16), ('section', 'tensor'),...]
    ppermute x1 -> x35, starting transfers between devices: 1.56 us -> 34.1 us  [the longest x9 12.7 us: swap_section(): return lax.ppermute(value, 'section', SWAP_SECTION)]
    another operation x5 -> x0, loops' own time: 14.9 us -> none  [the longest x1 7.91 us: shards(): lax.cond(is_first, lambda: (jnp.zeros_like(projected), jnp.zeros_like(sha...]
    dot_general x15 -> x23, matrix products: 84.6 us -> 90.3 us  [the longest x17 75.1 us: dot(): lax.dot_general(left, right, (((left_dim,), (right_dim,)), ((), ())), pre...]
    convert_element_type x10 -> x14, other arithmetic: 33.4 us -> 34.3 us  [the longest x3 13.5 us: sum_groups(): g.astype(f32)]
  transfers between devices with their start and end apart: 7 -> 37, of which waited for: 6 -> 21; matrix products, arithmetic and copies ran while one was open for 8% -> 16% of each run, Pallas kernels for 0% -> 0%
where the time goes in v1:
time: 689 us; the launch traced here: 684 us
  waiting for transfers between devices  410 us (60%)
  matrix products  90.3 us (13%)
  other arithmetic  57.7 us (8%)
  blocking collectives  43.8 us (6%)
  starting transfers between devices  34.2 us (5%)
  local copies, waits for them, and re-layouts  31.2 us (5%)
  between operations  16.7 us (2%)
    psum x2, waiting for transfers between devices, sum_groups(): lax.psum(tuple((g.astype(bf16) for g in grads)), 'dp')  279 us
    dot_general x17, matrix products, dot(): lax.dot_general(left, right, (((left_dim,), (right_dim,)), ((), ())), pre...  75.1 us
    psum x1, blocking collectives, shards(): lax.psum((gain_terms, stat_terms), ('section', 'dp', 'tensor'))  43.8 us
    ppermute x9, waiting for transfers between devices, swap_section(): return lax.ppermute(value, 'section', SWAP_SECTION)  42.7 us
    ppermute x6, waiting for transfers between devices, swap_high(): return lax.ppermute(value, 'tensor', SWAP_HIGH)  41.6 us
    ppermute x6, waiting for transfers between devices, swap_both(): return lax.ppermute(value, ('section', 'tensor'), SWAP_BOTH)  21.1 us
  transfers between devices with their start and end apart: 37, of which 21 were waited for; matrix products, arithmetic and copies ran while one was open for 16% of the time, Pallas kernels for 0%

profile of v1, /device:TPU:0, one launch (start us, length us, event | category | flops | bytes accessed | tf_op | source)
XLA Modules:
  0.0 683.8 jit_solution(14906106893681586144)
XLA Ops:
  7.3 3.1 fusion
  11.0 5.2 fusion.30
  16.2 3.0 collective-permute-start.1
  22.5 2.7 collective-permute-start
  35.2 5.2 collective-permute-done
  42.5 12.0 %collective-permute-done.2 = bf16[2048,256]{1,0:T(8,128)(2,1)} collective-permute-done((bf16[2048,256]{1,0:T(8,128)(2,1)}, bf16[2048,256]{1,0:T(8,128)(2,1)}, u32[]{:S(2)}, u32[]{:S(2)}) %collective-permute-start.2) | collective-permute-done | bytes 1048608 | tf_op jit(solution)/shard_map/ppermute | solution.py:179
  54.5 4.4 convolution_convert_fusion.1
  58.8 3.0 dynamic-slice_bitcast_fusion.3
  61.9 4.3 collective-permute-done.3
  66.2 3.0 fusion.17
  75.2 10.8 %collective-permute-done.4 = bf16[120,2048]{1,0:T(8,128)(2,1)} collective-permute-done((bf16[120,2048]{1,0:T(8,128)(2,1)}, bf16[120,2048]{1,0:T(8,128)(2,1)}, u32[]{:S(2)}, u32[]{:S(2)}) %collective-permute-start.4) | collective-permute-done | bytes 491552 | tf_op jit(solution)/shard_map/ppermute | solution.py:36
  86.0 9.0 %collective-permute-done.5 = bf16[120,2048]{1,0:T(8,128)(2,1)} collective-permute-done((bf16[120,2048]{1,0:T(8,128)(2,1)}, bf16[120,2048]{1,0:T(8,128)(2,1)}, u32[]{:S(2)}, u32[]{:S(2)}) %collective-permute-start.5) | collective-permute-done | bytes 491552 | tf_op jit(solution)/shard_map/ppermute | solution.py:32
  96.9 2.7 multiply_reduce_fusion.5
  105.1 11.9 %collective-permute-done.7 = bf16[120,2048]{1,0:T(8,128)(2,1)} collective-permute-done((bf16[120,2048]{1,0:T(8,128)(2,1)}, bf16[120,2048]{1,0:T(8,128)(2,1)}, u32[]{:S(2)}, u32[]{:S(2)}) %collective-permute-start.7) | collective-permute-done | bytes 491552 | tf_op jit(solution)/shard_map/ppermute | solution.py:40
  117.0 6.5 fusion.97
  131.2 3.1 fusion.96
  134.4 4.5 multiply_convert_fusion.1
  138.9 3.3 fusion.98
  142.3 4.1 add_convert_fusion
  147.1 3.6 collective-permute-done.18
  156.2 4.4 convolution_convert_fusion.4
  160.7 6.2 collective-permute-done.19
  166.9 10.6 %collective-permute-done.20 = bf16[120,2048]{1,0:T(8,128)(2,1)S(1)} collective-permute-done((bf16[120,2048]{1,0:T(8,128)(2,1)}, bf16[120,2048]{1,0:T(8,128)(2,1)S(1)}, u32[]{:S(2)}, u32[]{:S(2)}) %collective-permute-start.20) | collective-permute-done | bytes 491552 | tf_op jit(solution)/shard_map/ppermute | solution.py:32
  183.2 4.4 convolution_convert_fusion.2
  189.6 7.3 %collective-permute-done.22 = bf16[120,2048]{1,0:T(8,128)(2,1)} collective-permute-done((bf16[120,2048]{1,0:T(8,128)(2,1)S(1)}, bf16[120,2048]{1,0:T(8,128)(2,1)}, u32[]{:S(2)}, u32[]{:S(2)}) %collective-permute-start.22) | collective-permute-done | bytes 491552 | tf_op jit(solution)/shard_map/ppermute | solution.py:40
  196.9 4.6 convolution_convert_fusion.3
  202.0 69.4 %all-reduce.5.cloned.1.call-done = bf16[688,2048]{1,0:T(8,128)(2,1)} async-done(((bf16[688,2048]{1,0:T(8,128)(2,1)}), bf16[688,2048]{1,0:T(8,128)(2,1)}) %all-reduce.5.cloned.1.call-update) | async-done | bytes 2818064 | tf_op jit(solution)/shard_map/psum | solution.py:137
  271.5 5.0 convert_element_type.317
  289.0 4.9 multiply_reduce_fusion
  293.9 7.4 %multiply_convert_fusion = bf16[2,960,960]{1,2,0:T(8,128)(2,1)} fusion(f32[2,960,960]{1,2,0:T(8,128)} %get-tuple-element.65, f32[2,960,960]{1,2,0:T(8,128)S(1)} %bitcast.216, f32[2,960]{1,0:T(2,128)S(1)} %get-tuple-element.64, f32[2,960]{1,0:T(2,128)S(1)} %log_add_fusion), kind=kLoop, calls=%fused_computation.14 | loop fusion | flops 7372800 | bytes 18447360 | tf_op jit(solution)/shard_map/convert_element_type | solution.py:128
  301.3 4.1 fusion.37
  310.2 4.7 fusion.18
  314.9 5.2 collective-permute-done.29
  320.2 4.0 fusion.56
  324.3 5.5 convolution_convert_fusion
  332.2 5.5 fusion.53
  337.6 6.1 fusion.8
  356.2 9.4 %collective-permute-done.15 = bf16[960,256]{1,0:T(8,128)(2,1)S(1)} collective-permute-done((bf16[960,256]{1,0:T(8,128)(2,1)}, bf16[960,256]{1,0:T(8,128)(2,1)S(1)}, u32[]{:S(2)}, u32[]{:S(2)}) %collective-permute-start.15) | collective-permute-done | bytes 491552 | tf_op jit(solution)/shard_map/ppermute | solution.py:36
  365.6 11.7 %collective-permute-done.16 = bf16[960,256]{1,0:T(8,128)(2,1)S(1)} collective-permute-done((bf16[960,256]{1,0:T(8,128)(2,1)}, bf16[960,256]{1,0:T(8,128)(2,1)S(1)}, u32[]{:S(2)}, u32[]{:S(2)}) %collective-permute-start.16) | collective-permute-done | bytes 491552 | tf_op jit(solution)/shard_map/ppermute | solution.py:32
  377.2 2.7 multiply_reduce_fusion.2
  381.4 43.8 %all-reduce = (f32[3,2048]{1,0:T(4,128)S(1)}, f32[3]{0:T(128)S(1)}) all-reduce(f32[3,2048]{1,0:T(4,128)S(1)} %pad_maximum_fusion.6, f32[3]{0:T(128)S(1)} %pad_maximum_fusion.7), channel_id=1, replica_groups=mesh['section'=2,'dp'=4,'tensor'=4] {'section','dp','tensor'}, use_global_device_ids=true, to_apply=%region_11.12 | all-reduce | flops 6147 | bytes 49176 | tf_op jit(solution)/shard_map/psum | solution.py:252
  426.5 2.7 fusion.14
  434.2 9.4 %collective-permute-done.32 = bf16[960,256]{1,0:T(8,128)(2,1)S(1)} collective-permute-done((bf16[960,256]{1,0:T(8,128)(2,1)S(1)}, bf16[960,256]{1,0:T(8,128)(2,1)S(1)}, u32[]{:S(2)}, u32[]{:S(2)}) %collective-permute-start.32) | collective-permute-done | bytes 491552 | tf_op jit(solution)/shard_map/ppermute | solution.py:36
  443.7 9.4 %collective-permute-done.33 = bf16[960,256]{1,0:T(8,128)(2,1)S(1)} collective-permute-done((bf16[960,256]{1,0:T(8,128)(2,1)S(1)}, bf16[960,256]{1,0:T(8,128)(2,1)S(1)}, u32[]{:S(2)}, u32[]{:S(2)}) %collective-permute-start.33) | collective-permute-done | bytes 491552 | tf_op jit(solution)/shard_map/ppermute | solution.py:32
  454.1 210.0 %all-reduce.7.cloned.1.call-done = (bf16[1,2048,512]{2,1,0:T(8,128)(2,1)}, bf16[1,2048,512]{2,1,0:T(8,128)(2,1)}, bf16[2048,688]{0,1:T(8,128)(2,1)}, bf16[2048,688]{0,1:T(8,128)(2,1)}) async-done(((bf16[1,2048,512]{2,1,0:T(8,128)(2,1)}, bf16[1,2048,512]{2,1,0:T(8,128)(2,1)}, bf16[2048,688]{0,1:T(8,128)(2,1)}, bf16[2048,688]{0,1:T(8,128)(2,1)}), (bf16[1,2048,512]{2,1,0:T(8,128)(2,1)}, ...) | async-done | bytes 9830416 | tf_op jit(solution)/shard_map/psum | solution.py:137
  664.1 5.2 convert_element_type.321
  669.3 3.2 convert_element_type.323
  672.7 3.9 fusion.11
  (232 shorter events, 91.0 us)
Async XLA Ops:
  7.2 127.2 %copy-start = (bf16[2048,688]{0,1:T(8,128)(2,1)S(1)}, bf16[2048,688]{0,1:T(8,128)(2,1)}, u32[]{:S(2)}) copy-start(bf16[2048,688]{0,1:T(8,128)(2,1)} %param.15) | copy-start | bytes 8454148
  7.2 264.3 %all-reduce.5.cloned.1.call-start = ((), (), s32[]{:S(2)}) async-start(), calls=%async_computation | async-start | bytes 5636096 | tf_op jit(solution)/shard_map/psum | solution.py:137
  11.0 8.3 %copy-start.6 = (bf16[960,2048]{1,0:T(8,128)(2,1)S(1)}, bf16[960,2048]{1,0:T(8,128)(2,1)}, u32[]{:S(2)}) copy-start(bf16[960,2048]{1,0:T(8,128)(2,1)} %param.9) | copy-start | bytes 11796484
  16.2 14.6 %collective-permute-start.1 = (bf16[960,256]{1,0:T(8,128)(2,1)S(1)}, bf16[960,256]{1,0:T(8,128)(2,1)}, u32[]{:S(2)}, u32[]{:S(2)}) collective-permute-start(bf16[960,256]{1,0:T(8,128)(2,1)S(1)} %constant_dynamic-slice_fusion.1), channel_id=1, source_target_pairs={{0,16},{16,0},{1,17},{17,1},{2,18},{18,2},{3,19},{19,3},{4,20},{20... | collective-permute-start | bytes 1474568 | tf_op jit(solution)/shard_map/ppermute | solution.py:36
  22.5 17.9 %collective-permute-start = (bf16[960,256]{1,0:T(8,128)(2,1)}, bf16[960,256]{1,0:T(8,128)(2,1)}, u32[]{:S(2)}, u32[]{:S(2)}) collective-permute-start(bf16[960,256]{1,0:T(8,128)(2,1)} %slice.37), channel_id=1, source_target_pairs={{0,16},{1,17},{2,18},{3,19},{4,20},{5,21},{6,22},{7,23},{8,24},{9,... | collective-permute-start | bytes 1474568 | tf_op jit(solution)/shard_map/ppermute | solution.py:178
  27.6 26.8 %collective-permute-start.2 = (bf16[2048,256]{1,0:T(8,128)(2,1)}, bf16[2048,256]{1,0:T(8,128)(2,1)}, u32[]{:S(2)}, u32[]{:S(2)}) collective-permute-start(bf16[2048,256]{1,0:T(8,128)(2,1)} %slice.38), channel_id=1, source_target_pairs={{16,0},{17,1},{18,2},{19,3},{20,4},{21,5},{22,6},{23,7},{24,8},{25... | collective-permute-start | bytes 3145736 | tf_op jit(solution)/shard_map/ppermute | solution.py:179
  35.2 19.3 %copy-start.12 = (bf16[2048,512]{1,0:T(8,128)(2,1)S(1)}, bf16[2048,512]{1,0:T(8,128)(2,1)}, u32[]{:S(2)}) copy-start(bf16[2048,512]{1,0:T(8,128)(2,1)} %copy-done.11) | copy-start | bytes 6291460
  61.9 4.3 collective-permute-start.3
  61.9 13.2 %copy-start.39 = (bf16[2048]{0:T(1024)(128)(2,1)S(1)}, bf16[2048]{0:T(1024)(128)(2,1)}, u32[]{:S(2)}) copy-start(bf16[2048]{0:T(1024)(128)(2,1)} %param.14) | copy-start | bytes 12292
  71.6 14.4 %collective-permute-start.4 = (bf16[120,2048]{1,0:T(8,128)(2,1)}, bf16[120,2048]{1,0:T(8,128)(2,1)}, u32[]{:S(2)}, u32[]{:S(2)}) collective-permute-start(bf16[120,2048]{1,0:T(8,128)(2,1)} %get-tuple-element.45), channel_id=1, source_target_pairs={{0,16},{16,0},{1,17},{17,1},{2,18},{18,2},{3,19},{19,3},{4,20},{20... | collective-permute-start | bytes 1474568 | tf_op jit(solution)/shard_map/ppermute | solution.py:36
  71.6 23.4 %collective-permute-start.5 = (bf16[120,2048]{1,0:T(8,128)(2,1)}, bf16[120,2048]{1,0:T(8,128)(2,1)}, u32[]{:S(2)}, u32[]{:S(2)}) collective-permute-start(bf16[120,2048]{1,0:T(8,128)(2,1)} %get-tuple-element.47), channel_id=1, source_target_pairs={{0,2},{1,3},{2,0},{3,1},{4,6},{5,7},{6,4},{7,5},{8,10},{9,11},{10,... | collective-permute-start | bytes 1474568 | tf_op jit(solution)/shard_map/ppermute | solution.py:32
  73.4 23.5 %collective-permute-start.6 = (bf16[120,2048]{1,0:T(8,128)(2,1)}, bf16[120,2048]{1,0:T(8,128)(2,1)}, u32[]{:S(2)}, u32[]{:S(2)}) collective-permute-start(bf16[120,2048]{1,0:T(8,128)(2,1)} %get-tuple-element.46), channel_id=1, source_target_pairs={{0,18},{1,19},{2,16},{3,17},{16,2},{17,3},{18,0},{19,1},{4,22},{5,... | collective-permute-start | bytes 1474568 | tf_op jit(solution)/shard_map/ppermute | solution.py:40
  75.1 41.9 %copy-start.35 = (bf16[960,2048]{1,0:T(8,128)(2,1)S(1)}, bf16[960,2048]{1,0:T(8,128)(2,1)}, u32[]{:S(2)}) copy-start(bf16[960,2048]{1,0:T(8,128)(2,1)} %param.10) | copy-start | bytes 11796484
  101.6 15.4 %collective-permute-start.7 = (bf16[120,2048]{1,0:T(8,128)(2,1)}, bf16[120,2048]{1,0:T(8,128)(2,1)}, u32[]{:S(2)}, u32[]{:S(2)}) collective-permute-start(bf16[120,2048]{1,0:T(8,128)(2,1)} %multiply_convert_fusion.4), channel_id=1, source_target_pairs={{0,18},{1,19},{2,16},{3,17},{16,2},{17,3},{18,0},{19,1},{4,22},{5,... | collective-permute-start | bytes 1474568 | tf_op jit(solution)/shard_map/ppermute | solution.py:40
  103.3 21.3 %collective-permute-start.9 = (bf16[120,2048]{1,0:T(8,128)(2,1)}, bf16[120,2048]{1,0:T(8,128)(2,1)}, u32[]{:S(2)}, u32[]{:S(2)}) collective-permute-start(bf16[120,2048]{1,0:T(8,128)(2,1)} %multiply_convert_fusion.4), channel_id=1, source_target_pairs={{0,16},{16,0},{1,17},{17,1},{2,18},{18,2},{3,19},{19,3},{4,20},{20... | collective-permute-start | bytes 1474568 | tf_op jit(solution)/shard_map/ppermute | solution.py:36
  103.6 22.1 %collective-permute-start.11 = (bf16[120,2048]{1,0:T(8,128)(2,1)}, bf16[120,2048]{1,0:T(8,128)(2,1)}, u32[]{:S(2)}, u32[]{:S(2)}) collective-permute-start(bf16[120,2048]{1,0:T(8,128)(2,1)} %multiply_convert_fusion.4), channel_id=1, source_target_pairs={{0,2},{1,3},{2,0},{3,1},{4,6},{5,7},{6,4},{7,5},{8,10},{9,11},{10,... | collective-permute-start | bytes 1474568 | tf_op jit(solution)/shard_map/ppermute | solution.py:32
  117.0 10.5 %collective-permute-start.8 = (bf16[120,2048]{1,0:T(8,128)(2,1)}, bf16[120,2048]{1,0:T(8,128)(2,1)}, u32[]{:S(2)}, u32[]{:S(2)}) collective-permute-start(bf16[120,2048]{1,0:T(8,128)(2,1)} %collective-permute-done.7), channel_id=1, source_target_pairs={{0,1},{1,0},{2,3},{3,2},{4,5},{5,4},{6,7},{7,6},{8,9},{9,8},{10,11... | collective-permute-start | bytes 1474568 | tf_op jit(solution)/shard_map/ppermute | solution.py:28
  123.5 7.7 %collective-permute-start.13 = (bf16[120,2048]{1,0:T(8,128)(2,1)}, bf16[120,2048]{1,0:T(8,128)(2,1)S(1)}, u32[]{:S(2)}, u32[]{:S(2)}) collective-permute-start(bf16[120,2048]{1,0:T(8,128)(2,1)} %multiply_convert_fusion.4), channel_id=1, source_target_pairs={{0,1},{1,0},{2,3},{3,2},{4,5},{5,4},{6,7},{7,6},{8,9},{9,8},{10,11... | collective-permute-start | bytes 1474568 | tf_op jit(solution)/shard_map/ppermute | solution.py:28
  124.7 5.1 collective-permute-start.10
  125.8 5.1 collective-permute-start.12
  138.9 17.2 %copy-start.48 = (bf16[960,688]{0,1:T(8,128)(2,1)}, bf16[960,688]{0,1:T(8,128)(2,1)S(1)}, u32[]{:S(2)}) copy-start(bf16[960,688]{0,1:T(8,128)(2,1)S(1)} %get-tuple-element.32) | copy-start | bytes 3962884
  146.5 9.6 %copy-start.36 = (bf16[960,2048]{1,0:T(8,128)(2,1)S(1)}, bf16[960,2048]{1,0:T(8,128)(2,1)}, u32[]{:S(2)}) copy-start(bf16[960,2048]{1,0:T(8,128)(2,1)} %param.10) | copy-start | bytes 11796484
  146.5 4.2 collective-permute-start.18
  152.7 14.3 %collective-permute-start.19 = (bf16[120,2048]{1,0:T(8,128)(2,1)}, bf16[120,2048]{1,0:T(8,128)(2,1)S(1)}, u32[]{:S(2)}, u32[]{:S(2)}) collective-permute-start(bf16[120,2048]{1,0:T(8,128)(2,1)} %get-tuple-element.39), channel_id=1, source_target_pairs={{0,16},{16,0},{1,17},{17,1},{2,18},{18,2},{3,19},{19,3},{4,20},{20... | collective-permute-start | bytes 1474568 | tf_op jit(solution)/shard_map/ppermute | solution.py:36
  153.8 23.7 %collective-permute-start.20 = (bf16[120,2048]{1,0:T(8,128)(2,1)}, bf16[120,2048]{1,0:T(8,128)(2,1)S(1)}, u32[]{:S(2)}, u32[]{:S(2)}) collective-permute-start(bf16[120,2048]{1,0:T(8,128)(2,1)} %get-tuple-element.41), channel_id=1, source_target_pairs={{0,2},{1,3},{2,0},{3,1},{4,6},{5,7},{6,4},{7,5},{8,10},{9,11},{10,... | collective-permute-start | bytes 1474568 | tf_op jit(solution)/shard_map/ppermute | solution.py:32
  154.7 22.9 %collective-permute-start.21 = (bf16[120,2048]{1,0:T(8,128)(2,1)S(1)}, bf16[120,2048]{1,0:T(8,128)(2,1)}, u32[]{:S(2)}, u32[]{:S(2)}) collective-permute-start(bf16[120,2048]{1,0:T(8,128)(2,1)S(1)} %get-tuple-element.40), channel_id=1, source_target_pairs={{0,18},{1,19},{2,16},{3,17},{16,2},{17,3},{18,0},{19,1},{4,22},{5,... | collective-permute-start | bytes 1474568 | tf_op jit(solution)/shard_map/ppermute | solution.py:40
  156.2 21.4 %copy-start.5 = (f32[120,2048]{1,0:T(8,128)S(1)}, f32[120,2048]{1,0:T(8,128)}, u32[]{:S(2)}) copy-start(f32[120,2048]{1,0:T(8,128)} %copy-done.3) | copy-start | bytes 2949124
  160.6 503.5 %all-reduce.7.cloned.1.call-start = ((), (), s32[]{:S(2)}) async-start(), calls=%async_computation.1 | async-start | bytes 19660800 | tf_op jit(solution)/shard_map/psum | solution.py:137
  160.7 22.5 %copy-start.21 = (bf16[960,2048]{1,0:T(8,128)(2,1)S(1)}, bf16[960,2048]{1,0:T(8,128)(2,1)}, u32[]{:S(2)}) copy-start(bf16[960,2048]{1,0:T(8,128)(2,1)} %copy-done.20) | copy-start | bytes 11796484
  160.7 22.5 %copy-start.47 = (bf16[960,688]{0,1:T(8,128)(2,1)S(1)}, bf16[960,688]{0,1:T(8,128)(2,1)}, u32[]{:S(2)}) copy-start(bf16[960,688]{0,1:T(8,128)(2,1)} %copy-done.46) | copy-start | bytes 3962884
  181.7 15.2 %copy-start.45 = (bf16[960,688]{0,1:T(8,128)(2,1)S(1)}, bf16[960,688]{0,1:T(8,128)(2,1)}, u32[]{:S(2)}) copy-start(bf16[960,688]{0,1:T(8,128)(2,1)} %copy-done.44) | copy-start | bytes 3962884
  181.7 15.2 %collective-permute-start.22 = (bf16[120,2048]{1,0:T(8,128)(2,1)S(1)}, bf16[120,2048]{1,0:T(8,128)(2,1)}, u32[]{:S(2)}, u32[]{:S(2)}) collective-permute-start(bf16[120,2048]{1,0:T(8,128)(2,1)S(1)} %get-tuple-element.25), channel_id=1, source_target_pairs={{0,18},{1,19},{2,16},{3,17},{16,2},{17,3},{18,0},{19,1},{4,22},{5,... | collective-permute-start | bytes 1474568 | tf_op jit(solution)/shard_map/ppermute | solution.py:40
  187.6 88.9 %collective-permute-start.24 = (bf16[120,2048]{1,0:T(8,128)(2,1)S(1)}, bf16[120,2048]{1,0:T(8,128)(2,1)}, u32[]{:S(2)}, u32[]{:S(2)}) collective-permute-start(bf16[120,2048]{1,0:T(8,128)(2,1)S(1)} %get-tuple-element.25), channel_id=1, source_target_pairs={{0,16},{16,0},{1,17},{17,1},{2,18},{18,2},{3,19},{19,3},{4,20},{20... | collective-permute-start | bytes 1474568 | tf_op jit(solution)/shard_map/ppermute | solution.py:36
  188.6 89.6 %collective-permute-start.26 = (bf16[120,2048]{1,0:T(8,128)(2,1)S(1)}, bf16[120,2048]{1,0:T(8,128)(2,1)S(1)}, u32[]{:S(2)}, u32[]{:S(2)}) collective-permute-start(bf16[120,2048]{1,0:T(8,128)(2,1)S(1)} %get-tuple-element.25), channel_id=1, source_target_pairs={{0,2},{1,3},{2,0},{3,1},{4,6},{5,7},{6,4},{7,5},{8,10},{9,11},{10,... | collective-permute-start | bytes 1474568 | tf_op jit(solution)/shard_map/ppermute | solution.py:32
  196.9 81.9 %collective-permute-start.23 = (bf16[120,2048]{1,0:T(8,128)(2,1)}, bf16[120,2048]{1,0:T(8,128)(2,1)}, u32[]{:S(2)}, u32[]{:S(2)}) collective-permute-start(bf16[120,2048]{1,0:T(8,128)(2,1)} %collective-permute-done.22), channel_id=1, source_target_pairs={{0,1},{1,0},{2,3},{3,2},{4,5},{5,4},{6,7},{7,6},{8,9},{9,8},{10,11... | collective-permute-start | bytes 1474568 | tf_op jit(solution)/shard_map/ppermute | solution.py:28
  201.5 79.9 %collective-permute-start.28 = (bf16[120,2048]{1,0:T(8,128)(2,1)S(1)}, bf16[120,2048]{1,0:T(8,128)(2,1)S(1)}, u32[]{:S(2)}, u32[]{:S(2)}) collective-permute-start(bf16[120,2048]{1,0:T(8,128)(2,1)S(1)} %get-tuple-element.25), channel_id=1, source_target_pairs={{0,1},{1,0},{2,3},{3,2},{4,5},{5,4},{6,7},{7,6},{8,9},{9,8},{10,11... | collective-permute-start | bytes 1474568 | tf_op jit(solution)/shard_map/ppermute | solution.py:28
  276.5 4.6 collective-permute-start.25
  278.2 3.0 collective-permute-start.27
  288.2 20.8 %collective-permute-start.30 = (bf16[960,256]{1,0:T(8,128)(2,1)}, bf16[960,256]{1,0:T(8,128)(2,1)}, u32[]{:S(2)}, u32[]{:S(2)}) collective-permute-start(bf16[960,256]{1,0:T(8,128)(2,1)} %bitcast_select_fusion), channel_id=1, source_target_pairs={{0,16},{16,0},{1,17},{17,1},{2,18},{18,2},{3,19},{19,3},{4,20},{20... | collective-permute-start | bytes 1474568 | tf_op jit(solution)/shard_map/ppermute | solution.py:36
  306.7 13.4 %collective-permute-start.29 = (bf16[960,256]{1,0:T(8,128)(2,1)S(1)}, bf16[960,256]{1,0:T(8,128)(2,1)S(1)}, u32[]{:S(2)}, u32[]{:S(2)}) collective-permute-start(bf16[960,256]{1,0:T(8,128)(2,1)S(1)} %bitcast.227), channel_id=1, source_target_pairs={{0,16},{16,0},{1,17},{17,1},{2,18},{18,2},{3,19},{19,3},{4,20},{20... | collective-permute-start | bytes 1474568 | tf_op jit(solution)/shard_map/ppermute | solution.py:36
  330.3 19.5 %collective-permute-start.14 = (bf16[4,960,256]{2,1,0:T(8,128)(2,1)S(1)}, bf16[4,960,256]{2,1,0:T(8,128)(2,1)S(1)}, u32[]{:S(2)}, u32[]{:S(2)}) collective-permute-start(bf16[4,960,256]{2,1,0:T(8,128)(2,1)S(1)} %dynamic-slice_bitcast_fusion.2), channel_id=1, source_target_pairs={{0,1},{1,0},{2,3},{3,2},{4,5},{5,4},{6,7},{7,6},{8,9},{9,8},{10,11... | collective-permute-start | bytes 5898248 | tf_op jit(solution)/shard_map/ppermute | solution.py:28
  349.8 76.6 %collective-permute-start.31 = (bf16[4,960,256]{2,1,0:T(8,128)(2,1)}, bf16[4,960,256]{2,1,0:T(8,128)(2,1)}, u32[]{:S(2)}, u32[]{:S(2)}) collective-permute-start(bf16[4,960,256]{2,1,0:T(8,128)(2,1)} %dynamic-slice_bitcast_fusion), channel_id=1, source_target_pairs={{0,1},{1,0},{2,3},{3,2},{4,5},{5,4},{6,7},{7,6},{8,9},{9,8},{10,11... | collective-permute-start | bytes 5898248 | tf_op jit(solution)/shard_map/ppermute | solution.py:28
  351.4 14.2 %collective-permute-start.15 = (bf16[960,256]{1,0:T(8,128)(2,1)}, bf16[960,256]{1,0:T(8,128)(2,1)S(1)}, u32[]{:S(2)}, u32[]{:S(2)}) collective-permute-start(bf16[960,256]{1,0:T(8,128)(2,1)} %get-tuple-element.42), channel_id=1, source_target_pairs={{0,16},{16,0},{1,17},{17,1},{2,18},{18,2},{3,19},{19,3},{4,20},{20... | collective-permute-start | bytes 1474568 | tf_op jit(solution)/shard_map/ppermute | solution.py:36
  353.2 24.1 %collective-permute-start.16 = (bf16[960,256]{1,0:T(8,128)(2,1)}, bf16[960,256]{1,0:T(8,128)(2,1)S(1)}, u32[]{:S(2)}, u32[]{:S(2)}) collective-permute-start(bf16[960,256]{1,0:T(8,128)(2,1)} %get-tuple-element.44), channel_id=1, source_target_pairs={{0,2},{1,3},{2,0},{3,1},{4,6},{5,7},{6,4},{7,5},{8,10},{9,11},{10,... | collective-permute-start | bytes 1474568 | tf_op jit(solution)/shard_map/ppermute | solution.py:32
  354.6 22.6 %collective-permute-start.17 = (bf16[960,256]{1,0:T(8,128)(2,1)S(1)}, bf16[960,256]{1,0:T(8,128)(2,1)}, u32[]{:S(2)}, u32[]{:S(2)}) collective-permute-start(bf16[960,256]{1,0:T(8,128)(2,1)S(1)} %get-tuple-element.43), channel_id=1, source_target_pairs={{0,18},{1,19},{2,16},{3,17},{16,2},{17,3},{18,0},{19,1},{4,22},{5,... | collective-permute-start | bytes 1474568 | tf_op jit(solution)/shard_map/ppermute | solution.py:40
  429.2 14.4 %collective-permute-start.32 = (bf16[960,256]{1,0:T(8,128)(2,1)S(1)}, bf16[960,256]{1,0:T(8,128)(2,1)S(1)}, u32[]{:S(2)}, u32[]{:S(2)}) collective-permute-start(bf16[960,256]{1,0:T(8,128)(2,1)S(1)} %get-tuple-element.36), channel_id=1, source_target_pairs={{0,16},{16,0},{1,17},{17,1},{2,18},{18,2},{3,19},{19,3},{4,20},{20... | collective-permute-start | bytes 1474568 | tf_op jit(solution)/shard_map/ppermute | solution.py:36
  431.5 21.5 %collective-permute-start.33 = (bf16[960,256]{1,0:T(8,128)(2,1)S(1)}, bf16[960,256]{1,0:T(8,128)(2,1)S(1)}, u32[]{:S(2)}, u32[]{:S(2)}) collective-permute-start(bf16[960,256]{1,0:T(8,128)(2,1)S(1)} %get-tuple-element.38), channel_id=1, source_target_pairs={{0,2},{1,3},{2,0},{3,1},{4,6},{5,7},{6,4},{7,5},{8,10},{9,11},{10,... | collective-permute-start | bytes 1474568 | tf_op jit(solution)/shard_map/ppermute | solution.py:32
  432.1 20.9 %collective-permute-start.34 = (bf16[960,256]{1,0:T(8,128)(2,1)S(1)}, bf16[960,256]{1,0:T(8,128)(2,1)S(1)}, u32[]{:S(2)}, u32[]{:S(2)}) collective-permute-start(bf16[960,256]{1,0:T(8,128)(2,1)S(1)} %get-tuple-element.37), channel_id=1, source_target_pairs={{0,18},{1,19},{2,16},{3,17},{16,2},{17,3},{18,0},{19,1},{4,22},{5,... | collective-permute-start | bytes 1474568 | tf_op jit(solution)/shard_map/ppermute | solution.py:40
  (40 other events, 166.2 us)
Sparse Core Ops, SparseCore 0:
  160.7 110.6 all-reduce.4
  324.4 339.6 all-reduce.6

commit v2 on v1

v2 whole, which is shorter than its diff:
```python
import jax
import jax.numpy as jnp
from jax import lax
from jax.experimental import pallas as pl
from jax.experimental.pallas import tpu as pltpu
from jax.sharding import PartitionSpec as P

HEAD_SIZE = 128
epsilon = 1e-06
negative = -1e30
bf16 = jnp.bfloat16
f32 = jnp.float32

SWAP_SECTION = [(0, 1), (1, 0)]
SWAP_LOW = [(i, i ^ 1) for i in range(4)]
SWAP_HIGH = [(i, i ^ 2) for i in range(4)]
SWAP_BOTH = [(i, i ^ 6) for i in range(8)]


def place():
    section, tensor = lax.axis_index("section"), lax.axis_index("tensor")
    return section, tensor // 2, tensor % 2


def pick(blocks, index):
    return lax.dynamic_index_in_dim(blocks, index, 0, keepdims=False)


def swap_low(value):
    return lax.ppermute(value, "tensor", SWAP_LOW)


def swap_high(value):
    return lax.ppermute(value, "tensor", SWAP_HIGH)


def swap_section(value):
    return lax.ppermute(value, "section", SWAP_SECTION)


def swap_both(value):
    return lax.ppermute(value, ("section", "tensor"), SWAP_BOTH)


def meet(*values):
    return lax.optimization_barrier(values)


def add_low(left, right):
    return (left.astype(f32) + right.astype(f32)).astype(bf16)


def scatter_half(blocks):
    pairs = blocks.reshape((4, 2) + blocks.shape[1:])
    low = place()[2]
    kept = lax.dynamic_index_in_dim(pairs, low, 1, keepdims=False)
    sent = lax.dynamic_index_in_dim(pairs, 1 - low, 1, keepdims=False)
    [half] = meet(add_low(kept, swap_low(sent)))
    return half


def scatter_across(half):
    section, high, _ = place()

    def toward(a, b):
        return pick(half, (section ^ a) * 2 + (high ^ b))

    mid = half.shape[2] // 2
    across = toward(1, 1)
    left_met, right_met = swap_section(across[:, :mid]), swap_high(across[:, mid:])
    return left_met, right_met, toward(1, 0), toward(0, 1), toward(0, 0)


def scatter_last(left_met, right_met, to_section, to_high, own):
    mid = left_met.shape[1]
    to_section = jnp.concatenate([to_section[:, :mid], add_low(to_section[:, mid:], right_met)], axis=1)
    to_high = jnp.concatenate([add_low(to_high[:, :mid], left_met), to_high[:, mid:]], axis=1)
    from_section, from_high = swap_section(to_section), swap_high(to_high)
    return own.astype(f32) + from_section.astype(f32) + from_high.astype(f32)


def scatter_sum(blocks):
    return scatter_last(*scatter_across(scatter_half(blocks)))


def gather_plane(block):
    section, high, low = place()
    rows, width = block.shape
    mid = width // 2
    by_section, by_high = swap_section(block), swap_high(block)
    across_left, across_right = swap_high(by_section[:, :mid]), swap_section(by_high[:, mid:])
    found = [
        (block, 0, 0, 0),
        (by_section, 1, 0, 0),
        (by_high, 0, 1, 0),
        (across_left, 1, 1, 0),
        (across_right, 1, 1, mid),
    ]
    whole = jnp.zeros((8 * rows, width), block.dtype)
    for value, a, b, column in found:
        other = swap_low(value)
        chip = ((section ^ a) * 2 + (high ^ b)) * 2
        whole = lax.dynamic_update_slice(whole, value, ((chip + low) * rows, column))
        whole = lax.dynamic_update_slice(whole, other, ((chip + 1 - low) * rows, column))
    return whole


def tensor_rows(whole):
    rows = whole.shape[0] // lax.axis_size("tensor")
    return lax.dynamic_slice_in_dim(whole, lax.axis_index("tensor") * rows, rows, 0)


def other_groups(slices):
    group, count = lax.axis_index("dp"), slices.shape[0]
    return [pick(slices, group ^ k)[None] for k in range(1, count)]


def by_slice(whole):
    return whole.reshape(lax.axis_size("tensor"), -1, whole.shape[1])


def segment_ids(length_row, tok_count):
    slots = length_row.shape[0]
    upto = jnp.arange(slots)[None, :] <= jnp.arange(slots)[:, None]
    seq_ends = jnp.sum(jnp.where(upto, length_row[None, :], 0), axis=1)
    places = jnp.arange(tok_count, dtype=jnp.int32)
    return jnp.sum((places[:, None] >= seq_ends[None, :]).astype(jnp.int32), axis=1)


def norm_back(source, inverse, gain_vec, grad_in):
    scaled = grad_in * gain_vec
    inner_mean = jnp.mean(scaled * source, axis=-1, keepdims=True)
    return inverse * scaled - source * inverse**3 * inner_mean


def dot(left, right, left_dim, right_dim):
    return lax.dot_general(
        left, right, (((left_dim,), (right_dim,)), ((), ())), preferred_element_type=f32
    )


def feed_forward_grads(order, hidden_blocks, grad_pieces, gate_weight, up_weight, down_weight):
    columns_at_once = 256
    count = len(grad_pieces)
    flat = [(at, i) for at, piece in enumerate(grad_pieces) for i in range(piece.shape[0])]
    starts = [flat.index((at, 0)) for at in range(count)]
    rows, width = hidden_blocks.shape[1:]
    units, steps, block = gate_weight.shape[0], len(flat) // 2, 2 * rows
    chunks = width // columns_at_once

    def kernel(order_ref, hidden_ref, *refs):
        grads, refs = refs[:count], refs[count:]
        weights, outs, kept, refs = refs[:3], refs[3:6], refs[6:9], refs[9:]
        hidden_buf, grad_buf, hidden_cols, grad_cols, row_sems, col_sems = refs
        step = pl.program_id(0)

        def row_copies(at, do):
            slot = lax.rem(at, 2)
            for static_at in range(steps):

                @pl.when(at == static_at)
                def _():
                    for i in range(2):
                        segment = static_at * 2 + i
                        piece, index = flat[segment]
                        found = hidden_ref.at[order_ref[segment]]
                        do(pltpu.make_async_copy(found, hidden_buf.at[slot, i], row_sems.at[slot, 0, i]))
                        found = grads[piece].at[index]
                        do(pltpu.make_async_copy(found, grad_buf.at[slot, i], row_sems.at[slot, 1, i]))

        def col_copies(at, do):
            slot = lax.rem(at, 2)
            columns = pl.ds(pl.multiple_of(at * columns_at_once, columns_at_once), columns_at_once)
            for segment in range(2 * steps):
                found = hidden_ref.at[order_ref[segment], :, columns]
                do(pltpu.make_async_copy(found, hidden_cols.at[slot, segment], col_sems.at[slot, 0, segment]))
            for piece in range(count):
                found = grads[piece].at[:, :, columns]
                into = grad_cols.at[slot, pl.ds(starts[piece], grad_pieces[piece].shape[0])]
                do(pltpu.make_async_copy(found, into, col_sems.at[slot, 1, piece]))

        @pl.when(step == 0)
        def _():
            row_copies(step, lambda c: c.start())

        @pl.when(step + 1 < steps)
        def _():
            row_copies(step + 1, lambda c: c.start())

        @pl.when(step == steps - 1)
        def _():
            col_copies(0, lambda c: c.start())

        @pl.when(step < steps)
        def _():
            row_copies(step, lambda c: c.wait())
            slot = lax.rem(step, 2)
            h = hidden_buf[slot].reshape(block, width)
            o = grad_buf[slot].reshape(block, width)
            gate = dot(weights[0][...], h, 1, 1)
            up = dot(weights[1][...], h, 1, 1)
            back = dot(weights[2][...], o, 1, 1)
            sig = jax.nn.sigmoid(gate)
            silu = gate * sig
            kept[0][step] = (silu * up).astype(bf16)
            kept[1][step] = (back * up * sig * (1.0 + gate * (1.0 - sig))).astype(bf16)
            kept[2][step] = (back * silu).astype(bf16)

        @pl.when(step >= steps)
        def _():
            chunk = step - steps
            col_copies(chunk, lambda c: c.wait())

            @pl.when(chunk + 1 < chunks)
            def _():
                col_copies(chunk + 1, lambda c: c.start())

            slot = lax.rem(chunk, 2)
            h = hidden_cols[slot].reshape(steps * block, columns_at_once)
            o = grad_cols[slot].reshape(steps * block, columns_at_once)
            for i, right in ((0, o), (1, h), (2, h)):
                parts = [dot(kept[i][j], right[j * block : (j + 1) * block], 1, 0) for j in range(steps)]
                outs[i][...] = sum(parts[1:], parts[0])

    anywhere = pl.BlockSpec(memory_space=pl.ANY)
    weight = pl.BlockSpec((units, width), lambda i, order: (0, 0), pipeline_mode=pl.Buffered(1))
    result = pl.BlockSpec((units, columns_at_once), lambda i, order: (0, jnp.maximum(i - steps, 0)))
    whole_rows = pltpu.VMEM((2, 2, rows, width), bf16)
    some_columns = pltpu.VMEM((2, 2 * steps, rows, columns_at_once), bf16)
    return pl.pallas_call(
        kernel,
        out_shape=[jax.ShapeDtypeStruct((units, width), f32)] * 3,
        grid_spec=pltpu.PrefetchScalarGridSpec(
            num_scalar_prefetch=1,
            grid=(steps + chunks,),
            in_specs=[anywhere] * (1 + count) + [weight] * 3,
            out_specs=[result] * 3,
            scratch_shapes=[pltpu.VMEM((steps, units, block), bf16)] * 3
            + [whole_rows, whole_rows, some_columns, some_columns]
            + [pltpu.SemaphoreType.DMA((2, 2, 2)), pltpu.SemaphoreType.DMA((2, 2, 2 * steps))],
        ),
        compiler_params=pltpu.CompilerParams(vmem_limit_bytes=60 * 2**20),
        name="feed_forward_grads",
    )(order, hidden_blocks, *grad_pieces, gate_weight, up_weight, down_weight)


def whole_block(shape):
    return pl.BlockSpec(shape, lambda *_: (0,) * len(shape), pipeline_mode=pl.Buffered(1))


def kernel_params(mebibytes=56):
    return pltpu.CompilerParams(vmem_limit_bytes=mebibytes * 2**20)


def row_scale(value):
    return lax.rsqrt(jnp.mean(value * value, axis=-1, keepdims=True) + epsilon)


def normed_projections(inputs, gain_row, weights):
    tok_count, width = inputs.shape
    rows, half = tok_count // 4, weights.shape[2] // 2

    def kernel(inputs_ref, gain_ref, weights_ref, normed_ref, first_ref, second_ref):
        value = inputs_ref[...].astype(f32)
        normed = (value * row_scale(value) * gain_ref[...]).astype(bf16)
        normed_ref[...] = normed
        for which, out in enumerate((first_ref, second_ref)):
            product = dot(normed, weights_ref[which], 1, 0).astype(bf16)
            out[0] = product[:, :half]
            out[1] = product[:, half:]

    halves = jax.ShapeDtypeStruct((2, tok_count, half), bf16)
    halves_block = pl.BlockSpec((2, rows, half), lambda i: (0, i, 0))
    row_block = pl.BlockSpec((rows, width), lambda i: (i, 0))
    return pl.pallas_call(
        kernel,
        out_shape=[jax.ShapeDtypeStruct(inputs.shape, bf16), halves, halves],
        grid=(4,),
        in_specs=[row_block, whole_block((1, width)), whole_block(weights.shape)],
        out_specs=[row_block, halves_block, halves_block],
        compiler_params=kernel_params(),
        name="normed_projections",
    )(inputs, gain_row[None], weights)


def allowed_pairs(seg_column, seg_row, start, rows):
    last = start + rows
    shape = (rows, last)
    places = lax.broadcasted_iota(jnp.int32, shape, 0) + start
    causal = lax.broadcasted_iota(jnp.int32, shape, 1) <= places
    return causal & (seg_column[start:last] == seg_row[:, :last])


def attend_forward(queries, keys, values, out_weight, seg_ids):
    tok_count, flat = queries.shape
    width, heads, rows = out_weight.shape[0], flat // HEAD_SIZE, tok_count // 4

    def kernel(q_ref, k_ref, v_ref, weight_ref, column_ref, row_ref, out_ref, branch_ref, log_ref):
        seg_column, seg_row = column_ref[...], row_ref[...]
        for start in range(0, tok_count, rows):
            last = start + rows
            allowed = allowed_pairs(seg_column, seg_row, start, rows)
            for head in range(heads):
                at = slice(head * HEAD_SIZE, (head + 1) * HEAD_SIZE)
                scores = dot(q_ref[start:last, at], k_ref[:last, at], 1, 1) * HEAD_SIZE ** (-0.5)
                scores = jnp.where(allowed, scores, negative)
                maximum = jnp.max(scores, axis=-1, keepdims=True)
                exponent = jnp.exp(scores - maximum)
                total = jnp.sum(exponent, axis=-1, keepdims=True)
                probs = (exponent * (1.0 / total)).astype(bf16)
                out_ref[start:last, at] = dot(probs, v_ref[:last, at], 1, 0).astype(bf16)
                log_ref[head, start:last] = maximum + jnp.log(total)
            branch_ref[start:last] = dot(out_ref[start:last], weight_ref[...], 1, 1).astype(bf16)

    shapes = [(tok_count, flat), (tok_count, width), (heads, tok_count, 1)]
    return pl.pallas_call(
        kernel,
        out_shape=[jax.ShapeDtypeStruct(s, k) for s, k in zip(shapes, (bf16, bf16, f32))],
        compiler_params=kernel_params(),
        name="attend_forward",
    )(queries, keys, values, out_weight, seg_ids[:, None], seg_ids[None])


def attend_backward(queries, keys, values, out_weight, grad_branch, seg_ids, log_total):
    tok_count, flat = queries.shape
    heads, rows = flat // HEAD_SIZE, tok_count // 4
    scale = HEAD_SIZE ** (-0.5)

    def kernel(q_ref, k_ref, v_ref, weight_ref, branch_ref, column_ref, row_ref, log_ref, dq_ref, dk_ref, dv_ref, dk_sum, dv_sum):
        seg_column, seg_row = column_ref[...], row_ref[...]
        dk_sum[...] = jnp.zeros_like(dk_sum)
        dv_sum[...] = jnp.zeros_like(dv_sum)
        for start in range(0, tok_count, rows):
            last = start + rows
            allowed = allowed_pairs(seg_column, seg_row, start, rows)
            grad_out = dot(branch_ref[start:last], weight_ref[...], 1, 0).astype(bf16)
            for head in range(heads):
                at = slice(head * HEAD_SIZE, (head + 1) * HEAD_SIZE)
                scores = dot(q_ref[start:last, at], k_ref[:last, at], 1, 1) * scale
                probs = jnp.exp(jnp.where(allowed, scores, negative) - log_ref[head, start:last])
                grad_probs = dot(grad_out[:, at], v_ref[:last, at], 1, 1)
                inner = jnp.sum(probs * grad_probs, axis=-1, keepdims=True)
                grad_scores = (probs * (grad_probs - inner)).astype(bf16)
                dq_ref[start:last, at] = (dot(grad_scores, k_ref[:last, at], 1, 0) * scale).astype(bf16)
                dk_sum[:last, at] += dot(grad_scores, q_ref[start:last, at], 0, 0)
                dv_sum[:last, at] += dot(probs.astype(bf16), grad_out[:, at], 0, 0)
        dk_ref[...] = (dk_sum[...] * scale).astype(bf16)
        dv_ref[...] = dv_sum[...].astype(bf16)

    return pl.pallas_call(
        kernel,
        out_shape=[jax.ShapeDtypeStruct((tok_count, flat), bf16)] * 3,
        scratch_shapes=[pltpu.VMEM((tok_count, flat), f32)] * 2,
        compiler_params=kernel_params(),
        name="attend_backward",
    )(queries, keys, values, out_weight, grad_branch, seg_ids[:, None], seg_ids[None], log_total)


def feed_forward_own(hidden_in, grad_hidden, gate_weight, up_weight):
    tok_count, width = hidden_in.shape
    units, rows = gate_weight.shape[0], tok_count // 4

    def kernel(in_ref, back_ref, gate_ref, up_ref, hidden_ref, grad_ref):
        gate = dot(in_ref[...], gate_ref[...], 1, 1)
        up = dot(in_ref[...], up_ref[...], 1, 1)
        back = back_ref[...]
        sig = jax.nn.sigmoid(gate)
        silu = gate * sig
        hidden_ref[...] = (silu * up).astype(bf16)
        grad_up = (back * silu).astype(bf16)
        grad_gate = (back * up * sig * (1.0 + gate * (1.0 - sig))).astype(bf16)
        grad = dot(grad_gate, gate_ref[...], 1, 0) + dot(grad_up, up_ref[...], 1, 0)
        grad_ref[...] = grad.astype(bf16)

    row_block = pl.BlockSpec((rows, width), lambda i: (i, 0))
    unit_block = pl.BlockSpec((rows, units), lambda i: (i, 0))
    weight = whole_block((units, width))
    return pl.pallas_call(
        kernel,
        out_shape=[jax.ShapeDtypeStruct((tok_count, units), bf16), jax.ShapeDtypeStruct((tok_count, width), bf16)],
        grid=(4,),
        in_specs=[row_block, unit_block, weight, weight],
        out_specs=[unit_block, row_block],
        compiler_params=kernel_params(),
        name="feed_forward_own",
    )(hidden_in, grad_hidden, gate_weight, up_weight)


def input_gradient(inputs, gain_row, first_grad, value_grad, weights, parts):
    tok_count, width = inputs.shape
    rows, columns, inner = tok_count // 4, width // parts, first_grad.shape[1]

    def kernel(inputs_ref, gain_ref, first_ref, value_ref, weights_ref, out_ref, gain_out):
        grad = dot(first_ref[...], weights_ref[0], 1, 1) + dot(value_ref[...], weights_ref[1], 1, 1)
        value = inputs_ref[...].astype(f32)
        inverse = row_scale(value)
        normal = value * inverse

        @pl.when(pl.program_id(0) == 0)
        def _():
            gain_out[...] = jnp.zeros_like(gain_out)

        gain_out[...] += jnp.sum(grad * normal, axis=0, keepdims=True)
        scaled = grad * gain_ref[...]
        inner_mean = jnp.mean(scaled * value, axis=-1, keepdims=True)
        result = (inverse * scaled - value * (inverse * inverse * inverse * inner_mean)).astype(bf16)
        for part in range(parts):
            out_ref[part] = result[:, part * columns : (part + 1) * columns]

    row_block = pl.BlockSpec((rows, width), lambda i: (i, 0))
    grad_block = pl.BlockSpec((rows, inner), lambda i: (i, 0))
    return pl.pallas_call(
        kernel,
        out_shape=[jax.ShapeDtypeStruct((parts, tok_count, columns), bf16), jax.ShapeDtypeStruct((1, width), f32)],
        grid=(4,),
        in_specs=[row_block, whole_block((1, width)), grad_block, grad_block, whole_block(weights.shape)],
        out_specs=[pl.BlockSpec((parts, rows, columns), lambda i: (0, i, 0)), pl.BlockSpec((1, width), lambda i: (0, 0))],
        compiler_params=kernel_params(),
        name="input_gradient",
    )(inputs, gain_row[None], first_grad, value_grad, weights)


def output_parts(hidden, down_weight, parts):
    tok_count, units = hidden.shape
    columns = down_weight.shape[1] // parts

    def kernel(hidden_ref, weight_ref, out_ref):
        out_ref[0] = dot(hidden_ref[...], weight_ref[...], 1, 0).astype(bf16)

    return pl.pallas_call(
        kernel,
        out_shape=jax.ShapeDtypeStruct((parts, tok_count, columns), bf16),
        grid=(parts,),
        in_specs=[whole_block((tok_count, units)), pl.BlockSpec((units, columns), lambda i: (0, i))],
        out_specs=pl.BlockSpec((1, tok_count, columns), lambda i: (i, 0, 0)),
        compiler_params=kernel_params(),
        name="output_parts",
    )(hidden, down_weight)


def gathers(group_count):
    return group_count in (2, 4)


def sum_plane(value):
    value = value + swap_section(value)
    both = lax.ppermute(value, "tensor", [(i, i ^ 3) for i in range(4)])
    return value, swap_low(value), swap_high(value), both


def sum_pairs(terms):
    return (terms[0] + terms[1]) + (terms[2] + terms[3])


def sum_over_groups(value):
    count = lax.axis_size("dp")

    def across(distance):
        return lax.ppermute(value, "dp", [(i, i ^ distance) for i in range(count)])

    if count == 4:
        return sum_pairs([value, across(1), across(2), across(3)])
    if count & (count - 1):
        return lax.psum(value, "dp")
    for bit in range(count.bit_length() - 1):
        value = value + across(2**bit)
    return value


def sum_groups(*grads):
    return [g.astype(f32) for g in lax.psum(tuple(g.astype(bf16) for g in grads), "dp")]


def shards(
    block_input,
    out_grad,
    seq_lengths,
    attn_gains,
    attn_weights,
    ffn_gain,
    gate_weight,
    up_weight,
    down_weight,
):
    tok_count, width = block_input.shape
    section = lax.axis_index("section")
    is_first = section == 0
    plane = lax.axis_size("section") * lax.axis_size("tensor")
    plane_pos = section * lax.axis_size("tensor") + lax.axis_index("tensor")
    rows, columns = tok_count // plane, width // plane
    row_start = plane_pos * rows

    def own_rows(value):
        return lax.dynamic_slice_in_dim(value, row_start, rows, 0)

    all_tokens = gathers(lax.axis_size("dp"))
    grad_slices, grad_near = None, []
    if all_tokens:
        grad_slice, block_input = meet(tensor_rows(out_grad), block_input)
        grad_slices = lax.all_gather(grad_slice, "dp", axis=0, tiled=False)
    seg_ids = segment_ids(seq_lengths[0], tok_count)
    is_valid = (seg_ids < seq_lengths.shape[1]).astype(f32)[:, None]
    gain_row = attn_gains[0].astype(f32)
    weights = attn_weights[0]
    w_second = weights[1]
    half = weights.shape[2] // 2
    normed, first_proj, second_proj = normed_projections(block_input, gain_row, weights)

    first_own, first_met = pick(first_proj, section), swap_section(pick(first_proj, 1 - section))
    second_met = lax.ppermute(second_proj[1], "section", [(0, 1)])
    out_weight_met = lax.ppermute(w_second[:, :half], "section", [(1, 0)])
    queries = jnp.where(is_first, first_met, first_own)
    keys = jnp.where(is_first, first_own, first_met)
    values = jnp.where(is_first, second_proj[0], second_met)
    out_weight = jnp.where(is_first, out_weight_met, w_second[:, half:])

    attn_out, branch_part, log_total = attend_forward(queries, keys, values, out_weight, seg_ids)
    branch = scatter_sum(branch_part.reshape(plane, rows, width))
    branch, grad_slices = meet(branch, grad_slices)
    residual = own_rows(block_input).astype(f32) + branch
    resid_inv = lax.rsqrt(jnp.mean(residual * residual, axis=-1, keepdims=True) + epsilon)
    gain_ffn = ffn_gain.astype(f32)
    hidden_block = (residual * resid_inv * gain_ffn).astype(bf16)
    hidden_in = gather_plane(hidden_block)
    if all_tokens:
        hidden_block, grad_slices = meet(hidden_block, grad_slices)
        hidden_all = lax.all_gather(hidden_block, ("dp", "section", "tensor"), axis=0, tiled=True)
        grad_near = other_groups(grad_slices)
        grad_near, hidden_in = meet(grad_near, hidden_in)
    branch_sq = jnp.sum(branch * branch * own_rows(is_valid))

    def whole_units(hidden_in, out_grad):
        gate_act, up_act = dot(hidden_in, gate_weight, 1, 0), dot(hidden_in, up_weight, 1, 0)
        grad_hidden = dot(out_grad, down_weight, 1, 1)
        sig = jax.nn.sigmoid(gate_act)
        hidden = (gate_act * sig * up_act).astype(bf16)
        grad_up = (grad_hidden * gate_act * sig).astype(bf16)
        grad_gate = (grad_hidden * up_act * sig * (1.0 + gate_act * (1.0 - sig))).astype(bf16)
        return dot(hidden, out_grad, 0, 0), dot(hidden_in, grad_gate, 0, 0), dot(hidden_in, grad_up, 0, 0)

    gate_units, up_units = gate_weight.T, up_weight.T
    hidden, grad_hidden_part = feed_forward_own(hidden_in, dot(out_grad, down_weight, 1, 1), gate_units, up_units)
    grad_half, hidden = meet(scatter_half(grad_hidden_part.reshape(plane, rows, width)), hidden)
    grad_terms, output_part = meet(scatter_across(grad_half), output_parts(hidden, down_weight, plane))
    grad_hidden_in = scatter_last(*grad_terms)
    ffn_gain_term = jnp.sum(grad_hidden_in * residual * resid_inv, axis=0)
    grad_residual = own_rows(out_grad).astype(f32) + norm_back(residual, resid_inv, gain_ffn, grad_hidden_in)
    grad_branch_low = gather_plane(grad_residual.astype(bf16))
    if all_tokens:
        grad_near, grad_branch_low = meet(grad_near, grad_branch_low)
        grad_high = [swap_high(grad_near[0])]

    def add_own(parts, own):
        own = own.reshape(rows, plane, columns).transpose(1, 0, 2)
        mixed = (lax.dynamic_slice_in_dim(parts, row_start, rows, 1).astype(f32) + own).astype(bf16)
        return lax.dynamic_update_slice_in_dim(parts, mixed, row_start, 1)

    output_half = scatter_half(add_own(output_part, residual))
    grad_q, grad_k, grad_v = attend_backward(
        queries, keys, values, out_weight, grad_branch_low, seg_ids, log_total
    )
    second_back = swap_section(jnp.where(is_first, attn_out, grad_v))

    def joined(own, met):
        return jnp.concatenate([jnp.where(is_first, own, met), jnp.where(is_first, met, own)], axis=1)

    second_right = joined(jnp.where(is_first, grad_v, attn_out), second_back)
    second_left = jnp.where(is_first, normed, grad_branch_low)
    second_sum = dot(second_left, second_right, 0, 0).astype(bf16)
    if len(grad_near) > 1:
        second_back, grad_high, grad_near[1] = meet(second_back, grad_high, grad_near[1])
        grad_high.append(swap_high(grad_near[1]))
    first_back = swap_section(jnp.where(is_first, grad_q, grad_k))
    if len(grad_near) > 2:
        first_back, grad_high, grad_near[2] = meet(first_back, grad_high, grad_near[2])
        grad_high.append(swap_high(grad_near[2]))
    first_grad = joined(jnp.where(is_first, grad_k, grad_q), first_back)
    value_grad = jnp.where(is_first, second_right, jnp.zeros_like(second_right))
    first_sum = dot(normed, first_grad, 0, 0).astype(bf16)
    output_half, first_sum, second_sum = meet(output_half, first_sum, second_sum)
    output_terms = scatter_across(output_half)
    if all_tokens:
        first_sum, second_sum, hidden_all = meet(first_sum, second_sum, hidden_all)
        grad_pieces = [by_slice(out_grad)] + grad_near + grad_high
        grad_pieces += [swap_low(v) for v in grad_near] + [swap_low(v) for v in grad_high]
        tensor, group, groups = lax.axis_index("tensor"), lax.axis_index("dp"), lax.axis_size("dp")
        order = [group * 4 + i for i in range(4)]
        order += [(group ^ k) * 4 + (tensor ^ i) for i in (0, 2, 1, 3) for k in range(1, groups)]
        down_grad, gate_grad, up_grad = feed_forward_grads(
            jnp.stack(order).astype(jnp.int32),
            hidden_all.reshape(4 * groups, -1, width),
            grad_pieces,
            gate_units,
            up_units,
            down_weight,
        )
        output_terms, first_grad, value_grad, down_grad = meet(output_terms, first_grad, value_grad, down_grad)
        gate_grad, up_grad = gate_grad.T, up_grad.T
    else:
        down_grad, gate_grad, up_grad = sum_groups(*whole_units(hidden_in, out_grad))
    input_part, attn_gain_term = input_gradient(block_input, gain_row, first_grad, value_grad, weights, plane)
    input_terms = scatter_across(scatter_half(add_own(input_part, grad_residual)))
    output_sum = scatter_last(*output_terms)
    block_output = output_sum.astype(bf16)
    output_sq = jnp.sum(output_sum * output_sum * is_valid)

    count_term = jnp.where(plane_pos == 0, jnp.sum(seq_lengths).astype(f32), 0.0)
    section_rows = jnp.where(
        jnp.arange(2, dtype=jnp.int32)[:, None] == section, attn_gain_term, 0.0
    )
    stat_terms = jnp.pad(jnp.stack([output_sq, branch_sq, count_term]), (0, width - 3))
    terms = jnp.concatenate([section_rows, ffn_gain_term[None, :], stat_terms[None, :]], axis=0)
    gains = sum_plane(terms)
    first_sum, second_sum = lax.psum((first_sum, second_sum), "dp")
    if all_tokens:
        first_sum, second_sum, input_terms, gains = meet(first_sum, second_sum, input_terms, gains)
    input_grad = scatter_last(*input_terms).astype(bf16)
    gains = sum_over_groups(sum_pairs(gains))
    attn_weight_grad = jnp.stack([first_sum, second_sum])[None].astype(f32)

    stats = gains[3]
    attn_gain_grad = lax.dynamic_slice_in_dim(gains, section, 1, 0)
    activation_rms = jnp.sqrt(stats[:2] / (stats[2] * width))
    return (
        block_output,
        input_grad,
        attn_gain_grad,
        attn_weight_grad,
        gains[2],
        gate_grad,
        up_grad,
        down_grad,
        activation_rms,
    )


def solution(mesh):
    both = ("section", "tensor")
    in_specs = (
        P("dp", None),
        P("dp", None),
        P("dp", None),
        P("section", None),
        P("section", None, None, "tensor"),
        P(),
        P(None, both),
        P(None, both),
        P(both, None),
    )
    out_specs = (
        P("dp", both),
        P("dp", both),
        P("section", None),
        P("section", None, None, "tensor"),
        P(),
        P(None, both),
        P(None, both),
        P(both, None),
        P(),
    )
    return jax.shard_map(
        shards, mesh=mesh, in_specs=in_specs, out_specs=out_specs, check_vma=False
    )
```

time: 689 us -> 515 us (0.75)
  waiting for transfers between devices: 410 us -> 180 us
  Pallas kernels: 0 us -> 157 us
  matrix products: 90.3 us -> 15.9 us
  blocking collectives: 43.8 us -> 0 us
  starting transfers between devices: 34.2 us -> 58.3 us
  other arithmetic: 57.7 us -> 42.4 us
    psum x2 -> x1, waiting for transfers between devices: 279 us -> 12.4 us  [shards(): first_sum, second_sum = lax.psum((first_sum, second_sum), 'dp')]
    pallas_call x0 -> x7, Pallas kernels: none -> 157 us  [the longest x1 85.8 us: feed_forward_grads(): pl.pallas_call(kernel, out_shape=[jax.ShapeDtypeStruct((units, width), f3...]
    dot_general x17 -> x3, matrix products: 75.1 us -> 15.9 us  [dot(): lax.dot_general(left, right, (((left_dim,), (right_dim,)), ((), ())), pre...]
    psum x1 -> x0, blocking collectives: 43.8 us -> none  [shards(): lax.psum((gain_terms, stat_terms), ('section', 'dp', 'tensor'))]
    ppermute x6 -> x16, waiting for transfers between devices: 41.6 us -> 78.8 us  [swap_high(): return lax.ppermute(value, 'tensor', SWAP_HIGH)]
    convert_element_type x12 -> x15, other arithmetic: 34.3 us -> 14.9 us  [the longest x12 9.33 us: add_low(): return (left.astype(f32) + right.astype(f32)).astype(bf16)]
    ppermute x7 -> x5, waiting for transfers between devices: 26.3 us -> 10.6 us  [the longest x1 7.99 us: shards(): second_met = lax.ppermute(second_proj[1], 'section', [(0, 1)])]
    dot_general x6 -> x0, matrix products: 15.2 us -> none  [the longest x1 4.86 us: attend_backward(): jnp.einsum('qhd,khd->hqk', g_heads, v_heads, preferred_element_type=f32)]
  transfers between devices with their start and end apart: 37 -> 62, of which waited for: 21 -> 31; matrix products, arithmetic and copies ran while one was open for 16% -> 17% of each run, Pallas kernels for 0% -> 31%
where the time goes in v2:
time: 515 us; the launch traced here: 507 us
  waiting for transfers between devices  180 us (35%)
  Pallas kernels  157 us (30%)
  starting transfers between devices  58.3 us (11%)
  other arithmetic  42.4 us (8%)
  local copies, waits for them, and re-layouts  36.6 us (7%)
  between operations  16.3 us (3%)
  matrix products  15.9 us (3%)
    pallas_call x1, Pallas kernels, feed_forward_grads(): pl.pallas_call(kernel, out_shape=[jax.ShapeDtypeStruct((units, width), f3...  85.8 us
    ppermute x16, waiting for transfers between devices, swap_high(): return lax.ppermute(value, 'tensor', SWAP_HIGH)  78.8 us
    ppermute x16, waiting for transfers between devices, swap_section(): return lax.ppermute(value, 'section', SWAP_SECTION)  55.7 us
    ppermute x16, starting transfers between devices, swap_high(): return lax.ppermute(value, 'tensor', SWAP_HIGH)  21.7 us
    ppermute x16, starting transfers between devices, swap_section(): return lax.ppermute(value, 'section', SWAP_SECTION)  21.6 us
    pallas_call x1, Pallas kernels, feed_forward_own(): pl.pallas_call(kernel, out_shape=[jax.ShapeDtypeStruct((tok_count, units)...  18.1 us
    dot_general x3, matrix products, dot(): lax.dot_general(left, right, (((left_dim,), (right_dim,)), ((), ())), pre...  15.9 us
    pallas_call x1, Pallas kernels, input_gradient(): pl.pallas_call(kernel, out_shape=[jax.ShapeDtypeStruct((parts, tok_count,...  13.8 us
  transfers between devices with their start and end apart: 62, of which 31 were waited for; matrix products, arithmetic and copies ran while one was open for 17% of the time, Pallas kernels for 31%

profile of v2, /device:TPU:0, one launch (start us, length us, event | category | flops | bytes accessed | tf_op | source)
XLA Modules:
  0.0 506.8 jit_solution(4814483010300403457)
XLA Ops:
  11.9 2.3 constant_dynamic-slice_fusion.4
  14.2 9.1 %normed_projections.1 = (bf16[960,2048]{1,0:T(8,128)(2,1)}, bf16[2,960,256]{2,1,0:T(8,128)(2,1)}, bf16[2,960,256]{2,1,0:T(8,128)(2,1)}) custom-call(bf16[960,2048]{1,0:T(8,128)(2,1)} %inputs_ref.1, f32[1,2048]{1,0:T(1,128)} %convert_element_type.229.gain_ref, bf16[2,2048,512]{2,1,0:T(8,128)(2,1)} %bitcast.148), custom_call_target="tpu_custom_call" | custom-call | tf_op jit(solution)/shard_map/normed_projections/pallas_call | solution.py:275
  25.1 5.7 %collective-permute-start.1 = (bf16[960,256]{1,0:T(8,128)(2,1)}, bf16[960,256]{1,0:T(8,128)(2,1)}, u32[]{:S(2)}, u32[]{:S(2)}) collective-permute-start(bf16[960,256]{1,0:T(8,128)(2,1)} %slice_bitcast_fusion.1), channel_id=1, source_target_pairs={{0,16},{1,17},{2,18},{3,19},{4,20},{5,21},{6,22},{7,23},{8,24},{9,... | collective-permute-start | bytes 1474568 | tf_op jit(solution)/shard_map/ppermute | solution.py:510
  33.9 8.0 %collective-permute-done.1 = bf16[960,256]{1,0:T(8,128)(2,1)} collective-permute-done((bf16[960,256]{1,0:T(8,128)(2,1)}, bf16[960,256]{1,0:T(8,128)(2,1)}, u32[]{:S(2)}, u32[]{:S(2)}) %collective-permute-start.1) | collective-permute-done | bytes 491552 | tf_op jit(solution)/shard_map/ppermute | solution.py:510
  43.8 7.5 %collective-permute-done = bf16[960,256]{1,0:T(8,128)(2,1)} collective-permute-done((bf16[960,256]{1,0:T(8,128)(2,1)}, bf16[960,256]{1,0:T(8,128)(2,1)}, u32[]{:S(2)}, u32[]{:S(2)}) %collective-permute-start) | collective-permute-done | bytes 491552 | tf_op jit(solution)/shard_map/ppermute | solution.py:38
  51.3 2.2 bitcast_select_fusion.1
  54.6 9.7 %attend_forward.1 = (bf16[960,256]{1,0:T(8,128)(2,1)}, bf16[960,2048]{1,0:T(8,128)(2,1)}, f32[2,960,1]{2,1,0:T(8,128)}) custom-call(bf16[960,256]{1,0:T(8,128)(2,1)} %get-tuple-element.183.q_ref, bf16[960,256]{1,0:T(8,128)(2,1)} %get-tuple-element.182.k_ref, bf16[960,256]{1,0:T(8,128)(2,1)} %bitcast_select_fusion.v_ref, ...), custom_call_target="tpu_custom_call" | custom-call | tf_op jit(solution)/shard_map/attend_forward/pallas_call | solution.py:316
  66.1 4.0 collective-permute-done.3
  70.2 2.9 fusion.3
  73.2 2.6 collective-permute-start.6
  75.8 2.4 collective-permute-start.4
  78.3 3.8 collective-permute-done.6
  82.2 2.4 collective-permute-start.7
  86.6 9.1 %collective-permute-done.7 = bf16[120,2048]{1,0:T(8,128)(2,1)S(1)} collective-permute-done((bf16[120,2048]{1,0:T(8,128)(2,1)S(1)}, bf16[120,2048]{1,0:T(8,128)(2,1)S(1)}, u32[]{:S(2)}, u32[]{:S(2)}) %collective-permute-start.7) | collective-permute-done | bytes 491552 | tf_op jit(solution)/shard_map/ppermute | solution.py:34
  98.6 13.5 %all-gather.6.cloned.1.call-done = bf16[960,2048]{1,0:T(8,128)(2,1)} async-done(((bf16[240,2048]{1,0:T(8,128)(2,1)}), bf16[960,2048]{1,0:T(8,128)(2,1)}) %all-gather.6.cloned.1.call-update) | async-done | bytes 3932176 | tf_op jit(solution)/shard_map/all_gather | solution.py:500
  112.2 2.0 multiply_reduce_fusion.4
  114.1 2.4 broadcast.48.clone
  121.2 7.9 %fusion.27.back_ref = f32[960,688]{1,0:T(8,128)} fusion(bf16[960,2048]{1,0:T(8,128)(2,1)} %param.10, bf16[688,2048]{1,0:T(8,128)(2,1)} %refs_15_.1), kind=kOutput, calls=%fused_computation.140 | convolution fusion | flops 2705326080 | bytes 9392128 | tf_op jit(solution)/shard_map/dot_general | solution.py:137
  129.1 5.8 %collective-permute-done.9 = bf16[120,2048]{1,0:T(8,128)(2,1)S(1)} collective-permute-done((bf16[120,2048]{1,0:T(8,128)(2,1)}, bf16[120,2048]{1,0:T(8,128)(2,1)S(1)}, u32[]{:S(2)}, u32[]{:S(2)}) %collective-permute-start.9) | collective-permute-done | bytes 491552 | tf_op jit(solution)/shard_map/ppermute | solution.py:38
  134.9 3.6 constant_dynamic-slice_fusion.1
  143.3 3.7 collective-permute-done.13
  153.5 18.1 %feed_forward_own.1 = (bf16[960,688]{1,0:T(8,128)(2,1)}, bf16[960,2048]{1,0:T(8,128)(2,1)}) custom-call(bf16[960,2048]{1,0:T(8,128)(2,1)} %constant_dynamic-update-slice_fusion.18.in_ref, f32[960,688]{1,0:T(8,128)} %fusion.27.back_ref, bf16[688,2048]{1,0:T(8,128)(2,1)} %bitcast.154, bf16[688,2048]{1,0:T(8,128)(2,1)} %bitcast.156), custom_call_target="tpu_custom_call" | custom-call | tf_op jit(solution)/shard_map/feed_forward_own/pallas_call | solution.py:378
  174.0 3.6 collective-permute-done.17
  180.8 8.8 %output_parts.1 = bf16[8,960,256]{2,1,0:T(8,128)(2,1)} custom-call(bf16[960,688]{1,0:T(8,128)(2,1)} %get-tuple-element.90.hidden_ref, bf16[688,2048]{1,0:T(8,128)(2,1)} %refs_15_.1), custom_call_target="tpu_custom_call" | custom-call | tf_op jit(solution)/shard_map/output_parts/pallas_call | solution.py:430
  189.7 2.8 collective-permute-done.19
  196.4 20.9 %collective-permute-done.22 = bf16[120,2048]{1,0:T(8,128)(2,1)S(1)} collective-permute-done((bf16[120,2048]{1,0:T(8,128)(2,1)S(1)}, bf16[120,2048]{1,0:T(8,128)(2,1)S(1)}, u32[]{:S(2)}, u32[]{:S(2)}) %collective-permute-start.22) | collective-permute-done | bytes 491552 | tf_op jit(solution)/shard_map/ppermute | solution.py:34
  225.4 9.6 %collective-permute-done.24 = bf16[120,2048]{1,0:T(8,128)(2,1)S(1)} collective-permute-done((bf16[120,2048]{1,0:T(8,128)(2,1)S(1)}, bf16[120,2048]{1,0:T(8,128)(2,1)S(1)}, u32[]{:S(2)}, u32[]{:S(2)}) %collective-permute-start.24) | collective-permute-done | bytes 491552 | tf_op jit(solution)/shard_map/ppermute | solution.py:38
  239.9 5.4 %collective-permute-done.28 = bf16[120,1024]{1,0:T(8,128)(2,1)S(1)} collective-permute-done((bf16[120,1024]{1,0:T(8,128)(2,1)S(1)}, bf16[120,1024]{1,0:T(8,128)(2,1)S(1)}, u32[]{:S(2)}, u32[]{:S(2)}) %collective-permute-start.28) | collective-permute-done | bytes 245792 | tf_op jit(solution)/shard_map/ppermute | solution.py:34
  250.0 11.9 %attend_backward.1 = (bf16[960,256]{1,0:T(8,128)(2,1)}, bf16[960,256]{1,0:T(8,128)(2,1)}, bf16[960,256]{1,0:T(8,128)(2,1)}) custom-call(bf16[960,256]{1,0:T(8,128)(2,1)} %get-tuple-element.183.q_ref, bf16[960,256]{1,0:T(8,128)(2,1)} %get-tuple-element.182.k_ref, bf16[960,256]{1,0:T(8,128)(2,1)} %bitcast_select_fusion.v_ref, ...), custom_call_target="tpu_custom_call" | custom-call | tf_op jit(solution)/shard_map/attend_backward/pallas_call | solution.py:350
  263.9 11.7 %collective-permute-done.33 = bf16[960,256]{1,0:T(8,128)(2,1)} collective-permute-done((bf16[960,256]{1,0:T(8,128)(2,1)S(1)}, bf16[960,256]{1,0:T(8,128)(2,1)}, u32[]{:S(2)}, u32[]{:S(2)}) %collective-permute-start.33) | collective-permute-done | bytes 491552 | tf_op jit(solution)/shard_map/ppermute | solution.py:38
  280.4 3.1 fusion.1
  284.6 7.6 %collective-permute-done.32 = bf16[960,256]{1,0:T(8,128)(2,1)S(1)} collective-permute-done((bf16[960,256]{1,0:T(8,128)(2,1)S(1)}, bf16[960,256]{1,0:T(8,128)(2,1)S(1)}, u32[]{:S(2)}, u32[]{:S(2)}) %collective-permute-start.32) | collective-permute-done | bytes 491552 | tf_op jit(solution)/shard_map/ppermute | solution.py:38
  292.2 6.9 %collective-permute-done.35.refs_5_ = bf16[1,240,2048]{2,1,0:T(8,128)(2,1)} collective-permute-done((bf16[1,240,2048]{2,1,0:T(8,128)(2,1)}, bf16[1,240,2048]{2,1,0:T(8,128)(2,1)}, u32[]{:S(2)}, u32[]{:S(2)}) %collective-permute-start.35) | collective-permute-done | bytes 983072 | tf_op jit(solution)/shard_map/ppermute | solution.py:34
  300.4 4.2 fusion.7
  305.8 16.0 %collective-permute-done.38.refs_6_ = bf16[1,240,2048]{2,1,0:T(8,128)(2,1)} collective-permute-done((bf16[1,240,2048]{2,1,0:T(8,128)(2,1)}, bf16[1,240,2048]{2,1,0:T(8,128)(2,1)}, u32[]{:S(2)}, u32[]{:S(2)}) %collective-permute-start.38) | collective-permute-done | bytes 983072 | tf_op jit(solution)/shard_map/ppermute | solution.py:34
  321.8 3.8 convolution_convert_fusion
  329.0 2.3 broadcast_select_fusion.value_ref
  332.4 85.8 %feed_forward_grads.1 = (f32[688,2048]{1,0:T(8,128)}, f32[688,2048]{1,0:T(8,128)}, f32[688,2048]{1,0:T(8,128)}) custom-call(s32[16]{0:T(128)} %stack.88.order_ref, bf16[16,240,2048]{2,1,0:T(8,128)(2,1)} %bitcast.153, bf16[4,240,2048]{2,1,0:T(8,128)(2,1)} %bitcast.158, bf16[1,240,2048]{2,1,0:T(8,128)(2,1)} %get-tuple-element.107.refs_1_, ...), custom_call_target="tpu_custom_call" | custom-call | tf_op jit(solution)/shard_map/feed_forward_grads/pallas_call | solution.py:230
  418.2 13.8 %input_gradient.1 = (bf16[8,960,256]{2,1,0:T(8,128)(2,1)}, f32[1,2048]{1,0:T(1,128)}) custom-call(bf16[960,2048]{1,0:T(8,128)(2,1)} %inputs_ref.1, f32[1,2048]{1,0:T(1,128)} %convert_element_type.229.gain_ref, bf16[960,512]{1,0:T(8,128)(2,1)} %pad_maximum_fusion.first_ref, bf16[960,512]{1,0:T(8,128)(2,1)} %broadcast_select_fusion.value_ref, ...), custom_call_target="tpu_custom_call" | custom-call | tf_op jit(solution)/shard_map/input_gradient/pallas_call | solution.py:412
  432.1 2.0 fusion.17
  434.1 2.9 dynamic-slice_bitcast_fusion
  442.1 9.8 %collective-permute-done.46 = bf16[960,256]{1,0:T(8,128)(2,1)S(1)} collective-permute-done((bf16[960,256]{1,0:T(8,128)(2,1)}, bf16[960,256]{1,0:T(8,128)(2,1)S(1)}, u32[]{:S(2)}, u32[]{:S(2)}) %collective-permute-start.46) | collective-permute-done | bytes 491552 | tf_op jit(solution)/shard_map/ppermute | solution.py:34
  457.3 2.0 fusion
  463.9 2.6 collective-permute-done.53
  468.1 12.4 %all-reduce.4.cloned.1.call-done = (bf16[2048,512]{1,0:T(8,128)(2,1)}, bf16[2048,512]{1,0:T(8,128)(2,1)}) async-done(((bf16[2048,512]{1,0:T(8,128)(2,1)}, bf16[2048,512]{1,0:T(8,128)(2,1)}), (bf16[2048,512]{1,0:T(8,128)(2,1)}, bf16[2048,512]{1,0:T(8,128)(2,1)})) %all-reduce.4.cloned.1.call-update) | async-done | bytes 4194320 | tf_op jit(solution)/shard_map/psum | solution.py:614
  482.2 2.9 collective-permute-start.56
  488.5 3.9 maximum_convert_fusion
  494.8 2.7 collective-permute-done.55
  (253 shorter events, 102.3 us)
Async XLA Ops:
  7.2 105.0 %all-gather.6.cloned.1.call-start = ((), (), s32[]{:S(2)}) async-start(), calls=%async_computation.1 | async-start | bytes 4915200 | tf_op jit(solution)/shard_map/all_gather | solution.py:500
  10.0 43.5 %collective-permute-start.2 = (bf16[2048,256]{1,0:T(8,128)(2,1)}, bf16[2048,256]{1,0:T(8,128)(2,1)S(1)}, u32[]{:S(2)}, u32[]{:S(2)}) collective-permute-start(bf16[2048,256]{1,0:T(8,128)(2,1)} %slice.150), channel_id=1, source_target_pairs={{16,0},{17,1},{18,2},{19,3},{20,4},{21,5},{22,6},{23,7},{24,8},{25... | collective-permute-start | bytes 3145736 | tf_op jit(solution)/shard_map/ppermute | solution.py:511
  25.1 16.8 %collective-permute-start.1 = (bf16[960,256]{1,0:T(8,128)(2,1)}, bf16[960,256]{1,0:T(8,128)(2,1)}, u32[]{:S(2)}, u32[]{:S(2)}) collective-permute-start(bf16[960,256]{1,0:T(8,128)(2,1)} %slice_bitcast_fusion.1), channel_id=1, source_target_pairs={{0,16},{1,17},{2,18},{3,19},{4,20},{5,21},{6,22},{7,23},{8,24},{9,... | collective-permute-start | bytes 1474568 | tf_op jit(solution)/shard_map/ppermute | solution.py:510
  32.6 18.7 %collective-permute-start = (bf16[960,256]{1,0:T(8,128)(2,1)}, bf16[960,256]{1,0:T(8,128)(2,1)}, u32[]{:S(2)}, u32[]{:S(2)}) collective-permute-start(bf16[960,256]{1,0:T(8,128)(2,1)} %dynamic-slice_bitcast_fusion.19), channel_id=1, source_target_pairs={{0,16},{16,0},{1,17},{17,1},{2,18},{18,2},{3,19},{19,3},{4,20},{20... | collective-permute-start | bytes 1474568 | tf_op jit(solution)/shard_map/ppermute | solution.py:38
  32.6 292.9 %all-gather.4.cloned.1.call-start = ((), (), s32[]{:S(2)}) async-start(), calls=%async_computation | async-start | bytes 16220160 | tf_op jit(solution)/shard_map/all_gather | solution.py:527
  73.2 8.8 %collective-permute-start.6 = (bf16[120,1024]{1,0:T(8,128)(2,1)S(1)}, bf16[120,1024]{1,0:T(8,128)(2,1)S(1)}, u32[]{:S(2)}, u32[]{:S(2)}) collective-permute-start(bf16[120,1024]{1,0:T(8,128)(2,1)S(1)} %get-tuple-element.192), channel_id=1, source_target_pairs={{0,16},{16,0},{1,17},{17,1},{2,18},{18,2},{3,19},{19,3},{4,20},{20... | collective-permute-start | bytes 737288 | tf_op jit(solution)/shard_map/ppermute | solution.py:38
  75.8 8.7 %collective-permute-start.4 = (bf16[120,1024]{1,0:T(8,128)(2,1)S(1)}, bf16[120,1024]{1,0:T(8,128)(2,1)S(1)}, u32[]{:S(2)}, u32[]{:S(2)}) collective-permute-start(bf16[120,1024]{1,0:T(8,128)(2,1)S(1)} %get-tuple-element.191), channel_id=1, source_target_pairs={{0,2},{1,3},{2,0},{3,1},{4,6},{5,7},{6,4},{7,5},{8,10},{9,11},{10,... | collective-permute-start | bytes 737288 | tf_op jit(solution)/shard_map/ppermute | solution.py:34
  82.2 13.5 %collective-permute-start.7 = (bf16[120,2048]{1,0:T(8,128)(2,1)S(1)}, bf16[120,2048]{1,0:T(8,128)(2,1)S(1)}, u32[]{:S(2)}, u32[]{:S(2)}) collective-permute-start(bf16[120,2048]{1,0:T(8,128)(2,1)S(1)} %pad_maximum_fusion.4), channel_id=1, source_target_pairs={{0,2},{1,3},{2,0},{3,1},{4,6},{5,7},{6,4},{7,5},{8,10},{9,11},{10,... | collective-permute-start | bytes 1474568 | tf_op jit(solution)/shard_map/ppermute | solution.py:34
  84.7 12.7 %collective-permute-start.5 = (bf16[120,2048]{1,0:T(8,128)(2,1)S(1)}, bf16[120,2048]{1,0:T(8,128)(2,1)}, u32[]{:S(2)}, u32[]{:S(2)}) collective-permute-start(bf16[120,2048]{1,0:T(8,128)(2,1)S(1)} %pad_maximum_fusion.3), channel_id=1, source_target_pairs={{0,16},{16,0},{1,17},{17,1},{2,18},{18,2},{3,19},{19,3},{4,20},{20... | collective-permute-start | bytes 1474568 | tf_op jit(solution)/shard_map/ppermute | solution.py:38
  117.7 362.9 %all-reduce.4.cloned.1.call-start = ((), (), s32[]{:S(2)}) async-start(), calls=%async_computation.2 | async-start | bytes 8388608 | tf_op jit(solution)/shard_map/psum | solution.py:614
  118.2 16.8 %collective-permute-start.9 = (bf16[120,2048]{1,0:T(8,128)(2,1)}, bf16[120,2048]{1,0:T(8,128)(2,1)S(1)}, u32[]{:S(2)}, u32[]{:S(2)}) collective-permute-start(bf16[120,2048]{1,0:T(8,128)(2,1)} %get-tuple-element.116), channel_id=1, source_target_pairs={{0,16},{16,0},{1,17},{17,1},{2,18},{18,2},{3,19},{19,3},{4,20},{20... | collective-permute-start | bytes 1474568 | tf_op jit(solution)/shard_map/ppermute | solution.py:38
  119.8 21.9 %collective-permute-start.8 = (bf16[120,2048]{1,0:T(8,128)(2,1)}, bf16[120,2048]{1,0:T(8,128)(2,1)S(1)}, u32[]{:S(2)}, u32[]{:S(2)}) collective-permute-start(bf16[120,2048]{1,0:T(8,128)(2,1)} %get-tuple-element.116), channel_id=1, source_target_pairs={{0,1},{1,0},{2,3},{3,2},{4,5},{5,4},{6,7},{7,6},{8,9},{9,8},{10,11... | collective-permute-start | bytes 1474568 | tf_op jit(solution)/shard_map/ppermute | solution.py:30
  119.8 20.3 %collective-permute-start.11 = (bf16[120,2048]{1,0:T(8,128)(2,1)}, bf16[120,2048]{1,0:T(8,128)(2,1)S(1)}, u32[]{:S(2)}, u32[]{:S(2)}) collective-permute-start(bf16[120,2048]{1,0:T(8,128)(2,1)} %get-tuple-element.116), channel_id=1, source_target_pairs={{0,2},{1,3},{2,0},{3,1},{4,6},{5,7},{6,4},{7,5},{8,10},{9,11},{10,... | collective-permute-start | bytes 1474568 | tf_op jit(solution)/shard_map/ppermute | solution.py:34
  134.9 13.3 %collective-permute-start.10 = (bf16[120,2048]{1,0:T(8,128)(2,1)S(1)}, bf16[120,2048]{1,0:T(8,128)(2,1)S(1)}, u32[]{:S(2)}, u32[]{:S(2)}) collective-permute-start(bf16[120,2048]{1,0:T(8,128)(2,1)S(1)} %collective-permute-done.9), channel_id=1, source_target_pairs={{0,1},{1,0},{2,3},{3,2},{4,5},{5,4},{6,7},{7,6},{8,9},{9,8},{10,11... | collective-permute-start | bytes 1474568 | tf_op jit(solution)/shard_map/ppermute | solution.py:30
  138.6 8.4 %collective-permute-start.13 = (bf16[120,1024]{1,0:T(8,128)(2,1)S(1)}, bf16[120,1024]{1,0:T(8,128)(2,1)S(1)}, u32[]{:S(2)}, u32[]{:S(2)}) collective-permute-start(bf16[120,1024]{1,0:T(8,128)(2,1)S(1)} %slice.158), channel_id=1, source_target_pairs={{0,2},{1,3},{2,0},{3,1},{4,6},{5,7},{6,4},{7,5},{8,10},{9,11},{10,... | collective-permute-start | bytes 737288 | tf_op jit(solution)/shard_map/ppermute | solution.py:34
  140.1 8.1 %collective-permute-start.15 = (bf16[120,1024]{1,0:T(8,128)(2,1)S(1)}, bf16[120,1024]{1,0:T(8,128)(2,1)S(1)}, u32[]{:S(2)}, u32[]{:S(2)}) collective-permute-start(bf16[120,1024]{1,0:T(8,128)(2,1)S(1)} %slice.159), channel_id=1, source_target_pairs={{0,16},{16,0},{1,17},{17,1},{2,18},{18,2},{3,19},{19,3},{4,20},{20... | collective-permute-start | bytes 737288 | tf_op jit(solution)/shard_map/ppermute | solution.py:38
  141.6 8.2 %collective-permute-start.12 = (bf16[120,2048]{1,0:T(8,128)(2,1)S(1)}, bf16[120,2048]{1,0:T(8,128)(2,1)S(1)}, u32[]{:S(2)}, u32[]{:S(2)}) collective-permute-start(bf16[120,2048]{1,0:T(8,128)(2,1)S(1)} %collective-permute-done.11), channel_id=1, source_target_pairs={{0,1},{1,0},{2,3},{3,2},{4,5},{5,4},{6,7},{7,6},{8,9},{9,8},{10,11... | collective-permute-start | bytes 1474568 | tf_op jit(solution)/shard_map/ppermute | solution.py:30
  178.7 13.7 %collective-permute-start.19 = (bf16[120,1024]{1,0:T(8,128)(2,1)S(1)}, bf16[120,1024]{1,0:T(8,128)(2,1)S(1)}, u32[]{:S(2)}, u32[]{:S(2)}) collective-permute-start(bf16[120,1024]{1,0:T(8,128)(2,1)S(1)} %get-tuple-element.189), channel_id=1, source_target_pairs={{0,2},{1,3},{2,0},{3,1},{4,6},{5,7},{6,4},{7,5},{8,10},{9,11},{10,... | collective-permute-start | bytes 737288 | tf_op jit(solution)/shard_map/ppermute | solution.py:34
  179.4 13.7 %collective-permute-start.18 = (bf16[120,1024]{1,0:T(8,128)(2,1)S(1)}, bf16[120,1024]{1,0:T(8,128)(2,1)S(1)}, u32[]{:S(2)}, u32[]{:S(2)}) collective-permute-start(bf16[120,1024]{1,0:T(8,128)(2,1)S(1)} %get-tuple-element.190), channel_id=1, source_target_pairs={{0,16},{16,0},{1,17},{17,1},{2,18},{18,2},{3,19},{19,3},{4,20},{20... | collective-permute-start | bytes 737288 | tf_op jit(solution)/shard_map/ppermute | solution.py:38
  193.2 24.1 %collective-permute-start.22 = (bf16[120,2048]{1,0:T(8,128)(2,1)S(1)}, bf16[120,2048]{1,0:T(8,128)(2,1)S(1)}, u32[]{:S(2)}, u32[]{:S(2)}) collective-permute-start(bf16[120,2048]{1,0:T(8,128)(2,1)S(1)} %pad_maximum_fusion.6), channel_id=1, source_target_pairs={{0,2},{1,3},{2,0},{3,1},{4,6},{5,7},{6,4},{7,5},{8,10},{9,11},{10,... | collective-permute-start | bytes 1474568 | tf_op jit(solution)/shard_map/ppermute | solution.py:34
  194.8 24.0 %collective-permute-start.21 = (bf16[120,2048]{1,0:T(8,128)(2,1)S(1)}, bf16[120,2048]{1,0:T(8,128)(2,1)S(1)}, u32[]{:S(2)}, u32[]{:S(2)}) collective-permute-start(bf16[120,2048]{1,0:T(8,128)(2,1)S(1)} %pad_maximum_fusion.5), channel_id=1, source_target_pairs={{0,16},{16,0},{1,17},{17,1},{2,18},{18,2},{3,19},{19,3},{4,20},{20... | collective-permute-start | bytes 1474568 | tf_op jit(solution)/shard_map/ppermute | solution.py:38
  221.3 13.8 %collective-permute-start.24 = (bf16[120,2048]{1,0:T(8,128)(2,1)S(1)}, bf16[120,2048]{1,0:T(8,128)(2,1)S(1)}, u32[]{:S(2)}, u32[]{:S(2)}) collective-permute-start(bf16[120,2048]{1,0:T(8,128)(2,1)S(1)} %get-tuple-element.152), channel_id=1, source_target_pairs={{0,16},{16,0},{1,17},{17,1},{2,18},{18,2},{3,19},{19,3},{4,20},{20... | collective-permute-start | bytes 1474568 | tf_op jit(solution)/shard_map/ppermute | solution.py:38
  222.9 16.0 %collective-permute-start.26 = (bf16[120,2048]{1,0:T(8,128)(2,1)S(1)}, bf16[120,2048]{1,0:T(8,128)(2,1)S(1)}, u32[]{:S(2)}, u32[]{:S(2)}) collective-permute-start(bf16[120,2048]{1,0:T(8,128)(2,1)S(1)} %get-tuple-element.152), channel_id=1, source_target_pairs={{0,2},{1,3},{2,0},{3,1},{4,6},{5,7},{6,4},{7,5},{8,10},{9,11},{10,... | collective-permute-start | bytes 1474568 | tf_op jit(solution)/shard_map/ppermute | solution.py:34
  223.5 16.3 %collective-permute-start.23 = (bf16[120,2048]{1,0:T(8,128)(2,1)S(1)}, bf16[120,2048]{1,0:T(8,128)(2,1)S(1)}, u32[]{:S(2)}, u32[]{:S(2)}) collective-permute-start(bf16[120,2048]{1,0:T(8,128)(2,1)S(1)} %get-tuple-element.152), channel_id=1, source_target_pairs={{0,1},{1,0},{2,3},{3,2},{4,5},{5,4},{6,7},{7,6},{8,9},{9,8},{10,11... | collective-permute-start | bytes 1474568 | tf_op jit(solution)/shard_map/ppermute | solution.py:30
  235.1 11.5 %collective-permute-start.25 = (bf16[120,2048]{1,0:T(8,128)(2,1)S(1)}, bf16[120,2048]{1,0:T(8,128)(2,1)S(1)}, u32[]{:S(2)}, u32[]{:S(2)}) collective-permute-start(bf16[120,2048]{1,0:T(8,128)(2,1)S(1)} %collective-permute-done.24), channel_id=1, source_target_pairs={{0,1},{1,0},{2,3},{3,2},{4,5},{5,4},{6,7},{7,6},{8,9},{9,8},{10,11... | collective-permute-start | bytes 1474568 | tf_op jit(solution)/shard_map/ppermute | solution.py:30
  236.7 43.7 %collective-permute-start.20 = (bf16[4,960,256]{2,1,0:T(8,128)(2,1)S(1)}, bf16[4,960,256]{2,1,0:T(8,128)(2,1)}, u32[]{:S(2)}, u32[]{:S(2)}) collective-permute-start(bf16[4,960,256]{2,1,0:T(8,128)(2,1)S(1)} %dynamic-slice_bitcast_fusion.1), channel_id=1, source_target_pairs={{0,1},{1,0},{2,3},{3,2},{4,5},{5,4},{6,7},{7,6},{8,9},{9,8},{10,11... | collective-permute-start | bytes 5898248 | tf_op jit(solution)/shard_map/ppermute | solution.py:30
  248.1 27.5 %collective-permute-start.34 = (bf16[1,240,2048]{2,1,0:T(8,128)(2,1)}, bf16[1,240,2048]{2,1,0:T(8,128)(2,1)}, u32[]{:S(2)}, u32[]{:S(2)}) collective-permute-start(bf16[1,240,2048]{2,1,0:T(8,128)(2,1)} %get-tuple-element.107.refs_1_), channel_id=1, source_target_pairs={{0,2},{1,3},{2,0},{3,1},{4,6},{5,7},{6,4},{7,5},{8,10},{9,11},{10,... | collective-permute-start | bytes 2949128 | tf_op jit(solution)/shard_map/ppermute | solution.py:34
  262.0 13.6 %collective-permute-start.33 = (bf16[960,256]{1,0:T(8,128)(2,1)S(1)}, bf16[960,256]{1,0:T(8,128)(2,1)}, u32[]{:S(2)}, u32[]{:S(2)}) collective-permute-start(bf16[960,256]{1,0:T(8,128)(2,1)S(1)} %broadcast_select_fusion.6), channel_id=1, source_target_pairs={{0,16},{16,0},{1,17},{17,1},{2,18},{18,2},{3,19},{19,3},{4,20},{20... | collective-permute-start | bytes 1474568 | tf_op jit(solution)/shard_map/ppermute | solution.py:38
  275.6 23.5 %collective-permute-start.35 = (bf16[1,240,2048]{2,1,0:T(8,128)(2,1)}, bf16[1,240,2048]{2,1,0:T(8,128)(2,1)}, u32[]{:S(2)}, u32[]{:S(2)}) collective-permute-start(bf16[1,240,2048]{2,1,0:T(8,128)(2,1)} %get-tuple-element.110.refs_2_), channel_id=1, source_target_pairs={{0,2},{1,3},{2,0},{3,1},{4,6},{5,7},{6,4},{7,5},{8,10},{9,11},{10,... | collective-permute-start | bytes 2949128 | tf_op jit(solution)/shard_map/ppermute | solution.py:34
  277.4 27.9 %collective-permute-start.39 = (bf16[1,240,2048]{2,1,0:T(8,128)(2,1)}, bf16[1,240,2048]{2,1,0:T(8,128)(2,1)}, u32[]{:S(2)}, u32[]{:S(2)}) collective-permute-start(bf16[1,240,2048]{2,1,0:T(8,128)(2,1)} %get-tuple-element.107.refs_1_), channel_id=1, source_target_pairs={{0,1},{1,0},{2,3},{3,2},{4,5},{5,4},{6,7},{7,6},{8,9},{9,8},{10,11... | collective-permute-start | bytes 2949128 | tf_op jit(solution)/shard_map/ppermute | solution.py:30
  278.6 13.6 %collective-permute-start.32 = (bf16[960,256]{1,0:T(8,128)(2,1)S(1)}, bf16[960,256]{1,0:T(8,128)(2,1)S(1)}, u32[]{:S(2)}, u32[]{:S(2)}) collective-permute-start(bf16[960,256]{1,0:T(8,128)(2,1)S(1)} %broadcast_select_fusion.7), channel_id=1, source_target_pairs={{0,16},{16,0},{1,17},{17,1},{2,18},{18,2},{3,19},{19,3},{4,20},{20... | collective-permute-start | bytes 1474568 | tf_op jit(solution)/shard_map/ppermute | solution.py:38
  299.2 22.6 %collective-permute-start.38 = (bf16[1,240,2048]{2,1,0:T(8,128)(2,1)}, bf16[1,240,2048]{2,1,0:T(8,128)(2,1)}, u32[]{:S(2)}, u32[]{:S(2)}) collective-permute-start(bf16[1,240,2048]{2,1,0:T(8,128)(2,1)} %get-tuple-element.118.refs_3_), channel_id=1, source_target_pairs={{0,2},{1,3},{2,0},{3,1},{4,6},{5,7},{6,4},{7,5},{8,10},{9,11},{10,... | collective-permute-start | bytes 2949128 | tf_op jit(solution)/shard_map/ppermute | solution.py:34
  304.6 22.0 %collective-permute-start.40 = (bf16[1,240,2048]{2,1,0:T(8,128)(2,1)}, bf16[1,240,2048]{2,1,0:T(8,128)(2,1)}, u32[]{:S(2)}, u32[]{:S(2)}) collective-permute-start(bf16[1,240,2048]{2,1,0:T(8,128)(2,1)} %get-tuple-element.110.refs_2_), channel_id=1, source_target_pairs={{0,1},{1,0},{2,3},{3,2},{4,5},{5,4},{6,7},{7,6},{8,9},{9,8},{10,11... | collective-permute-start | bytes 2949128 | tf_op jit(solution)/shard_map/ppermute | solution.py:30
  304.6 27.8 %collective-permute-start.41 = (bf16[1,240,2048]{2,1,0:T(8,128)(2,1)}, bf16[1,240,2048]{2,1,0:T(8,128)(2,1)}, u32[]{:S(2)}, u32[]{:S(2)}) collective-permute-start(bf16[1,240,2048]{2,1,0:T(8,128)(2,1)} %get-tuple-element.118.refs_3_), channel_id=1, source_target_pairs={{0,1},{1,0},{2,3},{3,2},{4,5},{5,4},{6,7},{7,6},{8,9},{9,8},{10,11... | collective-permute-start | bytes 2949128 | tf_op jit(solution)/shard_map/ppermute | solution.py:30
  305.1 22.8 %collective-permute-start.42 = (bf16[1,240,2048]{2,1,0:T(8,128)(2,1)}, bf16[1,240,2048]{2,1,0:T(8,128)(2,1)}, u32[]{:S(2)}, u32[]{:S(2)}) collective-permute-start(bf16[1,240,2048]{2,1,0:T(8,128)(2,1)} %collective-permute-done.34.refs_4_), channel_id=1, source_target_pairs={{0,1},{1,0},{2,3},{3,2},{4,5},{5,4},{6,7},{7,6},{8,9},{9,8},{10,11... | collective-permute-start | bytes 2949128 | tf_op jit(solution)/shard_map/ppermute | solution.py:30
  305.3 27.1 %collective-permute-start.43 = (bf16[1,240,2048]{2,1,0:T(8,128)(2,1)}, bf16[1,240,2048]{2,1,0:T(8,128)(2,1)}, u32[]{:S(2)}, u32[]{:S(2)}) collective-permute-start(bf16[1,240,2048]{2,1,0:T(8,128)(2,1)} %collective-permute-done.35.refs_5_), channel_id=1, source_target_pairs={{0,1},{1,0},{2,3},{3,2},{4,5},{5,4},{6,7},{7,6},{8,9},{9,8},{10,11... | collective-permute-start | bytes 2949128 | tf_op jit(solution)/shard_map/ppermute | solution.py:30
  321.8 10.6 %collective-permute-start.44 = (bf16[1,240,2048]{2,1,0:T(8,128)(2,1)}, bf16[1,240,2048]{2,1,0:T(8,128)(2,1)}, u32[]{:S(2)}, u32[]{:S(2)}) collective-permute-start(bf16[1,240,2048]{2,1,0:T(8,128)(2,1)} %collective-permute-done.38.refs_6_), channel_id=1, source_target_pairs={{0,1},{1,0},{2,3},{3,2},{4,5},{5,4},{6,7},{7,6},{8,9},{9,8},{10,11... | collective-permute-start | bytes 2949128 | tf_op jit(solution)/shard_map/ppermute | solution.py:30
  326.6 91.6 %collective-permute-start.37 = (bf16[960,128]{1,0:T(8,128)(2,1)S(1)}, bf16[960,128]{1,0:T(8,128)(2,1)S(1)}, u32[]{:S(2)}, u32[]{:S(2)}) collective-permute-start(bf16[960,128]{1,0:T(8,128)(2,1)S(1)} %get-tuple-element.187), channel_id=1, source_target_pairs={{0,2},{1,3},{2,0},{3,1},{4,6},{5,7},{6,4},{7,5},{8,10},{9,11},{10,... | collective-permute-start | bytes 737288 | tf_op jit(solution)/shard_map/ppermute | solution.py:34
  327.9 90.3 %collective-permute-start.36 = (bf16[960,128]{1,0:T(8,128)(2,1)S(1)}, bf16[960,128]{1,0:T(8,128)(2,1)S(1)}, u32[]{:S(2)}, u32[]{:S(2)}) collective-permute-start(bf16[960,128]{1,0:T(8,128)(2,1)S(1)} %get-tuple-element.188), channel_id=1, source_target_pairs={{0,16},{16,0},{1,17},{17,1},{2,18},{18,2},{3,19},{19,3},{4,20},{20... | collective-permute-start | bytes 737288 | tf_op jit(solution)/shard_map/ppermute | solution.py:38
  437.1 20.3 %collective-permute-start.47 = (bf16[4,960,256]{2,1,0:T(8,128)(2,1)}, bf16[4,960,256]{2,1,0:T(8,128)(2,1)S(1)}, u32[]{:S(2)}, u32[]{:S(2)}) collective-permute-start(bf16[4,960,256]{2,1,0:T(8,128)(2,1)} %dynamic-slice_bitcast_fusion), channel_id=1, source_target_pairs={{0,1},{1,0},{2,3},{3,2},{4,5},{5,4},{6,7},{7,6},{8,9},{9,8},{10,11... | collective-permute-start | bytes 5898248 | tf_op jit(solution)/shard_map/ppermute | solution.py:30
  438.1 13.8 %collective-permute-start.46 = (bf16[960,256]{1,0:T(8,128)(2,1)}, bf16[960,256]{1,0:T(8,128)(2,1)S(1)}, u32[]{:S(2)}, u32[]{:S(2)}) collective-permute-start(bf16[960,256]{1,0:T(8,128)(2,1)} %pad_maximum_fusion.8), channel_id=1, source_target_pairs={{0,2},{1,3},{2,0},{3,1},{4,6},{5,7},{6,4},{7,5},{8,10},{9,11},{10,... | collective-permute-start | bytes 1474568 | tf_op jit(solution)/shard_map/ppermute | solution.py:34
  440.2 13.6 %collective-permute-start.45 = (bf16[960,256]{1,0:T(8,128)(2,1)}, bf16[960,256]{1,0:T(8,128)(2,1)S(1)}, u32[]{:S(2)}, u32[]{:S(2)}) collective-permute-start(bf16[960,256]{1,0:T(8,128)(2,1)} %pad_maximum_fusion.7), channel_id=1, source_target_pairs={{0,16},{16,0},{1,17},{17,1},{2,18},{18,2},{3,19},{19,3},{4,20},{20... | collective-permute-start | bytes 1474568 | tf_op jit(solution)/shard_map/ppermute | solution.py:38
  459.5 8.6 %collective-permute-start.49 = (bf16[960,128]{1,0:T(8,128)(2,1)S(1)}, bf16[960,128]{1,0:T(8,128)(2,1)S(1)}, u32[]{:S(2)}, u32[]{:S(2)}) collective-permute-start(bf16[960,128]{1,0:T(8,128)(2,1)S(1)} %get-tuple-element.185), channel_id=1, source_target_pairs={{0,2},{1,3},{2,0},{3,1},{4,6},{5,7},{6,4},{7,5},{8,10},{9,11},{10,... | collective-permute-start | bytes 737288 | tf_op jit(solution)/shard_map/ppermute | solution.py:34
  480.6 11.8 %collective-permute-start.58 = (f32[4,2048]{1,0:T(4,128)S(1)}, f32[4,2048]{1,0:T(4,128)S(1)}, u32[]{:S(2)}, u32[]{:S(2)}) collective-permute-start(f32[4,2048]{1,0:T(4,128)S(1)} %add_add_fusion.1), channel_id=1, source_target_pairs={{0,12},{4,8},{8,4},{12,0},{1,13},{5,9},{9,5},{13,1},{2,14},{6,10},... | collective-permute-start | bytes 98312 | tf_op jit(solution)/shard_map/ppermute | solution.py:459
  481.7 10.7 %collective-permute-start.57 = (f32[4,2048]{1,0:T(4,128)S(1)}, f32[4,2048]{1,0:T(4,128)S(1)}, u32[]{:S(2)}, u32[]{:S(2)}) collective-permute-start(f32[4,2048]{1,0:T(4,128)S(1)} %add_add_fusion.1), channel_id=1, source_target_pairs={{0,8},{4,12},{8,0},{12,4},{1,9},{5,13},{9,1},{13,5},{2,10},{6,14},... | collective-permute-start | bytes 98312 | tf_op jit(solution)/shard_map/ppermute | solution.py:459
  482.2 10.3 %collective-permute-start.56 = (f32[4,2048]{1,0:T(4,128)S(1)}, f32[4,2048]{1,0:T(4,128)S(1)}, u32[]{:S(2)}, u32[]{:S(2)}) collective-permute-start(f32[4,2048]{1,0:T(4,128)S(1)} %add_add_fusion.1), channel_id=1, source_target_pairs={{0,4},{4,0},{8,12},{12,8},{1,5},{5,1},{9,13},{13,9},{2,6},{6,2},{1... | collective-permute-start | bytes 98312 | tf_op jit(solution)/shard_map/ppermute | solution.py:459
  485.3 12.2 %collective-permute-start.55 = (bf16[960,256]{1,0:T(8,128)(2,1)S(1)}, bf16[960,256]{1,0:T(8,128)(2,1)S(1)}, u32[]{:S(2)}, u32[]{:S(2)}) collective-permute-start(bf16[960,256]{1,0:T(8,128)(2,1)S(1)} %pad_maximum_fusion.10), channel_id=1, source_target_pairs={{0,2},{1,3},{2,0},{3,1},{4,6},{5,7},{6,4},{7,5},{8,10},{9,11},{10,... | collective-permute-start | bytes 1474568 | tf_op jit(solution)/shard_map/ppermute | solution.py:34
  486.9 11.9 %collective-permute-start.54 = (bf16[960,256]{1,0:T(8,128)(2,1)S(1)}, bf16[960,256]{1,0:T(8,128)(2,1)S(1)}, u32[]{:S(2)}, u32[]{:S(2)}) collective-permute-start(bf16[960,256]{1,0:T(8,128)(2,1)S(1)} %pad_maximum_fusion.9), channel_id=1, source_target_pairs={{0,16},{16,0},{1,17},{17,1},{2,18},{18,2},{3,19},{19,3},{4,20},{20... | collective-permute-start | bytes 1474568 | tf_op jit(solution)/shard_map/ppermute | solution.py:38
  (41 other events, 374.2 us)
Sparse Core Ops, SparseCore 0:
  32.7 79.3 all-gather.5
  117.8 130.1 all-gather.3
  325.7 154.8 all-reduce.3

commit v3 on v2

--- a/solution.py
+++ b/solution.py
@@ -105,9 +105,9 @@
     return whole
 
 
-def tensor_rows(whole):
+def tensor_rows(whole, other=0):
     rows = whole.shape[0] // lax.axis_size("tensor")
-    return lax.dynamic_slice_in_dim(whole, lax.axis_index("tensor") * rows, rows, 0)
+    return lax.dynamic_slice_in_dim(whole, (lax.axis_index("tensor") ^ other) * rows, rows, 0)
 
 
 def other_groups(slices):
@@ -540,7 +540,8 @@
 
     gate_units, up_units = gate_weight.T, up_weight.T
     hidden, grad_hidden_part = feed_forward_own(hidden_in, dot(out_grad, down_weight, 1, 1), gate_units, up_units)
-    grad_half, hidden = meet(scatter_half(grad_hidden_part.reshape(plane, rows, width)), hidden)
+    grad_half = scatter_half(grad_hidden_part.reshape(plane, rows, width))
+    grad_half, hidden = meet(grad_half, hidden)
     grad_terms, output_part = meet(scatter_across(grad_half), output_parts(hidden, down_weight, plane))
     grad_hidden_in = scatter_last(*grad_terms)
     ffn_gain_term = jnp.sum(grad_hidden_in * residual * resid_inv, axis=0)
@@ -548,7 +549,9 @@
     grad_branch_low = gather_plane(grad_residual.astype(bf16))
     if all_tokens:
         grad_near, grad_branch_low = meet(grad_near, grad_branch_low)
-        grad_high = [swap_high(grad_near[0])]
+        grad_far, grad_near[0] = meet(tensor_rows(out_grad, 2)[None], grad_near[0])
+        grad_far = lax.ppermute(grad_far, "dp", [(i, i ^ 1) for i in range(lax.axis_size("dp"))])
+        grad_high = [grad_far] + [swap_high(v) for v in grad_near[1:2]]
 
     def add_own(parts, own):
         own = own.reshape(rows, plane, columns).transpose(1, 0, 2)
@@ -567,13 +570,12 @@
     second_right = joined(jnp.where(is_first, grad_v, attn_out), second_back)
     second_left = jnp.where(is_first, normed, grad_branch_low)
     second_sum = dot(second_left, second_right, 0, 0).astype(bf16)
-    if len(grad_near) > 1:
-        second_back, grad_high, grad_near[1] = meet(second_back, grad_high, grad_near[1])
-        grad_high.append(swap_high(grad_near[1]))
+    if len(grad_near) > 2:
+        second_back, grad_high, grad_near[2] = meet(second_back, grad_high, grad_near[2])
+        grad_high.append(swap_high(grad_near[2]))
     first_back = swap_section(jnp.where(is_first, grad_q, grad_k))
     if len(grad_near) > 2:
-        first_back, grad_high, grad_near[2] = meet(first_back, grad_high, grad_near[2])
-        grad_high.append(swap_high(grad_near[2]))
+        first_back, grad_high = meet(first_back, grad_high)
     first_grad = joined(jnp.where(is_first, grad_k, grad_q), first_back)
     value_grad = jnp.where(is_first, second_right, jnp.zeros_like(second_right))
     first_sum = dot(normed, first_grad, 0, 0).astype(bf16)

time: 515 us -> 503 us (0.977)
  waiting for transfers between devices: 180 us -> 158 us
  local copies, waits for them, and re-layouts: 36.6 us -> 48 us
    ppermute x16, waiting for transfers between devices: 55.7 us -> 45 us  [swap_section(): return lax.ppermute(value, 'section', SWAP_SECTION)]
    ppermute x16 -> x15, waiting for transfers between devices: 78.8 us -> 69 us  [swap_high(): return lax.ppermute(value, 'tensor', SWAP_HIGH)]
    ppermute x16 -> x15, starting transfers between devices: 21.7 us -> 19.7 us  [swap_high(): return lax.ppermute(value, 'tensor', SWAP_HIGH)]
  transfers between devices with their start and end apart: 62 -> 62, of which waited for: 31 -> 28; matrix products, arithmetic and copies ran while one was open for 17% -> 19% of each run, Pallas kernels for 31% -> 32%
where the time goes in v3:
time: 503 us; the launch traced here: 495 us
  waiting for transfers between devices  158 us (31%)
  Pallas kernels  157 us (31%)
  starting transfers between devices  57.2 us (11%)
  local copies, waits for them, and re-layouts  48 us (10%)
  other arithmetic  41.6 us (8%)
  between operations  16.3 us (3%)
  matrix products  15.9 us (3%)
    pallas_call x1, Pallas kernels, feed_forward_grads(): pl.pallas_call(kernel, out_shape=[jax.ShapeDtypeStruct((units, width), f3...  85.8 us
    ppermute x15, waiting for transfers between devices, swap_high(): return lax.ppermute(value, 'tensor', SWAP_HIGH)  69 us
    ppermute x16, waiting for transfers between devices, swap_section(): return lax.ppermute(value, 'section', SWAP_SECTION)  45 us
    ppermute x16, starting transfers between devices, swap_section(): return lax.ppermute(value, 'section', SWAP_SECTION)  22.5 us
    ppermute x15, starting transfers between devices, swap_high(): return lax.ppermute(value, 'tensor', SWAP_HIGH)  19.7 us
    pallas_call x1, Pallas kernels, feed_forward_own(): pl.pallas_call(kernel, out_shape=[jax.ShapeDtypeStruct((tok_count, units)...  18.1 us
    dot_general x3, matrix products, dot(): lax.dot_general(left, right, (((left_dim,), (right_dim,)), ((), ())), pre...  15.9 us
    pallas_call x1, Pallas kernels, input_gradient(): pl.pallas_call(kernel, out_shape=[jax.ShapeDtypeStruct((parts, tok_count,...  13.8 us
  transfers between devices with their start and end apart: 62, of which 28 were waited for; matrix products, arithmetic and copies ran while one was open for 19% of the time, Pallas kernels for 32%

profile of v3, /device:TPU:0, one launch (start us, length us, event | category | flops | bytes accessed | tf_op | source)
XLA Modules:
  0.0 494.7 jit_solution(13348012695251966815)
XLA Ops:
  11.9 3.0 dynamic-slice_bitcast_fusion.4
  14.9 9.1 %normed_projections.1 = (bf16[960,2048]{1,0:T(8,128)(2,1)}, bf16[2,960,256]{2,1,0:T(8,128)(2,1)}, bf16[2,960,256]{2,1,0:T(8,128)(2,1)}) custom-call(bf16[960,2048]{1,0:T(8,128)(2,1)} %inputs_ref.1, f32[1,2048]{1,0:T(1,128)} %convert_element_type.229.gain_ref, bf16[2,2048,512]{2,1,0:T(8,128)(2,1)} %bitcast.150), custom_call_target="tpu_custom_call" | custom-call | tf_op jit(solution)/shard_map/normed_projections/pallas_call | solution.py:275
  25.8 5.7 %collective-permute-start.1 = (bf16[960,256]{1,0:T(8,128)(2,1)}, bf16[960,256]{1,0:T(8,128)(2,1)}, u32[]{:S(2)}, u32[]{:S(2)}) collective-permute-start(bf16[960,256]{1,0:T(8,128)(2,1)} %slice_bitcast_fusion.1), channel_id=1, source_target_pairs={{0,16},{1,17},{2,18},{3,19},{4,20},{5,21},{6,22},{7,23},{8,24},{9,... | collective-permute-start | bytes 1474568 | tf_op jit(solution)/shard_map/ppermute | solution.py:510
  34.7 8.0 %collective-permute-done.1 = bf16[960,256]{1,0:T(8,128)(2,1)} collective-permute-done((bf16[960,256]{1,0:T(8,128)(2,1)}, bf16[960,256]{1,0:T(8,128)(2,1)}, u32[]{:S(2)}, u32[]{:S(2)}) %collective-permute-start.1) | collective-permute-done | bytes 491552 | tf_op jit(solution)/shard_map/ppermute | solution.py:510
  44.6 7.5 %collective-permute-done = bf16[960,256]{1,0:T(8,128)(2,1)} collective-permute-done((bf16[960,256]{1,0:T(8,128)(2,1)}, bf16[960,256]{1,0:T(8,128)(2,1)}, u32[]{:S(2)}, u32[]{:S(2)}) %collective-permute-start) | collective-permute-done | bytes 491552 | tf_op jit(solution)/shard_map/ppermute | solution.py:38
  52.1 2.2 bitcast_select_fusion.1
  55.4 9.7 %attend_forward.1 = (bf16[960,256]{1,0:T(8,128)(2,1)}, bf16[960,2048]{1,0:T(8,128)(2,1)}, f32[2,960,1]{2,1,0:T(8,128)}) custom-call(bf16[960,256]{1,0:T(8,128)(2,1)} %get-tuple-element.191.q_ref, bf16[960,256]{1,0:T(8,128)(2,1)} %get-tuple-element.190.k_ref, bf16[960,256]{1,0:T(8,128)(2,1)} %bitcast_select_fusion.v_ref, ...), custom_call_target="tpu_custom_call" | custom-call | tf_op jit(solution)/shard_map/attend_forward/pallas_call | solution.py:316
  66.9 4.0 collective-permute-done.3
  70.9 2.9 fusion.3
  74.0 2.6 collective-permute-start.6
  76.6 2.4 collective-permute-start.4
  79.0 3.8 collective-permute-done.6
  82.9 2.4 collective-permute-start.7
  87.3 9.1 %collective-permute-done.7 = bf16[120,2048]{1,0:T(8,128)(2,1)S(1)} collective-permute-done((bf16[120,2048]{1,0:T(8,128)(2,1)S(1)}, bf16[120,2048]{1,0:T(8,128)(2,1)S(1)}, u32[]{:S(2)}, u32[]{:S(2)}) %collective-permute-start.7) | collective-permute-done | bytes 491552 | tf_op jit(solution)/shard_map/ppermute | solution.py:34
  99.4 13.5 %all-gather.6.cloned.1.call-done = bf16[960,2048]{1,0:T(8,128)(2,1)} async-done(((bf16[240,2048]{1,0:T(8,128)(2,1)}), bf16[960,2048]{1,0:T(8,128)(2,1)}) %all-gather.6.cloned.1.call-update) | async-done | bytes 3932176 | tf_op jit(solution)/shard_map/all_gather | solution.py:500
  114.9 2.4 broadcast.48.clone
  122.0 7.9 %fusion.27.back_ref = f32[960,688]{1,0:T(8,128)} fusion(bf16[960,2048]{1,0:T(8,128)(2,1)} %param.10, bf16[688,2048]{1,0:T(8,128)(2,1)} %refs_15_.1), kind=kOutput, calls=%fused_computation.141 | convolution fusion | flops 2705326080 | bytes 9392128 | tf_op jit(solution)/shard_map/dot_general | solution.py:137
  129.9 5.8 %collective-permute-done.9 = bf16[120,2048]{1,0:T(8,128)(2,1)S(1)} collective-permute-done((bf16[120,2048]{1,0:T(8,128)(2,1)}, bf16[120,2048]{1,0:T(8,128)(2,1)S(1)}, u32[]{:S(2)}, u32[]{:S(2)}) %collective-permute-start.9) | collective-permute-done | bytes 491552 | tf_op jit(solution)/shard_map/ppermute | solution.py:38
  135.7 3.6 constant_dynamic-slice_fusion.1
  144.0 3.7 collective-permute-done.13
  154.3 18.1 %feed_forward_own.1 = (bf16[960,688]{1,0:T(8,128)(2,1)}, bf16[960,2048]{1,0:T(8,128)(2,1)}) custom-call(bf16[960,2048]{1,0:T(8,128)(2,1)} %constant_dynamic-update-slice_fusion.18.in_ref, f32[960,688]{1,0:T(8,128)} %fusion.27.back_ref, bf16[688,2048]{1,0:T(8,128)(2,1)} %bitcast.156, bf16[688,2048]{1,0:T(8,128)(2,1)} %bitcast.158), custom_call_target="tpu_custom_call" | custom-call | tf_op jit(solution)/shard_map/feed_forward_own/pallas_call | solution.py:378
  174.7 3.6 collective-permute-done.17
  181.6 8.8 %output_parts.1 = bf16[8,960,256]{2,1,0:T(8,128)(2,1)} custom-call(bf16[960,688]{1,0:T(8,128)(2,1)} %get-tuple-element.93.hidden_ref, bf16[688,2048]{1,0:T(8,128)(2,1)} %refs_15_.1), custom_call_target="tpu_custom_call" | custom-call | tf_op jit(solution)/shard_map/output_parts/pallas_call | solution.py:430
  190.4 2.8 collective-permute-done.19
  197.2 20.9 %collective-permute-done.22 = bf16[120,2048]{1,0:T(8,128)(2,1)S(1)} collective-permute-done((bf16[120,2048]{1,0:T(8,128)(2,1)S(1)}, bf16[120,2048]{1,0:T(8,128)(2,1)S(1)}, u32[]{:S(2)}, u32[]{:S(2)}) %collective-permute-start.22) | collective-permute-done | bytes 491552 | tf_op jit(solution)/shard_map/ppermute | solution.py:34
  220.0 2.4 broadcast.48
  222.4 2.3 constant_dynamic-update-slice_fusion.7
  228.8 7.2 %collective-permute-done.24 = bf16[120,2048]{1,0:T(8,128)(2,1)S(1)} collective-permute-done((bf16[120,2048]{1,0:T(8,128)(2,1)S(1)}, bf16[120,2048]{1,0:T(8,128)(2,1)S(1)}, u32[]{:S(2)}, u32[]{:S(2)}) %collective-permute-start.24) | collective-permute-done | bytes 491552 | tf_op jit(solution)/shard_map/ppermute | solution.py:38
  235.9 2.9 dynamic-slice_bitcast_fusion.1
  243.5 3.8 collective-permute-done.28
  255.4 12.0 %attend_backward.1 = (bf16[960,256]{1,0:T(8,128)(2,1)}, bf16[960,256]{1,0:T(8,128)(2,1)}, bf16[960,256]{1,0:T(8,128)(2,1)}) custom-call(bf16[960,256]{1,0:T(8,128)(2,1)} %get-tuple-element.191.q_ref, bf16[960,256]{1,0:T(8,128)(2,1)} %get-tuple-element.190.k_ref, bf16[960,256]{1,0:T(8,128)(2,1)} %bitcast_select_fusion.v_ref, ...), custom_call_target="tpu_custom_call" | custom-call | tf_op jit(solution)/shard_map/attend_backward/pallas_call | solution.py:350
  267.4 2.8 collective-permute-start.33
  272.8 2.5 fusion.1
  275.3 7.0 %collective-permute-done.33 = bf16[960,256]{1,0:T(8,128)(2,1)S(1)} collective-permute-done((bf16[960,256]{1,0:T(8,128)(2,1)S(1)}, bf16[960,256]{1,0:T(8,128)(2,1)S(1)}, u32[]{:S(2)}, u32[]{:S(2)}) %collective-permute-start.33) | collective-permute-done | bytes 491552 | tf_op jit(solution)/shard_map/ppermute | solution.py:38
  283.7 4.2 fusion.7
  288.1 4.4 collective-permute-done.32
  292.5 14.3 %collective-permute-done.36.refs_6_ = bf16[1,240,2048]{2,1,0:T(8,128)(2,1)} collective-permute-done((bf16[1,240,2048]{2,1,0:T(8,128)(2,1)}, bf16[1,240,2048]{2,1,0:T(8,128)(2,1)}, u32[]{:S(2)}, u32[]{:S(2)}) %collective-permute-start.36) | collective-permute-done | bytes 983072 | tf_op jit(solution)/shard_map/ppermute | solution.py:34
  308.5 3.8 convolution_convert_fusion
  316.5 2.3 broadcast_select_fusion.value_ref
  319.9 85.8 %feed_forward_grads.1 = (f32[688,2048]{1,0:T(8,128)}, f32[688,2048]{1,0:T(8,128)}, f32[688,2048]{1,0:T(8,128)}) custom-call(s32[16]{0:T(128)} %stack.88.order_ref, bf16[16,240,2048]{2,1,0:T(8,128)(2,1)} %bitcast.155, bf16[4,240,2048]{2,1,0:T(8,128)(2,1)} %bitcast.160, bf16[1,240,2048]{2,1,0:T(8,128)(2,1)} %get-tuple-element.123.refs_1_, ...), custom_call_target="tpu_custom_call" | custom-call | tf_op jit(solution)/shard_map/feed_forward_grads/pallas_call | solution.py:230
  405.8 13.8 %input_gradient.1 = (bf16[8,960,256]{2,1,0:T(8,128)(2,1)}, f32[1,2048]{1,0:T(1,128)}) custom-call(bf16[960,2048]{1,0:T(8,128)(2,1)} %inputs_ref.1, f32[1,2048]{1,0:T(1,128)} %convert_element_type.229.gain_ref, bf16[960,512]{1,0:T(8,128)(2,1)} %pad_maximum_fusion.first_ref, bf16[960,512]{1,0:T(8,128)(2,1)} %broadcast_select_fusion.value_ref, ...), custom_call_target="tpu_custom_call" | custom-call | tf_op jit(solution)/shard_map/input_gradient/pallas_call | solution.py:412
  421.6 2.9 dynamic-slice_bitcast_fusion
  429.5 10.0 %collective-permute-done.46 = bf16[960,256]{1,0:T(8,128)(2,1)S(1)} collective-permute-done((bf16[960,256]{1,0:T(8,128)(2,1)}, bf16[960,256]{1,0:T(8,128)(2,1)S(1)}, u32[]{:S(2)}, u32[]{:S(2)}) %collective-permute-start.46) | collective-permute-done | bytes 491552 | tf_op jit(solution)/shard_map/ppermute | solution.py:34
  444.6 2.0 fusion
  455.2 13.3 %all-reduce.4.cloned.1.call-done = (bf16[2048,512]{1,0:T(8,128)(2,1)}, bf16[2048,512]{1,0:T(8,128)(2,1)}) async-done(((bf16[2048,512]{1,0:T(8,128)(2,1)}, bf16[2048,512]{1,0:T(8,128)(2,1)}), (bf16[2048,512]{1,0:T(8,128)(2,1)}, bf16[2048,512]{1,0:T(8,128)(2,1)})) %all-reduce.4.cloned.1.call-update) | async-done | bytes 4194320 | tf_op jit(solution)/shard_map/psum | solution.py:616
  470.1 2.9 collective-permute-start.56
  476.4 3.9 maximum_convert_fusion
  482.8 2.7 collective-permute-done.55
  (257 shorter events, 105.9 us)
Async XLA Ops:
  7.2 105.7 %all-gather.6.cloned.1.call-start = ((), (), s32[]{:S(2)}) async-start(), calls=%async_computation.1 | async-start | bytes 4915200 | tf_op jit(solution)/shard_map/all_gather | solution.py:500
  10.0 44.3 %collective-permute-start.2 = (bf16[2048,256]{1,0:T(8,128)(2,1)}, bf16[2048,256]{1,0:T(8,128)(2,1)S(1)}, u32[]{:S(2)}, u32[]{:S(2)}) collective-permute-start(bf16[2048,256]{1,0:T(8,128)(2,1)} %slice.150), channel_id=1, source_target_pairs={{16,0},{17,1},{18,2},{19,3},{20,4},{21,5},{22,6},{23,7},{24,8},{25... | collective-permute-start | bytes 3145736 | tf_op jit(solution)/shard_map/ppermute | solution.py:511
  25.8 16.8 %collective-permute-start.1 = (bf16[960,256]{1,0:T(8,128)(2,1)}, bf16[960,256]{1,0:T(8,128)(2,1)}, u32[]{:S(2)}, u32[]{:S(2)}) collective-permute-start(bf16[960,256]{1,0:T(8,128)(2,1)} %slice_bitcast_fusion.1), channel_id=1, source_target_pairs={{0,16},{1,17},{2,18},{3,19},{4,20},{5,21},{6,22},{7,23},{8,24},{9,... | collective-permute-start | bytes 1474568 | tf_op jit(solution)/shard_map/ppermute | solution.py:510
  33.4 18.7 %collective-permute-start = (bf16[960,256]{1,0:T(8,128)(2,1)}, bf16[960,256]{1,0:T(8,128)(2,1)}, u32[]{:S(2)}, u32[]{:S(2)}) collective-permute-start(bf16[960,256]{1,0:T(8,128)(2,1)} %dynamic-slice_bitcast_fusion.20), channel_id=1, source_target_pairs={{0,16},{16,0},{1,17},{17,1},{2,18},{18,2},{3,19},{19,3},{4,20},{20... | collective-permute-start | bytes 1474568 | tf_op jit(solution)/shard_map/ppermute | solution.py:38
  33.4 278.9 %all-gather.4.cloned.1.call-start = ((), (), s32[]{:S(2)}) async-start(), calls=%async_computation | async-start | bytes 16220160 | tf_op jit(solution)/shard_map/all_gather | solution.py:527
  74.0 8.8 %collective-permute-start.6 = (bf16[120,1024]{1,0:T(8,128)(2,1)S(1)}, bf16[120,1024]{1,0:T(8,128)(2,1)S(1)}, u32[]{:S(2)}, u32[]{:S(2)}) collective-permute-start(bf16[120,1024]{1,0:T(8,128)(2,1)S(1)} %get-tuple-element.200), channel_id=1, source_target_pairs={{0,16},{16,0},{1,17},{17,1},{2,18},{18,2},{3,19},{19,3},{4,20},{20... | collective-permute-start | bytes 737288 | tf_op jit(solution)/shard_map/ppermute | solution.py:38
  76.6 8.7 %collective-permute-start.4 = (bf16[120,1024]{1,0:T(8,128)(2,1)S(1)}, bf16[120,1024]{1,0:T(8,128)(2,1)S(1)}, u32[]{:S(2)}, u32[]{:S(2)}) collective-permute-start(bf16[120,1024]{1,0:T(8,128)(2,1)S(1)} %get-tuple-element.199), channel_id=1, source_target_pairs={{0,2},{1,3},{2,0},{3,1},{4,6},{5,7},{6,4},{7,5},{8,10},{9,11},{10,... | collective-permute-start | bytes 737288 | tf_op jit(solution)/shard_map/ppermute | solution.py:34
  82.9 13.5 %collective-permute-start.7 = (bf16[120,2048]{1,0:T(8,128)(2,1)S(1)}, bf16[120,2048]{1,0:T(8,128)(2,1)S(1)}, u32[]{:S(2)}, u32[]{:S(2)}) collective-permute-start(bf16[120,2048]{1,0:T(8,128)(2,1)S(1)} %pad_maximum_fusion.4), channel_id=1, source_target_pairs={{0,2},{1,3},{2,0},{3,1},{4,6},{5,7},{6,4},{7,5},{8,10},{9,11},{10,... | collective-permute-start | bytes 1474568 | tf_op jit(solution)/shard_map/ppermute | solution.py:34
  85.4 12.7 %collective-permute-start.5 = (bf16[120,2048]{1,0:T(8,128)(2,1)S(1)}, bf16[120,2048]{1,0:T(8,128)(2,1)}, u32[]{:S(2)}, u32[]{:S(2)}) collective-permute-start(bf16[120,2048]{1,0:T(8,128)(2,1)S(1)} %pad_maximum_fusion.3), channel_id=1, source_target_pairs={{0,16},{16,0},{1,17},{17,1},{2,18},{18,2},{3,19},{19,3},{4,20},{20... | collective-permute-start | bytes 1474568 | tf_op jit(solution)/shard_map/ppermute | solution.py:38
  118.4 350.1 %all-reduce.4.cloned.1.call-start = ((), (), s32[]{:S(2)}) async-start(), calls=%async_computation.2 | async-start | bytes 8388608 | tf_op jit(solution)/shard_map/psum | solution.py:616
  118.9 16.8 %collective-permute-start.9 = (bf16[120,2048]{1,0:T(8,128)(2,1)}, bf16[120,2048]{1,0:T(8,128)(2,1)S(1)}, u32[]{:S(2)}, u32[]{:S(2)}) collective-permute-start(bf16[120,2048]{1,0:T(8,128)(2,1)} %get-tuple-element.121), channel_id=1, source_target_pairs={{0,16},{16,0},{1,17},{17,1},{2,18},{18,2},{3,19},{19,3},{4,20},{20... | collective-permute-start | bytes 1474568 | tf_op jit(solution)/shard_map/ppermute | solution.py:38
  120.5 21.8 %collective-permute-start.8 = (bf16[120,2048]{1,0:T(8,128)(2,1)}, bf16[120,2048]{1,0:T(8,128)(2,1)S(1)}, u32[]{:S(2)}, u32[]{:S(2)}) collective-permute-start(bf16[120,2048]{1,0:T(8,128)(2,1)} %get-tuple-element.121), channel_id=1, source_target_pairs={{0,1},{1,0},{2,3},{3,2},{4,5},{5,4},{6,7},{7,6},{8,9},{9,8},{10,11... | collective-permute-start | bytes 1474568 | tf_op jit(solution)/shard_map/ppermute | solution.py:30
  120.5 20.3 %collective-permute-start.11 = (bf16[120,2048]{1,0:T(8,128)(2,1)}, bf16[120,2048]{1,0:T(8,128)(2,1)S(1)}, u32[]{:S(2)}, u32[]{:S(2)}) collective-permute-start(bf16[120,2048]{1,0:T(8,128)(2,1)} %get-tuple-element.121), channel_id=1, source_target_pairs={{0,2},{1,3},{2,0},{3,1},{4,6},{5,7},{6,4},{7,5},{8,10},{9,11},{10,... | collective-permute-start | bytes 1474568 | tf_op jit(solution)/shard_map/ppermute | solution.py:34
  135.7 13.3 %collective-permute-start.10 = (bf16[120,2048]{1,0:T(8,128)(2,1)S(1)}, bf16[120,2048]{1,0:T(8,128)(2,1)S(1)}, u32[]{:S(2)}, u32[]{:S(2)}) collective-permute-start(bf16[120,2048]{1,0:T(8,128)(2,1)S(1)} %collective-permute-done.9), channel_id=1, source_target_pairs={{0,1},{1,0},{2,3},{3,2},{4,5},{5,4},{6,7},{7,6},{8,9},{9,8},{10,11... | collective-permute-start | bytes 1474568 | tf_op jit(solution)/shard_map/ppermute | solution.py:30
  139.3 8.4 %collective-permute-start.13 = (bf16[120,1024]{1,0:T(8,128)(2,1)S(1)}, bf16[120,1024]{1,0:T(8,128)(2,1)S(1)}, u32[]{:S(2)}, u32[]{:S(2)}) collective-permute-start(bf16[120,1024]{1,0:T(8,128)(2,1)S(1)} %slice.158), channel_id=1, source_target_pairs={{0,2},{1,3},{2,0},{3,1},{4,6},{5,7},{6,4},{7,5},{8,10},{9,11},{10,... | collective-permute-start | bytes 737288 | tf_op jit(solution)/shard_map/ppermute | solution.py:34
  142.4 8.2 %collective-permute-start.12 = (bf16[120,2048]{1,0:T(8,128)(2,1)S(1)}, bf16[120,2048]{1,0:T(8,128)(2,1)S(1)}, u32[]{:S(2)}, u32[]{:S(2)}) collective-permute-start(bf16[120,2048]{1,0:T(8,128)(2,1)S(1)} %collective-permute-done.11), channel_id=1, source_target_pairs={{0,1},{1,0},{2,3},{3,2},{4,5},{5,4},{6,7},{7,6},{8,9},{9,8},{10,11... | collective-permute-start | bytes 1474568 | tf_op jit(solution)/shard_map/ppermute | solution.py:30
  179.4 13.7 %collective-permute-start.19 = (bf16[120,1024]{1,0:T(8,128)(2,1)S(1)}, bf16[120,1024]{1,0:T(8,128)(2,1)S(1)}, u32[]{:S(2)}, u32[]{:S(2)}) collective-permute-start(bf16[120,1024]{1,0:T(8,128)(2,1)S(1)} %get-tuple-element.197), channel_id=1, source_target_pairs={{0,2},{1,3},{2,0},{3,1},{4,6},{5,7},{6,4},{7,5},{8,10},{9,11},{10,... | collective-permute-start | bytes 737288 | tf_op jit(solution)/shard_map/ppermute | solution.py:34
  180.1 13.7 %collective-permute-start.18 = (bf16[120,1024]{1,0:T(8,128)(2,1)S(1)}, bf16[120,1024]{1,0:T(8,128)(2,1)S(1)}, u32[]{:S(2)}, u32[]{:S(2)}) collective-permute-start(bf16[120,1024]{1,0:T(8,128)(2,1)S(1)} %get-tuple-element.198), channel_id=1, source_target_pairs={{0,16},{16,0},{1,17},{17,1},{2,18},{18,2},{3,19},{19,3},{4,20},{20... | collective-permute-start | bytes 737288 | tf_op jit(solution)/shard_map/ppermute | solution.py:38
  194.0 24.1 %collective-permute-start.22 = (bf16[120,2048]{1,0:T(8,128)(2,1)S(1)}, bf16[120,2048]{1,0:T(8,128)(2,1)S(1)}, u32[]{:S(2)}, u32[]{:S(2)}) collective-permute-start(bf16[120,2048]{1,0:T(8,128)(2,1)S(1)} %pad_maximum_fusion.6), channel_id=1, source_target_pairs={{0,2},{1,3},{2,0},{3,1},{4,6},{5,7},{6,4},{7,5},{8,10},{9,11},{10,... | collective-permute-start | bytes 1474568 | tf_op jit(solution)/shard_map/ppermute | solution.py:34
  195.6 24.0 %collective-permute-start.21 = (bf16[120,2048]{1,0:T(8,128)(2,1)S(1)}, bf16[120,2048]{1,0:T(8,128)(2,1)S(1)}, u32[]{:S(2)}, u32[]{:S(2)}) collective-permute-start(bf16[120,2048]{1,0:T(8,128)(2,1)S(1)} %pad_maximum_fusion.5), channel_id=1, source_target_pairs={{0,16},{16,0},{1,17},{17,1},{2,18},{18,2},{3,19},{19,3},{4,20},{20... | collective-permute-start | bytes 1474568 | tf_op jit(solution)/shard_map/ppermute | solution.py:38
  224.7 11.3 %collective-permute-start.24 = (bf16[120,2048]{1,0:T(8,128)(2,1)S(1)}, bf16[120,2048]{1,0:T(8,128)(2,1)S(1)}, u32[]{:S(2)}, u32[]{:S(2)}) collective-permute-start(bf16[120,2048]{1,0:T(8,128)(2,1)S(1)} %get-tuple-element.158), channel_id=1, source_target_pairs={{0,16},{16,0},{1,17},{17,1},{2,18},{18,2},{3,19},{19,3},{4,20},{20... | collective-permute-start | bytes 1474568 | tf_op jit(solution)/shard_map/ppermute | solution.py:38
  226.2 14.6 %collective-permute-start.26 = (bf16[120,2048]{1,0:T(8,128)(2,1)S(1)}, bf16[120,2048]{1,0:T(8,128)(2,1)S(1)}, u32[]{:S(2)}, u32[]{:S(2)}) collective-permute-start(bf16[120,2048]{1,0:T(8,128)(2,1)S(1)} %get-tuple-element.158), channel_id=1, source_target_pairs={{0,2},{1,3},{2,0},{3,1},{4,6},{5,7},{6,4},{7,5},{8,10},{9,11},{10,... | collective-permute-start | bytes 1474568 | tf_op jit(solution)/shard_map/ppermute | solution.py:34
  226.8 15.1 %collective-permute-start.23 = (bf16[120,2048]{1,0:T(8,128)(2,1)S(1)}, bf16[120,2048]{1,0:T(8,128)(2,1)S(1)}, u32[]{:S(2)}, u32[]{:S(2)}) collective-permute-start(bf16[120,2048]{1,0:T(8,128)(2,1)S(1)} %get-tuple-element.158), channel_id=1, source_target_pairs={{0,1},{1,0},{2,3},{3,2},{4,5},{5,4},{6,7},{7,6},{8,9},{9,8},{10,11... | collective-permute-start | bytes 1474568 | tf_op jit(solution)/shard_map/ppermute | solution.py:30
  235.9 12.6 %collective-permute-start.25 = (bf16[120,2048]{1,0:T(8,128)(2,1)S(1)}, bf16[120,2048]{1,0:T(8,128)(2,1)S(1)}, u32[]{:S(2)}, u32[]{:S(2)}) collective-permute-start(bf16[120,2048]{1,0:T(8,128)(2,1)S(1)} %collective-permute-done.24), channel_id=1, source_target_pairs={{0,1},{1,0},{2,3},{3,2},{4,5},{5,4},{6,7},{7,6},{8,9},{9,8},{10,11... | collective-permute-start | bytes 1474568 | tf_op jit(solution)/shard_map/ppermute | solution.py:30
  238.9 32.5 %collective-permute-start.20 = (bf16[4,960,256]{2,1,0:T(8,128)(2,1)}, bf16[4,960,256]{2,1,0:T(8,128)(2,1)S(1)}, u32[]{:S(2)}, u32[]{:S(2)}) collective-permute-start(bf16[4,960,256]{2,1,0:T(8,128)(2,1)} %dynamic-slice_bitcast_fusion.1), channel_id=1, source_target_pairs={{0,1},{1,0},{2,3},{3,2},{4,5},{5,4},{6,7},{7,6},{8,9},{9,8},{10,11... | collective-permute-start | bytes 5898248 | tf_op jit(solution)/shard_map/ppermute | solution.py:30
  241.9 8.3 %collective-permute-start.27 = (bf16[120,2048]{1,0:T(8,128)(2,1)S(1)}, bf16[120,2048]{1,0:T(8,128)(2,1)S(1)}, u32[]{:S(2)}, u32[]{:S(2)}) collective-permute-start(bf16[120,2048]{1,0:T(8,128)(2,1)S(1)} %collective-permute-done.26), channel_id=1, source_target_pairs={{0,1},{1,0},{2,3},{3,2},{4,5},{5,4},{6,7},{7,6},{8,9},{9,8},{10,11... | collective-permute-start | bytes 1474568 | tf_op jit(solution)/shard_map/ppermute | solution.py:30
  253.9 28.4 %collective-permute-start.34 = (bf16[1,240,2048]{2,1,0:T(8,128)(2,1)}, bf16[1,240,2048]{2,1,0:T(8,128)(2,1)}, u32[]{:S(2)}, u32[]{:S(2)}) collective-permute-start(bf16[1,240,2048]{2,1,0:T(8,128)(2,1)} %get-tuple-element.111), channel_id=1, source_target_pairs={{0,4},{4,0},{8,12},{12,8},{1,5},{5,1},{9,13},{13,9},{2,6},{6,2},{1... | collective-permute-start | bytes 2949128 | tf_op jit(solution)/shard_map/ppermute | solution.py:553
  253.9 28.4 %collective-permute-start.35 = (bf16[1,240,2048]{2,1,0:T(8,128)(2,1)}, bf16[1,240,2048]{2,1,0:T(8,128)(2,1)}, u32[]{:S(2)}, u32[]{:S(2)}) collective-permute-start(bf16[1,240,2048]{2,1,0:T(8,128)(2,1)} %get-tuple-element.112.refs_2_), channel_id=1, source_target_pairs={{0,2},{1,3},{2,0},{3,1},{4,6},{5,7},{6,4},{7,5},{8,10},{9,11},{10,... | collective-permute-start | bytes 2949128 | tf_op jit(solution)/shard_map/ppermute | solution.py:34
  255.2 58.1 %collective-permute-start.40 = (bf16[1,240,2048]{2,1,0:T(8,128)(2,1)}, bf16[1,240,2048]{2,1,0:T(8,128)(2,1)}, u32[]{:S(2)}, u32[]{:S(2)}) collective-permute-start(bf16[1,240,2048]{2,1,0:T(8,128)(2,1)} %get-tuple-element.112.refs_2_), channel_id=1, source_target_pairs={{0,1},{1,0},{2,3},{3,2},{4,5},{5,4},{6,7},{7,6},{8,9},{9,8},{10,11... | collective-permute-start | bytes 2949128 | tf_op jit(solution)/shard_map/ppermute | solution.py:30
  267.4 14.8 %collective-permute-start.33 = (bf16[960,256]{1,0:T(8,128)(2,1)S(1)}, bf16[960,256]{1,0:T(8,128)(2,1)S(1)}, u32[]{:S(2)}, u32[]{:S(2)}) collective-permute-start(bf16[960,256]{1,0:T(8,128)(2,1)S(1)} %broadcast_select_fusion.6), channel_id=1, source_target_pairs={{0,16},{16,0},{1,17},{17,1},{2,18},{18,2},{3,19},{19,3},{4,20},{20... | collective-permute-start | bytes 1474568 | tf_op jit(solution)/shard_map/ppermute | solution.py:38
  272.6 19.8 %collective-permute-start.32 = (bf16[960,256]{1,0:T(8,128)(2,1)S(1)}, bf16[960,256]{1,0:T(8,128)(2,1)S(1)}, u32[]{:S(2)}, u32[]{:S(2)}) collective-permute-start(bf16[960,256]{1,0:T(8,128)(2,1)S(1)} %broadcast_select_fusion.7), channel_id=1, source_target_pairs={{0,16},{16,0},{1,17},{17,1},{2,18},{18,2},{3,19},{19,3},{4,20},{20... | collective-permute-start | bytes 1474568 | tf_op jit(solution)/shard_map/ppermute | solution.py:38
  282.3 25.2 %collective-permute-start.39 = (bf16[1,240,2048]{2,1,0:T(8,128)(2,1)S(1)}, bf16[1,240,2048]{2,1,0:T(8,128)(2,1)S(1)}, u32[]{:S(2)}, u32[]{:S(2)}) collective-permute-start(bf16[1,240,2048]{2,1,0:T(8,128)(2,1)S(1)} %copy-done.2), channel_id=1, source_target_pairs={{0,1},{1,0},{2,3},{3,2},{4,5},{5,4},{6,7},{7,6},{8,9},{9,8},{10,11... | collective-permute-start | bytes 2949128 | tf_op jit(solution)/shard_map/ppermute | solution.py:30
  282.3 24.5 %collective-permute-start.36 = (bf16[1,240,2048]{2,1,0:T(8,128)(2,1)}, bf16[1,240,2048]{2,1,0:T(8,128)(2,1)}, u32[]{:S(2)}, u32[]{:S(2)}) collective-permute-start(bf16[1,240,2048]{2,1,0:T(8,128)(2,1)} %get-tuple-element.116.refs_3_), channel_id=1, source_target_pairs={{0,2},{1,3},{2,0},{3,1},{4,6},{5,7},{6,4},{7,5},{8,10},{9,11},{10,... | collective-permute-start | bytes 2949128 | tf_op jit(solution)/shard_map/ppermute | solution.py:34
  287.9 26.6 %collective-permute-start.41 = (bf16[1,240,2048]{2,1,0:T(8,128)(2,1)}, bf16[1,240,2048]{2,1,0:T(8,128)(2,1)}, u32[]{:S(2)}, u32[]{:S(2)}) collective-permute-start(bf16[1,240,2048]{2,1,0:T(8,128)(2,1)} %get-tuple-element.116.refs_3_), channel_id=1, source_target_pairs={{0,1},{1,0},{2,3},{3,2},{4,5},{5,4},{6,7},{7,6},{8,9},{9,8},{10,11... | collective-permute-start | bytes 2949128 | tf_op jit(solution)/shard_map/ppermute | solution.py:30
  306.9 13.0 %collective-permute-start.42 = (bf16[1,240,2048]{2,1,0:T(8,128)(2,1)}, bf16[1,240,2048]{2,1,0:T(8,128)(2,1)}, u32[]{:S(2)}, u32[]{:S(2)}) collective-permute-start(bf16[1,240,2048]{2,1,0:T(8,128)(2,1)} %collective-permute-done.34.refs_4_), channel_id=1, source_target_pairs={{0,1},{1,0},{2,3},{3,2},{4,5},{5,4},{6,7},{7,6},{8,9},{9,8},{10,11... | collective-permute-start | bytes 2949128 | tf_op jit(solution)/shard_map/ppermute | solution.py:30
  307.0 12.9 %collective-permute-start.43 = (bf16[1,240,2048]{2,1,0:T(8,128)(2,1)}, bf16[1,240,2048]{2,1,0:T(8,128)(2,1)}, u32[]{:S(2)}, u32[]{:S(2)}) collective-permute-start(bf16[1,240,2048]{2,1,0:T(8,128)(2,1)} %collective-permute-done.35.refs_5_), channel_id=1, source_target_pairs={{0,1},{1,0},{2,3},{3,2},{4,5},{5,4},{6,7},{7,6},{8,9},{9,8},{10,11... | collective-permute-start | bytes 2949128 | tf_op jit(solution)/shard_map/ppermute | solution.py:30
  308.4 11.5 %collective-permute-start.44 = (bf16[1,240,2048]{2,1,0:T(8,128)(2,1)}, bf16[1,240,2048]{2,1,0:T(8,128)(2,1)}, u32[]{:S(2)}, u32[]{:S(2)}) collective-permute-start(bf16[1,240,2048]{2,1,0:T(8,128)(2,1)} %collective-permute-done.36.refs_6_), channel_id=1, source_target_pairs={{0,1},{1,0},{2,3},{3,2},{4,5},{5,4},{6,7},{7,6},{8,9},{9,8},{10,11... | collective-permute-start | bytes 2949128 | tf_op jit(solution)/shard_map/ppermute | solution.py:30
  313.3 92.4 %collective-permute-start.38 = (bf16[960,128]{1,0:T(8,128)(2,1)S(1)}, bf16[960,128]{1,0:T(8,128)(2,1)S(1)}, u32[]{:S(2)}, u32[]{:S(2)}) collective-permute-start(bf16[960,128]{1,0:T(8,128)(2,1)S(1)} %get-tuple-element.195), channel_id=1, source_target_pairs={{0,2},{1,3},{2,0},{3,1},{4,6},{5,7},{6,4},{7,5},{8,10},{9,11},{10,... | collective-permute-start | bytes 737288 | tf_op jit(solution)/shard_map/ppermute | solution.py:34
  314.5 91.2 %collective-permute-start.37 = (bf16[960,128]{1,0:T(8,128)(2,1)S(1)}, bf16[960,128]{1,0:T(8,128)(2,1)S(1)}, u32[]{:S(2)}, u32[]{:S(2)}) collective-permute-start(bf16[960,128]{1,0:T(8,128)(2,1)S(1)} %get-tuple-element.196), channel_id=1, source_target_pairs={{0,16},{16,0},{1,17},{17,1},{2,18},{18,2},{3,19},{19,3},{4,20},{20... | collective-permute-start | bytes 737288 | tf_op jit(solution)/shard_map/ppermute | solution.py:38
  424.6 20.0 %collective-permute-start.47 = (bf16[4,960,256]{2,1,0:T(8,128)(2,1)}, bf16[4,960,256]{2,1,0:T(8,128)(2,1)S(1)}, u32[]{:S(2)}, u32[]{:S(2)}) collective-permute-start(bf16[4,960,256]{2,1,0:T(8,128)(2,1)} %dynamic-slice_bitcast_fusion), channel_id=1, source_target_pairs={{0,1},{1,0},{2,3},{3,2},{4,5},{5,4},{6,7},{7,6},{8,9},{9,8},{10,11... | collective-permute-start | bytes 5898248 | tf_op jit(solution)/shard_map/ppermute | solution.py:30
  425.6 13.8 %collective-permute-start.46 = (bf16[960,256]{1,0:T(8,128)(2,1)}, bf16[960,256]{1,0:T(8,128)(2,1)S(1)}, u32[]{:S(2)}, u32[]{:S(2)}) collective-permute-start(bf16[960,256]{1,0:T(8,128)(2,1)} %pad_maximum_fusion.8), channel_id=1, source_target_pairs={{0,2},{1,3},{2,0},{3,1},{4,6},{5,7},{6,4},{7,5},{8,10},{9,11},{10,... | collective-permute-start | bytes 1474568 | tf_op jit(solution)/shard_map/ppermute | solution.py:34
  427.5 13.6 %collective-permute-start.45 = (bf16[960,256]{1,0:T(8,128)(2,1)}, bf16[960,256]{1,0:T(8,128)(2,1)S(1)}, u32[]{:S(2)}, u32[]{:S(2)}) collective-permute-start(bf16[960,256]{1,0:T(8,128)(2,1)} %pad_maximum_fusion.7), channel_id=1, source_target_pairs={{0,16},{16,0},{1,17},{17,1},{2,18},{18,2},{3,19},{19,3},{4,20},{20... | collective-permute-start | bytes 1474568 | tf_op jit(solution)/shard_map/ppermute | solution.py:38
  446.8 8.4 %collective-permute-start.49 = (bf16[960,128]{1,0:T(8,128)(2,1)S(1)}, bf16[960,128]{1,0:T(8,128)(2,1)S(1)}, u32[]{:S(2)}, u32[]{:S(2)}) collective-permute-start(bf16[960,128]{1,0:T(8,128)(2,1)S(1)} %get-tuple-element.193), channel_id=1, source_target_pairs={{0,2},{1,3},{2,0},{3,1},{4,6},{5,7},{6,4},{7,5},{8,10},{9,11},{10,... | collective-permute-start | bytes 737288 | tf_op jit(solution)/shard_map/ppermute | solution.py:34
  468.5 11.8 %collective-permute-start.58 = (f32[4,2048]{1,0:T(4,128)S(1)}, f32[4,2048]{1,0:T(4,128)S(1)}, u32[]{:S(2)}, u32[]{:S(2)}) collective-permute-start(f32[4,2048]{1,0:T(4,128)S(1)} %add_add_fusion.1), channel_id=1, source_target_pairs={{0,12},{4,8},{8,4},{12,0},{1,13},{5,9},{9,5},{13,1},{2,14},{6,10},... | collective-permute-start | bytes 98312 | tf_op jit(solution)/shard_map/ppermute | solution.py:459
  469.7 10.7 %collective-permute-start.57 = (f32[4,2048]{1,0:T(4,128)S(1)}, f32[4,2048]{1,0:T(4,128)S(1)}, u32[]{:S(2)}, u32[]{:S(2)}) collective-permute-start(f32[4,2048]{1,0:T(4,128)S(1)} %add_add_fusion.1), channel_id=1, source_target_pairs={{0,8},{4,12},{8,0},{12,4},{1,9},{5,13},{9,1},{13,5},{2,10},{6,14},... | collective-permute-start | bytes 98312 | tf_op jit(solution)/shard_map/ppermute | solution.py:459
  470.1 10.3 %collective-permute-start.56 = (f32[4,2048]{1,0:T(4,128)S(1)}, f32[4,2048]{1,0:T(4,128)S(1)}, u32[]{:S(2)}, u32[]{:S(2)}) collective-permute-start(f32[4,2048]{1,0:T(4,128)S(1)} %add_add_fusion.1), channel_id=1, source_target_pairs={{0,4},{4,0},{8,12},{12,8},{1,5},{5,1},{9,13},{13,9},{2,6},{6,2},{1... | collective-permute-start | bytes 98312 | tf_op jit(solution)/shard_map/ppermute | solution.py:459
  473.3 12.2 %collective-permute-start.55 = (bf16[960,256]{1,0:T(8,128)(2,1)S(1)}, bf16[960,256]{1,0:T(8,128)(2,1)S(1)}, u32[]{:S(2)}, u32[]{:S(2)}) collective-permute-start(bf16[960,256]{1,0:T(8,128)(2,1)S(1)} %pad_maximum_fusion.10), channel_id=1, source_target_pairs={{0,2},{1,3},{2,0},{3,1},{4,6},{5,7},{6,4},{7,5},{8,10},{9,11},{10,... | collective-permute-start | bytes 1474568 | tf_op jit(solution)/shard_map/ppermute | solution.py:34
  474.9 11.9 %collective-permute-start.54 = (bf16[960,256]{1,0:T(8,128)(2,1)S(1)}, bf16[960,256]{1,0:T(8,128)(2,1)S(1)}, u32[]{:S(2)}, u32[]{:S(2)}) collective-permute-start(bf16[960,256]{1,0:T(8,128)(2,1)S(1)} %pad_maximum_fusion.9), channel_id=1, source_target_pairs={{0,16},{16,0},{1,17},{17,1},{2,18},{18,2},{3,19},{19,3},{4,20},{20... | collective-permute-start | bytes 1474568 | tf_op jit(solution)/shard_map/ppermute | solution.py:38
  (43 other events, 368.2 us)
Sparse Core Ops, SparseCore 0:
  33.5 79.3 all-gather.5
  118.5 127.6 all-gather.3
  312.4 156.0 all-reduce.3

commit v4 on v3

--- a/solution.py
+++ b/solution.py
@@ -571,7 +571,7 @@
     second_left = jnp.where(is_first, normed, grad_branch_low)
     second_sum = dot(second_left, second_right, 0, 0).astype(bf16)
     if len(grad_near) > 2:
-        second_back, grad_high, grad_near[2] = meet(second_back, grad_high, grad_near[2])
+        grad_q, grad_k, grad_high[1], grad_near[2] = meet(grad_q, grad_k, grad_high[1], grad_near[2])
         grad_high.append(swap_high(grad_near[2]))
     first_back = swap_section(jnp.where(is_first, grad_q, grad_k))
     if len(grad_near) > 2:

time: 503 us -> 497 us (0.988)
  local copies, waits for them, and re-layouts: 48 us -> 39.4 us
    ppermute x1, waiting for transfers between devices: 0.01 us -> 5.5 us  [shards(): lax.ppermute(grad_far, 'dp', [(i, i ^ 1) for i in range(lax.axis_size('dp...]
  transfers between devices with their start and end apart: 62 -> 62, of which waited for: 28 -> 30; matrix products, arithmetic and copies ran while one was open for 19% -> 18% of each run, Pallas kernels for 32% -> 32%
where the time goes in v4:
time: 497 us; the launch traced here: 489 us
  waiting for transfers between devices  160 us (32%)
  Pallas kernels  157 us (32%)
  starting transfers between devices  58 us (12%)
  other arithmetic  42.3 us (9%)
  local copies, waits for them, and re-layouts  39.4 us (8%)
  between operations  16.3 us (3%)
  matrix products  15.8 us (3%)
    pallas_call x1, Pallas kernels, feed_forward_grads(): pl.pallas_call(kernel, out_shape=[jax.ShapeDtypeStruct((units, width), f3...  85.8 us
    ppermute x15, waiting for transfers between devices, swap_high(): return lax.ppermute(value, 'tensor', SWAP_HIGH)  66 us
    ppermute x16, waiting for transfers between devices, swap_section(): return lax.ppermute(value, 'section', SWAP_SECTION)  43 us
    ppermute x15, starting transfers between devices, swap_high(): return lax.ppermute(value, 'tensor', SWAP_HIGH)  21.2 us
    ppermute x16, starting transfers between devices, swap_section(): return lax.ppermute(value, 'section', SWAP_SECTION)  21.1 us
    pallas_call x1, Pallas kernels, feed_forward_own(): pl.pallas_call(kernel, out_shape=[jax.ShapeDtypeStruct((tok_count, units)...  18.1 us
    dot_general x3, matrix products, dot(): lax.dot_general(left, right, (((left_dim,), (right_dim,)), ((), ())), pre...  15.8 us
    pallas_call x1, Pallas kernels, input_gradient(): pl.pallas_call(kernel, out_shape=[jax.ShapeDtypeStruct((parts, tok_count,...  13.8 us
  transfers between devices with their start and end apart: 62, of which 30 were waited for; matrix products, arithmetic and copies ran while one was open for 18% of the time, Pallas kernels for 32%

profile of v4, /device:TPU:0, one launch (start us, length us, event | category | flops | bytes accessed | tf_op | source)
XLA Modules:
  0.0 489.4 jit_solution(6172152553220666195)
XLA Ops:
  11.9 3.0 dynamic-slice_bitcast_fusion.4
  14.9 9.1 %normed_projections.1 = (bf16[960,2048]{1,0:T(8,128)(2,1)}, bf16[2,960,256]{2,1,0:T(8,128)(2,1)}, bf16[2,960,256]{2,1,0:T(8,128)(2,1)}) custom-call(bf16[960,2048]{1,0:T(8,128)(2,1)} %inputs_ref.1, f32[1,2048]{1,0:T(1,128)} %convert_element_type.229.gain_ref, bf16[2,2048,512]{2,1,0:T(8,128)(2,1)} %bitcast.150), custom_call_target="tpu_custom_call" | custom-call | tf_op jit(solution)/shard_map/normed_projections/pallas_call | solution.py:275
  25.8 5.7 %collective-permute-start.1 = (bf16[960,256]{1,0:T(8,128)(2,1)}, bf16[960,256]{1,0:T(8,128)(2,1)}, u32[]{:S(2)}, u32[]{:S(2)}) collective-permute-start(bf16[960,256]{1,0:T(8,128)(2,1)} %slice_bitcast_fusion.1), channel_id=1, source_target_pairs={{0,16},{1,17},{2,18},{3,19},{4,20},{5,21},{6,22},{7,23},{8,24},{9,... | collective-permute-start | bytes 1474568 | tf_op jit(solution)/shard_map/ppermute | solution.py:510
  34.7 7.9 %collective-permute-done.1 = bf16[960,256]{1,0:T(8,128)(2,1)} collective-permute-done((bf16[960,256]{1,0:T(8,128)(2,1)}, bf16[960,256]{1,0:T(8,128)(2,1)}, u32[]{:S(2)}, u32[]{:S(2)}) %collective-permute-start.1) | collective-permute-done | bytes 491552 | tf_op jit(solution)/shard_map/ppermute | solution.py:510
  44.6 7.5 %collective-permute-done = bf16[960,256]{1,0:T(8,128)(2,1)} collective-permute-done((bf16[960,256]{1,0:T(8,128)(2,1)}, bf16[960,256]{1,0:T(8,128)(2,1)}, u32[]{:S(2)}, u32[]{:S(2)}) %collective-permute-start) | collective-permute-done | bytes 491552 | tf_op jit(solution)/shard_map/ppermute | solution.py:38
  52.1 2.2 bitcast_select_fusion.1
  55.4 9.7 %attend_forward.1 = (bf16[960,256]{1,0:T(8,128)(2,1)}, bf16[960,2048]{1,0:T(8,128)(2,1)}, f32[2,960,1]{2,1,0:T(8,128)}) custom-call(bf16[960,256]{1,0:T(8,128)(2,1)} %get-tuple-element.193.q_ref, bf16[960,256]{1,0:T(8,128)(2,1)} %get-tuple-element.192.k_ref, bf16[960,256]{1,0:T(8,128)(2,1)} %bitcast_select_fusion.v_ref, ...), custom_call_target="tpu_custom_call" | custom-call | tf_op jit(solution)/shard_map/attend_forward/pallas_call | solution.py:316
  66.9 4.0 collective-permute-done.3
  70.9 2.9 fusion.3
  74.0 2.6 collective-permute-start.6
  76.6 2.4 collective-permute-start.4
  79.0 3.8 collective-permute-done.6
  82.9 2.4 collective-permute-start.7
  87.3 9.1 %collective-permute-done.7 = bf16[120,2048]{1,0:T(8,128)(2,1)S(1)} collective-permute-done((bf16[120,2048]{1,0:T(8,128)(2,1)S(1)}, bf16[120,2048]{1,0:T(8,128)(2,1)S(1)}, u32[]{:S(2)}, u32[]{:S(2)}) %collective-permute-start.7) | collective-permute-done | bytes 491552 | tf_op jit(solution)/shard_map/ppermute | solution.py:34
  99.4 13.5 %all-gather.6.cloned.1.call-done = bf16[960,2048]{1,0:T(8,128)(2,1)} async-done(((bf16[240,2048]{1,0:T(8,128)(2,1)}), bf16[960,2048]{1,0:T(8,128)(2,1)}) %all-gather.6.cloned.1.call-update) | async-done | bytes 3932176 | tf_op jit(solution)/shard_map/all_gather | solution.py:500
  114.9 2.4 broadcast.48.clone
  122.0 7.9 %fusion.27.back_ref = f32[960,688]{1,0:T(8,128)} fusion(bf16[960,2048]{1,0:T(8,128)(2,1)} %param.10, bf16[688,2048]{1,0:T(8,128)(2,1)} %refs_15_.1), kind=kOutput, calls=%fused_computation.141 | convolution fusion | flops 2705326080 | bytes 9392128 | tf_op jit(solution)/shard_map/dot_general | solution.py:137
  129.9 5.8 %collective-permute-done.9 = bf16[120,2048]{1,0:T(8,128)(2,1)S(1)} collective-permute-done((bf16[120,2048]{1,0:T(8,128)(2,1)}, bf16[120,2048]{1,0:T(8,128)(2,1)S(1)}, u32[]{:S(2)}, u32[]{:S(2)}) %collective-permute-start.9) | collective-permute-done | bytes 491552 | tf_op jit(solution)/shard_map/ppermute | solution.py:38
  135.7 3.6 constant_dynamic-slice_fusion.1
  144.0 3.7 collective-permute-done.13
  154.3 18.1 %feed_forward_own.1 = (bf16[960,688]{1,0:T(8,128)(2,1)}, bf16[960,2048]{1,0:T(8,128)(2,1)}) custom-call(bf16[960,2048]{1,0:T(8,128)(2,1)} %constant_dynamic-update-slice_fusion.18.in_ref, f32[960,688]{1,0:T(8,128)} %fusion.27.back_ref, bf16[688,2048]{1,0:T(8,128)(2,1)} %bitcast.156, bf16[688,2048]{1,0:T(8,128)(2,1)} %bitcast.158), custom_call_target="tpu_custom_call" | custom-call | tf_op jit(solution)/shard_map/feed_forward_own/pallas_call | solution.py:378
  174.7 3.6 collective-permute-done.17
  181.6 8.8 %output_parts.1 = bf16[8,960,256]{2,1,0:T(8,128)(2,1)} custom-call(bf16[960,688]{1,0:T(8,128)(2,1)} %get-tuple-element.94.hidden_ref, bf16[688,2048]{1,0:T(8,128)(2,1)} %refs_15_.1), custom_call_target="tpu_custom_call" | custom-call | tf_op jit(solution)/shard_map/output_parts/pallas_call | solution.py:430
  190.4 2.8 collective-permute-done.19
  197.2 20.9 %collective-permute-done.22 = bf16[120,2048]{1,0:T(8,128)(2,1)S(1)} collective-permute-done((bf16[120,2048]{1,0:T(8,128)(2,1)S(1)}, bf16[120,2048]{1,0:T(8,128)(2,1)S(1)}, u32[]{:S(2)}, u32[]{:S(2)}) %collective-permute-start.22) | collective-permute-done | bytes 491552 | tf_op jit(solution)/shard_map/ppermute | solution.py:34
  226.2 9.6 %collective-permute-done.24 = bf16[120,2048]{1,0:T(8,128)(2,1)S(1)} collective-permute-done((bf16[120,2048]{1,0:T(8,128)(2,1)S(1)}, bf16[120,2048]{1,0:T(8,128)(2,1)S(1)}, u32[]{:S(2)}, u32[]{:S(2)}) %collective-permute-start.24) | collective-permute-done | bytes 491552 | tf_op jit(solution)/shard_map/ppermute | solution.py:38
  235.8 2.9 dynamic-slice_bitcast_fusion.1
  241.8 5.4 %collective-permute-done.28 = bf16[120,1024]{1,0:T(8,128)(2,1)S(1)} collective-permute-done((bf16[120,1024]{1,0:T(8,128)(2,1)S(1)}, bf16[120,1024]{1,0:T(8,128)(2,1)S(1)}, u32[]{:S(2)}, u32[]{:S(2)}) %collective-permute-start.28) | collective-permute-done | bytes 245792 | tf_op jit(solution)/shard_map/ppermute | solution.py:34
  252.0 11.9 %attend_backward.1 = (bf16[960,256]{1,0:T(8,128)(2,1)}, bf16[960,256]{1,0:T(8,128)(2,1)}, bf16[960,256]{1,0:T(8,128)(2,1)}) custom-call(bf16[960,256]{1,0:T(8,128)(2,1)} %get-tuple-element.193.q_ref, bf16[960,256]{1,0:T(8,128)(2,1)} %get-tuple-element.192.k_ref, bf16[960,256]{1,0:T(8,128)(2,1)} %bitcast_select_fusion.v_ref, ...), custom_call_target="tpu_custom_call" | custom-call | tf_op jit(solution)/shard_map/attend_backward/pallas_call | solution.py:350
  269.9 3.3 fusion.1
  273.2 5.2 %collective-permute-done.36 = bf16[960,256]{1,0:T(8,128)(2,1)} collective-permute-done((bf16[960,256]{1,0:T(8,128)(2,1)}, bf16[960,256]{1,0:T(8,128)(2,1)}, u32[]{:S(2)}, u32[]{:S(2)}) %collective-permute-start.36) | collective-permute-done | bytes 491552 | tf_op jit(solution)/shard_map/ppermute | solution.py:38
  282.0 4.2 fusion.7
  286.2 5.5 %collective-permute-done.34.refs_4_ = bf16[1,240,2048]{2,1,0:T(8,128)(2,1)} collective-permute-done((bf16[1,240,2048]{2,1,0:T(8,128)(2,1)}, bf16[1,240,2048]{2,1,0:T(8,128)(2,1)}, u32[]{:S(2)}, u32[]{:S(2)}) %collective-permute-start.34) | collective-permute-done | bytes 983072 | tf_op jit(solution)/shard_map/ppermute | solution.py:553
  293.0 10.0 %collective-permute-done.35.refs_6_ = bf16[1,240,2048]{2,1,0:T(8,128)(2,1)} collective-permute-done((bf16[1,240,2048]{2,1,0:T(8,128)(2,1)}, bf16[1,240,2048]{2,1,0:T(8,128)(2,1)}, u32[]{:S(2)}, u32[]{:S(2)}) %collective-permute-start.35) | collective-permute-done | bytes 983072 | tf_op jit(solution)/shard_map/ppermute | solution.py:34
  304.0 3.8 convolution_convert_fusion
  311.1 2.3 broadcast_select_fusion.value_ref
  314.5 85.8 %feed_forward_grads.1 = (f32[688,2048]{1,0:T(8,128)}, f32[688,2048]{1,0:T(8,128)}, f32[688,2048]{1,0:T(8,128)}) custom-call(s32[16]{0:T(128)} %stack.88.order_ref, bf16[16,240,2048]{2,1,0:T(8,128)(2,1)} %bitcast.155, bf16[4,240,2048]{2,1,0:T(8,128)(2,1)} %bitcast.160, bf16[1,240,2048]{2,1,0:T(8,128)(2,1)} %get-tuple-element.125.refs_1_, ...), custom_call_target="tpu_custom_call" | custom-call | tf_op jit(solution)/shard_map/feed_forward_grads/pallas_call | solution.py:230
  400.3 13.8 %input_gradient.1 = (bf16[8,960,256]{2,1,0:T(8,128)(2,1)}, f32[1,2048]{1,0:T(1,128)}) custom-call(bf16[960,2048]{1,0:T(8,128)(2,1)} %inputs_ref.1, f32[1,2048]{1,0:T(1,128)} %convert_element_type.229.gain_ref, bf16[960,512]{1,0:T(8,128)(2,1)} %pad_maximum_fusion.first_ref, bf16[960,512]{1,0:T(8,128)(2,1)} %broadcast_select_fusion.value_ref, ...), custom_call_target="tpu_custom_call" | custom-call | tf_op jit(solution)/shard_map/input_gradient/pallas_call | solution.py:412
  414.2 2.0 fusion.17
  416.2 3.0 dynamic-slice_bitcast_fusion
  424.4 9.6 %collective-permute-done.46 = bf16[960,256]{1,0:T(8,128)(2,1)S(1)} collective-permute-done((bf16[960,256]{1,0:T(8,128)(2,1)}, bf16[960,256]{1,0:T(8,128)(2,1)S(1)}, u32[]{:S(2)}, u32[]{:S(2)}) %collective-permute-start.46) | collective-permute-done | bytes 491552 | tf_op jit(solution)/shard_map/ppermute | solution.py:34
  434.0 2.1 collective-permute-done.45
  439.6 2.0 fusion
  446.0 2.5 collective-permute-done.53
  450.4 12.8 %all-reduce.4.cloned.1.call-done = (bf16[2048,512]{1,0:T(8,128)(2,1)}, bf16[2048,512]{1,0:T(8,128)(2,1)}) async-done(((bf16[2048,512]{1,0:T(8,128)(2,1)}, bf16[2048,512]{1,0:T(8,128)(2,1)}), (bf16[2048,512]{1,0:T(8,128)(2,1)}, bf16[2048,512]{1,0:T(8,128)(2,1)})) %all-reduce.4.cloned.1.call-update) | async-done | bytes 4194320 | tf_op jit(solution)/shard_map/psum | solution.py:616
  464.8 2.9 collective-permute-start.56
  471.1 3.9 maximum_convert_fusion
  477.5 2.7 collective-permute-done.55
  (255 shorter events, 102.6 us)
Async XLA Ops:
  7.2 105.7 %all-gather.6.cloned.1.call-start = ((), (), s32[]{:S(2)}) async-start(), calls=%async_computation.1 | async-start | bytes 4915200 | tf_op jit(solution)/shard_map/all_gather | solution.py:500
  10.0 44.3 %collective-permute-start.2 = (bf16[2048,256]{1,0:T(8,128)(2,1)}, bf16[2048,256]{1,0:T(8,128)(2,1)S(1)}, u32[]{:S(2)}, u32[]{:S(2)}) collective-permute-start(bf16[2048,256]{1,0:T(8,128)(2,1)} %slice.150), channel_id=1, source_target_pairs={{16,0},{17,1},{18,2},{19,3},{20,4},{21,5},{22,6},{23,7},{24,8},{25... | collective-permute-start | bytes 3145736 | tf_op jit(solution)/shard_map/ppermute | solution.py:511
  25.8 16.8 %collective-permute-start.1 = (bf16[960,256]{1,0:T(8,128)(2,1)}, bf16[960,256]{1,0:T(8,128)(2,1)}, u32[]{:S(2)}, u32[]{:S(2)}) collective-permute-start(bf16[960,256]{1,0:T(8,128)(2,1)} %slice_bitcast_fusion.1), channel_id=1, source_target_pairs={{0,16},{1,17},{2,18},{3,19},{4,20},{5,21},{6,22},{7,23},{8,24},{9,... | collective-permute-start | bytes 1474568 | tf_op jit(solution)/shard_map/ppermute | solution.py:510
  33.4 18.7 %collective-permute-start = (bf16[960,256]{1,0:T(8,128)(2,1)}, bf16[960,256]{1,0:T(8,128)(2,1)}, u32[]{:S(2)}, u32[]{:S(2)}) collective-permute-start(bf16[960,256]{1,0:T(8,128)(2,1)} %dynamic-slice_bitcast_fusion.20), channel_id=1, source_target_pairs={{0,16},{16,0},{1,17},{17,1},{2,18},{18,2},{3,19},{19,3},{4,20},{20... | collective-permute-start | bytes 1474568 | tf_op jit(solution)/shard_map/ppermute | solution.py:38
  33.4 274.4 %all-gather.4.cloned.1.call-start = ((), (), s32[]{:S(2)}) async-start(), calls=%async_computation | async-start | bytes 16220160 | tf_op jit(solution)/shard_map/all_gather | solution.py:527
  74.0 8.8 %collective-permute-start.6 = (bf16[120,1024]{1,0:T(8,128)(2,1)S(1)}, bf16[120,1024]{1,0:T(8,128)(2,1)S(1)}, u32[]{:S(2)}, u32[]{:S(2)}) collective-permute-start(bf16[120,1024]{1,0:T(8,128)(2,1)S(1)} %get-tuple-element.202), channel_id=1, source_target_pairs={{0,16},{16,0},{1,17},{17,1},{2,18},{18,2},{3,19},{19,3},{4,20},{20... | collective-permute-start | bytes 737288 | tf_op jit(solution)/shard_map/ppermute | solution.py:38
  76.6 8.7 %collective-permute-start.4 = (bf16[120,1024]{1,0:T(8,128)(2,1)S(1)}, bf16[120,1024]{1,0:T(8,128)(2,1)S(1)}, u32[]{:S(2)}, u32[]{:S(2)}) collective-permute-start(bf16[120,1024]{1,0:T(8,128)(2,1)S(1)} %get-tuple-element.201), channel_id=1, source_target_pairs={{0,2},{1,3},{2,0},{3,1},{4,6},{5,7},{6,4},{7,5},{8,10},{9,11},{10,... | collective-permute-start | bytes 737288 | tf_op jit(solution)/shard_map/ppermute | solution.py:34
  82.9 13.5 %collective-permute-start.7 = (bf16[120,2048]{1,0:T(8,128)(2,1)S(1)}, bf16[120,2048]{1,0:T(8,128)(2,1)S(1)}, u32[]{:S(2)}, u32[]{:S(2)}) collective-permute-start(bf16[120,2048]{1,0:T(8,128)(2,1)S(1)} %pad_maximum_fusion.4), channel_id=1, source_target_pairs={{0,2},{1,3},{2,0},{3,1},{4,6},{5,7},{6,4},{7,5},{8,10},{9,11},{10,... | collective-permute-start | bytes 1474568 | tf_op jit(solution)/shard_map/ppermute | solution.py:34
  85.4 12.7 %collective-permute-start.5 = (bf16[120,2048]{1,0:T(8,128)(2,1)S(1)}, bf16[120,2048]{1,0:T(8,128)(2,1)}, u32[]{:S(2)}, u32[]{:S(2)}) collective-permute-start(bf16[120,2048]{1,0:T(8,128)(2,1)S(1)} %pad_maximum_fusion.3), channel_id=1, source_target_pairs={{0,16},{16,0},{1,17},{17,1},{2,18},{18,2},{3,19},{19,3},{4,20},{20... | collective-permute-start | bytes 1474568 | tf_op jit(solution)/shard_map/ppermute | solution.py:38
  118.4 344.8 %all-reduce.4.cloned.1.call-start = ((), (), s32[]{:S(2)}) async-start(), calls=%async_computation.2 | async-start | bytes 8388608 | tf_op jit(solution)/shard_map/psum | solution.py:616
  118.9 16.8 %collective-permute-start.9 = (bf16[120,2048]{1,0:T(8,128)(2,1)}, bf16[120,2048]{1,0:T(8,128)(2,1)S(1)}, u32[]{:S(2)}, u32[]{:S(2)}) collective-permute-start(bf16[120,2048]{1,0:T(8,128)(2,1)} %get-tuple-element.123), channel_id=1, source_target_pairs={{0,16},{16,0},{1,17},{17,1},{2,18},{18,2},{3,19},{19,3},{4,20},{20... | collective-permute-start | bytes 1474568 | tf_op jit(solution)/shard_map/ppermute | solution.py:38
  120.5 21.9 %collective-permute-start.8 = (bf16[120,2048]{1,0:T(8,128)(2,1)}, bf16[120,2048]{1,0:T(8,128)(2,1)S(1)}, u32[]{:S(2)}, u32[]{:S(2)}) collective-permute-start(bf16[120,2048]{1,0:T(8,128)(2,1)} %get-tuple-element.123), channel_id=1, source_target_pairs={{0,1},{1,0},{2,3},{3,2},{4,5},{5,4},{6,7},{7,6},{8,9},{9,8},{10,11... | collective-permute-start | bytes 1474568 | tf_op jit(solution)/shard_map/ppermute | solution.py:30
  120.5 20.3 %collective-permute-start.11 = (bf16[120,2048]{1,0:T(8,128)(2,1)}, bf16[120,2048]{1,0:T(8,128)(2,1)S(1)}, u32[]{:S(2)}, u32[]{:S(2)}) collective-permute-start(bf16[120,2048]{1,0:T(8,128)(2,1)} %get-tuple-element.123), channel_id=1, source_target_pairs={{0,2},{1,3},{2,0},{3,1},{4,6},{5,7},{6,4},{7,5},{8,10},{9,11},{10,... | collective-permute-start | bytes 1474568 | tf_op jit(solution)/shard_map/ppermute | solution.py:34
  135.7 13.3 %collective-permute-start.10 = (bf16[120,2048]{1,0:T(8,128)(2,1)S(1)}, bf16[120,2048]{1,0:T(8,128)(2,1)S(1)}, u32[]{:S(2)}, u32[]{:S(2)}) collective-permute-start(bf16[120,2048]{1,0:T(8,128)(2,1)S(1)} %collective-permute-done.9), channel_id=1, source_target_pairs={{0,1},{1,0},{2,3},{3,2},{4,5},{5,4},{6,7},{7,6},{8,9},{9,8},{10,11... | collective-permute-start | bytes 1474568 | tf_op jit(solution)/shard_map/ppermute | solution.py:30
  139.3 8.4 %collective-permute-start.13 = (bf16[120,1024]{1,0:T(8,128)(2,1)S(1)}, bf16[120,1024]{1,0:T(8,128)(2,1)S(1)}, u32[]{:S(2)}, u32[]{:S(2)}) collective-permute-start(bf16[120,1024]{1,0:T(8,128)(2,1)S(1)} %slice.158), channel_id=1, source_target_pairs={{0,2},{1,3},{2,0},{3,1},{4,6},{5,7},{6,4},{7,5},{8,10},{9,11},{10,... | collective-permute-start | bytes 737288 | tf_op jit(solution)/shard_map/ppermute | solution.py:34
  140.8 8.1 %collective-permute-start.15 = (bf16[120,1024]{1,0:T(8,128)(2,1)S(1)}, bf16[120,1024]{1,0:T(8,128)(2,1)S(1)}, u32[]{:S(2)}, u32[]{:S(2)}) collective-permute-start(bf16[120,1024]{1,0:T(8,128)(2,1)S(1)} %slice.159), channel_id=1, source_target_pairs={{0,16},{16,0},{1,17},{17,1},{2,18},{18,2},{3,19},{19,3},{4,20},{20... | collective-permute-start | bytes 737288 | tf_op jit(solution)/shard_map/ppermute | solution.py:38
  142.4 8.2 %collective-permute-start.12 = (bf16[120,2048]{1,0:T(8,128)(2,1)S(1)}, bf16[120,2048]{1,0:T(8,128)(2,1)S(1)}, u32[]{:S(2)}, u32[]{:S(2)}) collective-permute-start(bf16[120,2048]{1,0:T(8,128)(2,1)S(1)} %collective-permute-done.11), channel_id=1, source_target_pairs={{0,1},{1,0},{2,3},{3,2},{4,5},{5,4},{6,7},{7,6},{8,9},{9,8},{10,11... | collective-permute-start | bytes 1474568 | tf_op jit(solution)/shard_map/ppermute | solution.py:30
  179.4 13.7 %collective-permute-start.19 = (bf16[120,1024]{1,0:T(8,128)(2,1)S(1)}, bf16[120,1024]{1,0:T(8,128)(2,1)S(1)}, u32[]{:S(2)}, u32[]{:S(2)}) collective-permute-start(bf16[120,1024]{1,0:T(8,128)(2,1)S(1)} %get-tuple-element.199), channel_id=1, source_target_pairs={{0,2},{1,3},{2,0},{3,1},{4,6},{5,7},{6,4},{7,5},{8,10},{9,11},{10,... | collective-permute-start | bytes 737288 | tf_op jit(solution)/shard_map/ppermute | solution.py:34
  180.1 13.7 %collective-permute-start.18 = (bf16[120,1024]{1,0:T(8,128)(2,1)S(1)}, bf16[120,1024]{1,0:T(8,128)(2,1)S(1)}, u32[]{:S(2)}, u32[]{:S(2)}) collective-permute-start(bf16[120,1024]{1,0:T(8,128)(2,1)S(1)} %get-tuple-element.200), channel_id=1, source_target_pairs={{0,16},{16,0},{1,17},{17,1},{2,18},{18,2},{3,19},{19,3},{4,20},{20... | collective-permute-start | bytes 737288 | tf_op jit(solution)/shard_map/ppermute | solution.py:38
  194.0 24.1 %collective-permute-start.22 = (bf16[120,2048]{1,0:T(8,128)(2,1)S(1)}, bf16[120,2048]{1,0:T(8,128)(2,1)S(1)}, u32[]{:S(2)}, u32[]{:S(2)}) collective-permute-start(bf16[120,2048]{1,0:T(8,128)(2,1)S(1)} %pad_maximum_fusion.6), channel_id=1, source_target_pairs={{0,2},{1,3},{2,0},{3,1},{4,6},{5,7},{6,4},{7,5},{8,10},{9,11},{10,... | collective-permute-start | bytes 1474568 | tf_op jit(solution)/shard_map/ppermute | solution.py:34
  195.6 24.0 %collective-permute-start.21 = (bf16[120,2048]{1,0:T(8,128)(2,1)S(1)}, bf16[120,2048]{1,0:T(8,128)(2,1)S(1)}, u32[]{:S(2)}, u32[]{:S(2)}) collective-permute-start(bf16[120,2048]{1,0:T(8,128)(2,1)S(1)} %pad_maximum_fusion.5), channel_id=1, source_target_pairs={{0,16},{16,0},{1,17},{17,1},{2,18},{18,2},{3,19},{19,3},{4,20},{20... | collective-permute-start | bytes 1474568 | tf_op jit(solution)/shard_map/ppermute | solution.py:38
  222.0 13.8 %collective-permute-start.24 = (bf16[120,2048]{1,0:T(8,128)(2,1)S(1)}, bf16[120,2048]{1,0:T(8,128)(2,1)S(1)}, u32[]{:S(2)}, u32[]{:S(2)}) collective-permute-start(bf16[120,2048]{1,0:T(8,128)(2,1)S(1)} %get-tuple-element.160), channel_id=1, source_target_pairs={{0,16},{16,0},{1,17},{17,1},{2,18},{18,2},{3,19},{19,3},{4,20},{20... | collective-permute-start | bytes 1474568 | tf_op jit(solution)/shard_map/ppermute | solution.py:38
  223.6 17.2 %collective-permute-start.26 = (bf16[120,2048]{1,0:T(8,128)(2,1)S(1)}, bf16[120,2048]{1,0:T(8,128)(2,1)S(1)}, u32[]{:S(2)}, u32[]{:S(2)}) collective-permute-start(bf16[120,2048]{1,0:T(8,128)(2,1)S(1)} %get-tuple-element.160), channel_id=1, source_target_pairs={{0,2},{1,3},{2,0},{3,1},{4,6},{5,7},{6,4},{7,5},{8,10},{9,11},{10,... | collective-permute-start | bytes 1474568 | tf_op jit(solution)/shard_map/ppermute | solution.py:34
  224.2 17.5 %collective-permute-start.23 = (bf16[120,2048]{1,0:T(8,128)(2,1)S(1)}, bf16[120,2048]{1,0:T(8,128)(2,1)S(1)}, u32[]{:S(2)}, u32[]{:S(2)}) collective-permute-start(bf16[120,2048]{1,0:T(8,128)(2,1)S(1)} %get-tuple-element.160), channel_id=1, source_target_pairs={{0,1},{1,0},{2,3},{3,2},{4,5},{5,4},{6,7},{7,6},{8,9},{9,8},{10,11... | collective-permute-start | bytes 1474568 | tf_op jit(solution)/shard_map/ppermute | solution.py:30
  235.8 12.7 %collective-permute-start.25 = (bf16[120,2048]{1,0:T(8,128)(2,1)S(1)}, bf16[120,2048]{1,0:T(8,128)(2,1)S(1)}, u32[]{:S(2)}, u32[]{:S(2)}) collective-permute-start(bf16[120,2048]{1,0:T(8,128)(2,1)S(1)} %collective-permute-done.24), channel_id=1, source_target_pairs={{0,1},{1,0},{2,3},{3,2},{4,5},{5,4},{6,7},{7,6},{8,9},{9,8},{10,11... | collective-permute-start | bytes 1474568 | tf_op jit(solution)/shard_map/ppermute | solution.py:30
  238.7 29.7 %collective-permute-start.20 = (bf16[4,960,256]{2,1,0:T(8,128)(2,1)}, bf16[4,960,256]{2,1,0:T(8,128)(2,1)S(1)}, u32[]{:S(2)}, u32[]{:S(2)}) collective-permute-start(bf16[4,960,256]{2,1,0:T(8,128)(2,1)} %dynamic-slice_bitcast_fusion.1), channel_id=1, source_target_pairs={{0,1},{1,0},{2,3},{3,2},{4,5},{5,4},{6,7},{7,6},{8,9},{9,8},{10,11... | collective-permute-start | bytes 5898248 | tf_op jit(solution)/shard_map/ppermute | solution.py:30
  250.0 29.5 %collective-permute-start.32 = (bf16[1,240,2048]{2,1,0:T(8,128)(2,1)}, bf16[1,240,2048]{2,1,0:T(8,128)(2,1)}, u32[]{:S(2)}, u32[]{:S(2)}) collective-permute-start(bf16[1,240,2048]{2,1,0:T(8,128)(2,1)} %get-tuple-element.109.refs_2_), channel_id=1, source_target_pairs={{0,2},{1,3},{2,0},{3,1},{4,6},{5,7},{6,4},{7,5},{8,10},{9,11},{10,... | collective-permute-start | bytes 2949128 | tf_op jit(solution)/shard_map/ppermute | solution.py:34
  264.7 13.7 %collective-permute-start.36 = (bf16[960,256]{1,0:T(8,128)(2,1)}, bf16[960,256]{1,0:T(8,128)(2,1)}, u32[]{:S(2)}, u32[]{:S(2)}) collective-permute-start(bf16[960,256]{1,0:T(8,128)(2,1)} %broadcast_select_fusion.3), channel_id=1, source_target_pairs={{0,16},{16,0},{1,17},{17,1},{2,18},{18,2},{3,19},{19,3},{4,20},{20... | collective-permute-start | bytes 1474568 | tf_op jit(solution)/shard_map/ppermute | solution.py:38
  267.2 41.7 %collective-permute-start.40 = (bf16[1,240,2048]{2,1,0:T(8,128)(2,1)}, bf16[1,240,2048]{2,1,0:T(8,128)(2,1)}, u32[]{:S(2)}, u32[]{:S(2)}) collective-permute-start(bf16[1,240,2048]{2,1,0:T(8,128)(2,1)} %get-tuple-element.109.refs_2_), channel_id=1, source_target_pairs={{0,1},{1,0},{2,3},{3,2},{4,5},{5,4},{6,7},{7,6},{8,9},{9,8},{10,11... | collective-permute-start | bytes 2949128 | tf_op jit(solution)/shard_map/ppermute | solution.py:30
  267.2 24.5 %collective-permute-start.34 = (bf16[1,240,2048]{2,1,0:T(8,128)(2,1)}, bf16[1,240,2048]{2,1,0:T(8,128)(2,1)}, u32[]{:S(2)}, u32[]{:S(2)}) collective-permute-start(bf16[1,240,2048]{2,1,0:T(8,128)(2,1)} %get-tuple-element.114), channel_id=1, source_target_pairs={{0,4},{4,0},{8,12},{12,8},{1,5},{5,1},{9,13},{13,9},{2,6},{6,2},{1... | collective-permute-start | bytes 2949128 | tf_op jit(solution)/shard_map/ppermute | solution.py:553
  269.7 34.0 %collective-permute-start.39 = (bf16[1,240,2048]{2,1,0:T(8,128)(2,1)}, bf16[1,240,2048]{2,1,0:T(8,128)(2,1)}, u32[]{:S(2)}, u32[]{:S(2)}) collective-permute-start(bf16[1,240,2048]{2,1,0:T(8,128)(2,1)} %get-tuple-element.125.refs_1_), channel_id=1, source_target_pairs={{0,1},{1,0},{2,3},{3,2},{4,5},{5,4},{6,7},{7,6},{8,9},{9,8},{10,11... | collective-permute-start | bytes 2949128 | tf_op jit(solution)/shard_map/ppermute | solution.py:30
  279.5 23.5 %collective-permute-start.35 = (bf16[1,240,2048]{2,1,0:T(8,128)(2,1)}, bf16[1,240,2048]{2,1,0:T(8,128)(2,1)}, u32[]{:S(2)}, u32[]{:S(2)}) collective-permute-start(bf16[1,240,2048]{2,1,0:T(8,128)(2,1)} %get-tuple-element.116.refs_3_), channel_id=1, source_target_pairs={{0,2},{1,3},{2,0},{3,1},{4,6},{5,7},{6,4},{7,5},{8,10},{9,11},{10,... | collective-permute-start | bytes 2949128 | tf_op jit(solution)/shard_map/ppermute | solution.py:34
  280.8 12.2 %collective-permute-start.33 = (bf16[960,256]{1,0:T(8,128)(2,1)S(1)}, bf16[960,256]{1,0:T(8,128)(2,1)S(1)}, u32[]{:S(2)}, u32[]{:S(2)}) collective-permute-start(bf16[960,256]{1,0:T(8,128)(2,1)S(1)} %broadcast_select_fusion.7), channel_id=1, source_target_pairs={{0,16},{16,0},{1,17},{17,1},{2,18},{18,2},{3,19},{19,3},{4,20},{20... | collective-permute-start | bytes 1474568 | tf_op jit(solution)/shard_map/ppermute | solution.py:38
  291.7 18.2 %collective-permute-start.41 = (bf16[1,240,2048]{2,1,0:T(8,128)(2,1)}, bf16[1,240,2048]{2,1,0:T(8,128)(2,1)}, u32[]{:S(2)}, u32[]{:S(2)}) collective-permute-start(bf16[1,240,2048]{2,1,0:T(8,128)(2,1)} %get-tuple-element.116.refs_3_), channel_id=1, source_target_pairs={{0,1},{1,0},{2,3},{3,2},{4,5},{5,4},{6,7},{7,6},{8,9},{9,8},{10,11... | collective-permute-start | bytes 2949128 | tf_op jit(solution)/shard_map/ppermute | solution.py:30
  303.1 11.3 %collective-permute-start.42 = (bf16[1,240,2048]{2,1,0:T(8,128)(2,1)}, bf16[1,240,2048]{2,1,0:T(8,128)(2,1)}, u32[]{:S(2)}, u32[]{:S(2)}) collective-permute-start(bf16[1,240,2048]{2,1,0:T(8,128)(2,1)} %collective-permute-done.34.refs_4_), channel_id=1, source_target_pairs={{0,1},{1,0},{2,3},{3,2},{4,5},{5,4},{6,7},{7,6},{8,9},{9,8},{10,11... | collective-permute-start | bytes 2949128 | tf_op jit(solution)/shard_map/ppermute | solution.py:30
  303.2 11.3 %collective-permute-start.43 = (bf16[1,240,2048]{2,1,0:T(8,128)(2,1)}, bf16[1,240,2048]{2,1,0:T(8,128)(2,1)}, u32[]{:S(2)}, u32[]{:S(2)}) collective-permute-start(bf16[1,240,2048]{2,1,0:T(8,128)(2,1)} %collective-permute-done.32.refs_5_), channel_id=1, source_target_pairs={{0,1},{1,0},{2,3},{3,2},{4,5},{5,4},{6,7},{7,6},{8,9},{9,8},{10,11... | collective-permute-start | bytes 2949128 | tf_op jit(solution)/shard_map/ppermute | solution.py:30
  303.7 10.8 %collective-permute-start.44 = (bf16[1,240,2048]{2,1,0:T(8,128)(2,1)}, bf16[1,240,2048]{2,1,0:T(8,128)(2,1)}, u32[]{:S(2)}, u32[]{:S(2)}) collective-permute-start(bf16[1,240,2048]{2,1,0:T(8,128)(2,1)} %collective-permute-done.35.refs_6_), channel_id=1, source_target_pairs={{0,1},{1,0},{2,3},{3,2},{4,5},{5,4},{6,7},{7,6},{8,9},{9,8},{10,11... | collective-permute-start | bytes 2949128 | tf_op jit(solution)/shard_map/ppermute | solution.py:30
  308.8 91.5 %collective-permute-start.38 = (bf16[960,128]{1,0:T(8,128)(2,1)S(1)}, bf16[960,128]{1,0:T(8,128)(2,1)S(1)}, u32[]{:S(2)}, u32[]{:S(2)}) collective-permute-start(bf16[960,128]{1,0:T(8,128)(2,1)S(1)} %get-tuple-element.197), channel_id=1, source_target_pairs={{0,2},{1,3},{2,0},{3,1},{4,6},{5,7},{6,4},{7,5},{8,10},{9,11},{10,... | collective-permute-start | bytes 737288 | tf_op jit(solution)/shard_map/ppermute | solution.py:34
  309.9 90.4 %collective-permute-start.37 = (bf16[960,128]{1,0:T(8,128)(2,1)S(1)}, bf16[960,128]{1,0:T(8,128)(2,1)S(1)}, u32[]{:S(2)}, u32[]{:S(2)}) collective-permute-start(bf16[960,128]{1,0:T(8,128)(2,1)S(1)} %get-tuple-element.198), channel_id=1, source_target_pairs={{0,16},{16,0},{1,17},{17,1},{2,18},{18,2},{3,19},{19,3},{4,20},{20... | collective-permute-start | bytes 737288 | tf_op jit(solution)/shard_map/ppermute | solution.py:38
  419.2 20.5 %collective-permute-start.47 = (bf16[4,960,256]{2,1,0:T(8,128)(2,1)}, bf16[4,960,256]{2,1,0:T(8,128)(2,1)S(1)}, u32[]{:S(2)}, u32[]{:S(2)}) collective-permute-start(bf16[4,960,256]{2,1,0:T(8,128)(2,1)} %dynamic-slice_bitcast_fusion), channel_id=1, source_target_pairs={{0,1},{1,0},{2,3},{3,2},{4,5},{5,4},{6,7},{7,6},{8,9},{9,8},{10,11... | collective-permute-start | bytes 5898248 | tf_op jit(solution)/shard_map/ppermute | solution.py:30
  420.2 13.8 %collective-permute-start.46 = (bf16[960,256]{1,0:T(8,128)(2,1)}, bf16[960,256]{1,0:T(8,128)(2,1)S(1)}, u32[]{:S(2)}, u32[]{:S(2)}) collective-permute-start(bf16[960,256]{1,0:T(8,128)(2,1)} %pad_maximum_fusion.8), channel_id=1, source_target_pairs={{0,2},{1,3},{2,0},{3,1},{4,6},{5,7},{6,4},{7,5},{8,10},{9,11},{10,... | collective-permute-start | bytes 1474568 | tf_op jit(solution)/shard_map/ppermute | solution.py:34
  422.5 13.6 %collective-permute-start.45 = (bf16[960,256]{1,0:T(8,128)(2,1)}, bf16[960,256]{1,0:T(8,128)(2,1)S(1)}, u32[]{:S(2)}, u32[]{:S(2)}) collective-permute-start(bf16[960,256]{1,0:T(8,128)(2,1)} %pad_maximum_fusion.7), channel_id=1, source_target_pairs={{0,16},{16,0},{1,17},{17,1},{2,18},{18,2},{3,19},{19,3},{4,20},{20... | collective-permute-start | bytes 1474568 | tf_op jit(solution)/shard_map/ppermute | solution.py:38
  441.8 8.6 %collective-permute-start.49 = (bf16[960,128]{1,0:T(8,128)(2,1)S(1)}, bf16[960,128]{1,0:T(8,128)(2,1)S(1)}, u32[]{:S(2)}, u32[]{:S(2)}) collective-permute-start(bf16[960,128]{1,0:T(8,128)(2,1)S(1)} %get-tuple-element.195), channel_id=1, source_target_pairs={{0,2},{1,3},{2,0},{3,1},{4,6},{5,7},{6,4},{7,5},{8,10},{9,11},{10,... | collective-permute-start | bytes 737288 | tf_op jit(solution)/shard_map/ppermute | solution.py:34
  463.2 11.8 %collective-permute-start.58 = (f32[4,2048]{1,0:T(4,128)S(1)}, f32[4,2048]{1,0:T(4,128)S(1)}, u32[]{:S(2)}, u32[]{:S(2)}) collective-permute-start(f32[4,2048]{1,0:T(4,128)S(1)} %add_add_fusion.1), channel_id=1, source_target_pairs={{0,12},{4,8},{8,4},{12,0},{1,13},{5,9},{9,5},{13,1},{2,14},{6,10},... | collective-permute-start | bytes 98312 | tf_op jit(solution)/shard_map/ppermute | solution.py:459
  464.4 10.7 %collective-permute-start.57 = (f32[4,2048]{1,0:T(4,128)S(1)}, f32[4,2048]{1,0:T(4,128)S(1)}, u32[]{:S(2)}, u32[]{:S(2)}) collective-permute-start(f32[4,2048]{1,0:T(4,128)S(1)} %add_add_fusion.1), channel_id=1, source_target_pairs={{0,8},{4,12},{8,0},{12,4},{1,9},{5,13},{9,1},{13,5},{2,10},{6,14},... | collective-permute-start | bytes 98312 | tf_op jit(solution)/shard_map/ppermute | solution.py:459
  464.8 10.3 %collective-permute-start.56 = (f32[4,2048]{1,0:T(4,128)S(1)}, f32[4,2048]{1,0:T(4,128)S(1)}, u32[]{:S(2)}, u32[]{:S(2)}) collective-permute-start(f32[4,2048]{1,0:T(4,128)S(1)} %add_add_fusion.1), channel_id=1, source_target_pairs={{0,4},{4,0},{8,12},{12,8},{1,5},{5,1},{9,13},{13,9},{2,6},{6,2},{1... | collective-permute-start | bytes 98312 | tf_op jit(solution)/shard_map/ppermute | solution.py:459
  467.9 12.2 %collective-permute-start.55 = (bf16[960,256]{1,0:T(8,128)(2,1)S(1)}, bf16[960,256]{1,0:T(8,128)(2,1)S(1)}, u32[]{:S(2)}, u32[]{:S(2)}) collective-permute-start(bf16[960,256]{1,0:T(8,128)(2,1)S(1)} %pad_maximum_fusion.10), channel_id=1, source_target_pairs={{0,2},{1,3},{2,0},{3,1},{4,6},{5,7},{6,4},{7,5},{8,10},{9,11},{10,... | collective-permute-start | bytes 1474568 | tf_op jit(solution)/shard_map/ppermute | solution.py:34
  469.6 11.9 %collective-permute-start.54 = (bf16[960,256]{1,0:T(8,128)(2,1)S(1)}, bf16[960,256]{1,0:T(8,128)(2,1)S(1)}, u32[]{:S(2)}, u32[]{:S(2)}) collective-permute-start(bf16[960,256]{1,0:T(8,128)(2,1)S(1)} %pad_maximum_fusion.9), channel_id=1, source_target_pairs={{0,16},{16,0},{1,17},{17,1},{2,18},{18,2},{3,19},{19,3},{4,20},{20... | collective-permute-start | bytes 1474568 | tf_op jit(solution)/shard_map/ppermute | solution.py:38
  (42 other events, 326.3 us)
Sparse Core Ops, SparseCore 0:
  33.5 79.3 all-gather.5
  118.5 130.1 all-gather.3
  308.0 155.1 all-reduce.3

commit v5 on v4

--- a/solution.py
+++ b/solution.py
@@ -516,14 +516,13 @@
 
     attn_out, branch_part, log_total = attend_forward(queries, keys, values, out_weight, seg_ids)
     branch = scatter_sum(branch_part.reshape(plane, rows, width))
-    branch, grad_slices = meet(branch, grad_slices)
     residual = own_rows(block_input).astype(f32) + branch
     resid_inv = lax.rsqrt(jnp.mean(residual * residual, axis=-1, keepdims=True) + epsilon)
     gain_ffn = ffn_gain.astype(f32)
     hidden_block = (residual * resid_inv * gain_ffn).astype(bf16)
+    hidden_block, grad_slices = meet(hidden_block, grad_slices)
     hidden_in = gather_plane(hidden_block)
     if all_tokens:
-        hidden_block, grad_slices = meet(hidden_block, grad_slices)
         hidden_all = lax.all_gather(hidden_block, ("dp", "section", "tensor"), axis=0, tiled=True)
         grad_near = other_groups(grad_slices)
         grad_near, hidden_in = meet(grad_near, hidden_in)

time: 497 us -> 494 us (level)
  local copies, waits for them, and re-layouts: 39.4 us -> 33.8 us
    ppermute x15, waiting for transfers between devices: 66 us -> 73.2 us  [swap_high(): return lax.ppermute(value, 'tensor', SWAP_HIGH)]
  transfers between devices with their start and end apart: 62 -> 62, of which waited for: 30 -> 33; matrix products, arithmetic and copies ran while one was open for 18% -> 18% of each run, Pallas kernels for 32% -> 32%
where the time goes in v5:
time: 494 us; the launch traced here: 486 us
  waiting for transfers between devices  161 us (33%)
  Pallas kernels  157 us (32%)
  starting transfers between devices  55.6 us (11%)
  other arithmetic  44.4 us (9%)
  local copies, waits for them, and re-layouts  33.8 us (7%)
  matrix products  18 us (4%)
  between operations  16.4 us (3%)
    pallas_call x1, Pallas kernels, feed_forward_grads(): pl.pallas_call(kernel, out_shape=[jax.ShapeDtypeStruct((units, width), f3...  85.8 us
    ppermute x15, waiting for transfers between devices, swap_high(): return lax.ppermute(value, 'tensor', SWAP_HIGH)  73.2 us
    ppermute x16, waiting for transfers between devices, swap_section(): return lax.ppermute(value, 'section', SWAP_SECTION)  43 us
    ppermute x16, starting transfers between devices, swap_section(): return lax.ppermute(value, 'section', SWAP_SECTION)  20.5 us
    ppermute x15, starting transfers between devices, swap_high(): return lax.ppermute(value, 'tensor', SWAP_HIGH)  19.4 us
    pallas_call x1, Pallas kernels, feed_forward_own(): pl.pallas_call(kernel, out_shape=[jax.ShapeDtypeStruct((tok_count, units)...  18.1 us
    dot_general x3, matrix products, dot(): lax.dot_general(left, right, (((left_dim,), (right_dim,)), ((), ())), pre...  18 us
    pallas_call x1, Pallas kernels, input_gradient(): pl.pallas_call(kernel, out_shape=[jax.ShapeDtypeStruct((parts, tok_count,...  13.9 us
  transfers between devices with their start and end apart: 62, of which 33 were waited for; matrix products, arithmetic and copies ran while one was open for 18% of the time, Pallas kernels for 32%

profile of v5, /device:TPU:0, one launch (start us, length us, event | category | flops | bytes accessed | tf_op | source)
XLA Modules:
  0.0 486.4 jit_solution(7192445592805375478)
XLA Ops:
  11.9 3.0 dynamic-slice_bitcast_fusion.4
  14.9 9.1 %normed_projections.1 = (bf16[960,2048]{1,0:T(8,128)(2,1)}, bf16[2,960,256]{2,1,0:T(8,128)(2,1)}, bf16[2,960,256]{2,1,0:T(8,128)(2,1)}) custom-call(bf16[960,2048]{1,0:T(8,128)(2,1)} %inputs_ref.1, f32[1,2048]{1,0:T(1,128)} %convert_element_type.229.gain_ref, bf16[2,2048,512]{2,1,0:T(8,128)(2,1)} %bitcast.152), custom_call_target="tpu_custom_call" | custom-call | tf_op jit(solution)/shard_map/normed_projections/pallas_call | solution.py:275
  25.9 6.6 %collective-permute-start.1 = (bf16[960,256]{1,0:T(8,128)(2,1)}, bf16[960,256]{1,0:T(8,128)(2,1)}, u32[]{:S(2)}, u32[]{:S(2)}) collective-permute-start(bf16[960,256]{1,0:T(8,128)(2,1)} %slice_bitcast_fusion.1), channel_id=1, source_target_pairs={{0,16},{1,17},{2,18},{3,19},{4,20},{5,21},{6,22},{7,23},{8,24},{9,... | collective-permute-start | bytes 1474568 | tf_op jit(solution)/shard_map/ppermute | solution.py:510
  35.6 8.0 %collective-permute-done.1 = bf16[960,256]{1,0:T(8,128)(2,1)} collective-permute-done((bf16[960,256]{1,0:T(8,128)(2,1)}, bf16[960,256]{1,0:T(8,128)(2,1)}, u32[]{:S(2)}, u32[]{:S(2)}) %collective-permute-start.1) | collective-permute-done | bytes 491552 | tf_op jit(solution)/shard_map/ppermute | solution.py:510
  45.5 7.5 %collective-permute-done = bf16[960,256]{1,0:T(8,128)(2,1)} collective-permute-done((bf16[960,256]{1,0:T(8,128)(2,1)}, bf16[960,256]{1,0:T(8,128)(2,1)}, u32[]{:S(2)}, u32[]{:S(2)}) %collective-permute-start) | collective-permute-done | bytes 491552 | tf_op jit(solution)/shard_map/ppermute | solution.py:38
  53.0 2.0 bitcast_select_fusion.1
  55.1 2.3 slice_select_fusion.weight_ref
  57.4 9.7 %attend_forward.1 = (bf16[960,256]{1,0:T(8,128)(2,1)}, bf16[960,2048]{1,0:T(8,128)(2,1)}, f32[2,960,1]{2,1,0:T(8,128)}) custom-call(bf16[960,256]{1,0:T(8,128)(2,1)} %get-tuple-element.188.q_ref, bf16[960,256]{1,0:T(8,128)(2,1)} %get-tuple-element.187.k_ref, bf16[960,256]{1,0:T(8,128)(2,1)} %bitcast_select_fusion.v_ref, ...), custom_call_target="tpu_custom_call" | custom-call | tf_op jit(solution)/shard_map/attend_forward/pallas_call | solution.py:316
  68.9 4.0 collective-permute-done.3
  73.0 2.9 fusion.3
  77.5 2.4 collective-permute-start.4
  79.8 4.3 collective-permute-done.6
  85.0 2.3 collective-permute-start.7
  88.8 9.5 %collective-permute-done.7 = bf16[120,2048]{1,0:T(8,128)(2,1)S(1)} collective-permute-done((bf16[120,2048]{1,0:T(8,128)(2,1)}, bf16[120,2048]{1,0:T(8,128)(2,1)S(1)}, u32[]{:S(2)}, u32[]{:S(2)}) %collective-permute-start.7) | collective-permute-done | bytes 491552 | tf_op jit(solution)/shard_map/ppermute | solution.py:34
  99.9 2.2 multiply_reduce_fusion.4
  103.0 10.9 %all-gather.6.cloned.1.call-done = bf16[960,2048]{1,0:T(8,128)(2,1)} async-done(((bf16[240,2048]{1,0:T(8,128)(2,1)}), bf16[960,2048]{1,0:T(8,128)(2,1)}) %all-gather.6.cloned.1.call-update) | async-done | bytes 3932176 | tf_op jit(solution)/shard_map/all_gather | solution.py:500
  116.0 7.8 %fusion.27.back_ref = f32[960,688]{1,0:T(8,128)} fusion(bf16[960,2048]{1,0:T(8,128)(2,1)} %param.10, bf16[688,2048]{1,0:T(8,128)(2,1)} %refs_15_.1), kind=kOutput, calls=%fused_computation.141 | convolution fusion | flops 2705326080 | bytes 9392128 | tf_op jit(solution)/shard_map/dot_general | solution.py:137
  125.3 3.5 constant_dynamic-slice_fusion.1
  130.5 9.5 %collective-permute-done.11 = bf16[120,2048]{1,0:T(8,128)(2,1)S(1)} collective-permute-done((bf16[120,2048]{1,0:T(8,128)(2,1)S(1)}, bf16[120,2048]{1,0:T(8,128)(2,1)S(1)}, u32[]{:S(2)}, u32[]{:S(2)}) %collective-permute-start.11) | collective-permute-done | bytes 491552 | tf_op jit(solution)/shard_map/ppermute | solution.py:34
  142.3 4.9 %collective-permute-done.15 = bf16[120,1024]{1,0:T(8,128)(2,1)S(1)} collective-permute-done((bf16[120,1024]{1,0:T(8,128)(2,1)S(1)}, bf16[120,1024]{1,0:T(8,128)(2,1)S(1)}, u32[]{:S(2)}, u32[]{:S(2)}) %collective-permute-start.15) | collective-permute-done | bytes 245792 | tf_op jit(solution)/shard_map/ppermute | solution.py:38
  151.1 18.1 %feed_forward_own.1 = (bf16[960,688]{1,0:T(8,128)(2,1)}, bf16[960,2048]{1,0:T(8,128)(2,1)}) custom-call(bf16[960,2048]{1,0:T(8,128)(2,1)} %copy-done.2, f32[960,688]{1,0:T(8,128)} %fusion.27.back_ref, bf16[688,2048]{1,0:T(8,128)(2,1)} %bitcast.158, bf16[688,2048]{1,0:T(8,128)(2,1)} %bitcast.160), custom_call_target="tpu_custom_call" | custom-call | tf_op jit(solution)/shard_map/feed_forward_own/pallas_call | solution.py:378
  171.3 3.8 collective-permute-done.17
  179.4 8.8 %output_parts.1 = bf16[8,960,256]{2,1,0:T(8,128)(2,1)} custom-call(bf16[960,688]{1,0:T(8,128)(2,1)} %get-tuple-element.91.hidden_ref, bf16[688,2048]{1,0:T(8,128)(2,1)} %refs_15_.1), custom_call_target="tpu_custom_call" | custom-call | tf_op jit(solution)/shard_map/output_parts/pallas_call | solution.py:430
  193.6 22.0 %collective-permute-done.22 = bf16[120,2048]{1,0:T(8,128)(2,1)S(1)} collective-permute-done((bf16[120,2048]{1,0:T(8,128)(2,1)S(1)}, bf16[120,2048]{1,0:T(8,128)(2,1)S(1)}, u32[]{:S(2)}, u32[]{:S(2)}) %collective-permute-start.22) | collective-permute-done | bytes 491552 | tf_op jit(solution)/shard_map/ppermute | solution.py:34
  216.7 2.5 constant_dynamic-update-slice_fusion.7
  224.7 9.7 %collective-permute-done.24 = bf16[120,2048]{1,0:T(8,128)(2,1)S(1)} collective-permute-done((bf16[120,2048]{1,0:T(8,128)(2,1)S(1)}, bf16[120,2048]{1,0:T(8,128)(2,1)S(1)}, u32[]{:S(2)}, u32[]{:S(2)}) %collective-permute-start.24) | collective-permute-done | bytes 491552 | tf_op jit(solution)/shard_map/ppermute | solution.py:38
  234.4 2.9 dynamic-slice_bitcast_fusion.1
  240.2 5.9 %collective-permute-done.28 = bf16[120,1024]{1,0:T(8,128)(2,1)S(1)} collective-permute-done((bf16[120,1024]{1,0:T(8,128)(2,1)S(1)}, bf16[120,1024]{1,0:T(8,128)(2,1)S(1)}, u32[]{:S(2)}, u32[]{:S(2)}) %collective-permute-start.28) | collective-permute-done | bytes 245792 | tf_op jit(solution)/shard_map/ppermute | solution.py:34
  250.2 11.9 %attend_backward.1 = (bf16[960,256]{1,0:T(8,128)(2,1)}, bf16[960,256]{1,0:T(8,128)(2,1)}, bf16[960,256]{1,0:T(8,128)(2,1)}) custom-call(bf16[960,256]{1,0:T(8,128)(2,1)} %get-tuple-element.188.q_ref, bf16[960,256]{1,0:T(8,128)(2,1)} %get-tuple-element.187.k_ref, bf16[960,256]{1,0:T(8,128)(2,1)} %bitcast_select_fusion.v_ref, ...), custom_call_target="tpu_custom_call" | custom-call | tf_op jit(solution)/shard_map/attend_backward/pallas_call | solution.py:350
  263.0 2.2 collective-permute-start.36
  267.7 3.3 fusion.1
  270.9 6.2 %collective-permute-done.36 = bf16[960,256]{1,0:T(8,128)(2,1)} collective-permute-done((bf16[960,256]{1,0:T(8,128)(2,1)}, bf16[960,256]{1,0:T(8,128)(2,1)}, u32[]{:S(2)}, u32[]{:S(2)}) %collective-permute-start.36) | collective-permute-done | bytes 491552 | tf_op jit(solution)/shard_map/ppermute | solution.py:38
  280.6 6.4 %fusion.7 = bf16[2048,512]{1,0:T(8,128)(2,1)} fusion(bf16[960,2048]{1,0:T(8,128)(2,1)} %get-tuple-element.93, bf16[960,2048]{1,0:T(8,128)(2,1)S(1)} %copy-done.1, pred[]{:T(512)S(6)} %eq.24, bf16[960,256]{1,0:T(8,128)(2,1)S(1)} %get-tuple-element.184, bf16[960,256]{1,0:T(8,128)(2,1)S(1)} %get-tuple-element.183), kind=kOutput, calls=%fused_computation.12 | convolution fusion | flops 2018246656 | bytes 10944513 | tf_op jit(solution)/shard_map/dot_general | solution.py:137
  287.1 3.3 collective-permute-done.34.refs_4_
  291.5 10.5 %collective-permute-done.35.refs_6_ = bf16[1,240,2048]{2,1,0:T(8,128)(2,1)} collective-permute-done((bf16[1,240,2048]{2,1,0:T(8,128)(2,1)S(1)}, bf16[1,240,2048]{2,1,0:T(8,128)(2,1)}, u32[]{:S(2)}, u32[]{:S(2)}) %collective-permute-start.35) | collective-permute-done | bytes 983072 | tf_op jit(solution)/shard_map/ppermute | solution.py:34
  303.0 3.8 convolution_convert_fusion
  309.7 2.6 broadcast_select_fusion.value_ref
  313.3 85.8 %feed_forward_grads.1 = (f32[688,2048]{1,0:T(8,128)}, f32[688,2048]{1,0:T(8,128)}, f32[688,2048]{1,0:T(8,128)}) custom-call(s32[16]{0:T(128)} %stack.88.order_ref, bf16[16,240,2048]{2,1,0:T(8,128)(2,1)} %bitcast.157, bf16[4,240,2048]{2,1,0:T(8,128)(2,1)} %bitcast.162, bf16[1,240,2048]{2,1,0:T(8,128)(2,1)} %get-tuple-element.121.refs_1_, ...), custom_call_target="tpu_custom_call" | custom-call | tf_op jit(solution)/shard_map/feed_forward_grads/pallas_call | solution.py:230
  400.0 13.9 %input_gradient.1 = (bf16[8,960,256]{2,1,0:T(8,128)(2,1)}, f32[1,2048]{1,0:T(1,128)}) custom-call(bf16[960,2048]{1,0:T(8,128)(2,1)} %inputs_ref.1, f32[1,2048]{1,0:T(1,128)} %convert_element_type.229.gain_ref, bf16[960,512]{1,0:T(8,128)(2,1)} %pad_maximum_fusion.first_ref, bf16[960,512]{1,0:T(8,128)(2,1)} %broadcast_select_fusion.value_ref, ...), custom_call_target="tpu_custom_call" | custom-call | tf_op jit(solution)/shard_map/input_gradient/pallas_call | solution.py:412
  415.9 3.0 dynamic-slice_bitcast_fusion
  424.0 9.6 %collective-permute-done.46 = bf16[960,256]{1,0:T(8,128)(2,1)S(1)} collective-permute-done((bf16[960,256]{1,0:T(8,128)(2,1)}, bf16[960,256]{1,0:T(8,128)(2,1)S(1)}, u32[]{:S(2)}, u32[]{:S(2)}) %collective-permute-start.46) | collective-permute-done | bytes 491552 | tf_op jit(solution)/shard_map/ppermute | solution.py:34
  433.7 2.4 collective-permute-done.45
  445.7 2.2 collective-permute-done.53
  447.9 2.4 collective-permute-done.52
  450.3 9.9 %all-reduce.4.cloned.1.call-done = (bf16[2048,512]{1,0:T(8,128)(2,1)}, bf16[2048,512]{1,0:T(8,128)(2,1)}) async-done(((bf16[2048,512]{1,0:T(8,128)(2,1)}, bf16[2048,512]{1,0:T(8,128)(2,1)}), (bf16[2048,512]{1,0:T(8,128)(2,1)}, bf16[2048,512]{1,0:T(8,128)(2,1)})) %all-reduce.4.cloned.1.call-update) | async-done | bytes 4194320 | tf_op jit(solution)/shard_map/psum | solution.py:615
  461.8 2.9 collective-permute-start.56
  468.1 3.9 maximum_convert_fusion
  474.5 2.7 collective-permute-done.55
  (265 shorter events, 95.0 us)
Async XLA Ops:
  7.2 106.7 %all-gather.6.cloned.1.call-start = ((), (), s32[]{:S(2)}) async-start(), calls=%async_computation.1 | async-start | bytes 4915200 | tf_op jit(solution)/shard_map/all_gather | solution.py:500
  10.0 45.1 %collective-permute-start.2 = (bf16[2048,256]{1,0:T(8,128)(2,1)}, bf16[2048,256]{1,0:T(8,128)(2,1)}, u32[]{:S(2)}, u32[]{:S(2)}) collective-permute-start(bf16[2048,256]{1,0:T(8,128)(2,1)} %slice.150), channel_id=1, source_target_pairs={{16,0},{17,1},{18,2},{19,3},{20,4},{21,5},{22,6},{23,7},{24,8},{25... | collective-permute-start | bytes 3145736 | tf_op jit(solution)/shard_map/ppermute | solution.py:511
  25.9 17.7 %collective-permute-start.1 = (bf16[960,256]{1,0:T(8,128)(2,1)}, bf16[960,256]{1,0:T(8,128)(2,1)}, u32[]{:S(2)}, u32[]{:S(2)}) collective-permute-start(bf16[960,256]{1,0:T(8,128)(2,1)} %slice_bitcast_fusion.1), channel_id=1, source_target_pairs={{0,16},{1,17},{2,18},{3,19},{4,20},{5,21},{6,22},{7,23},{8,24},{9,... | collective-permute-start | bytes 1474568 | tf_op jit(solution)/shard_map/ppermute | solution.py:510
  34.3 18.7 %collective-permute-start = (bf16[960,256]{1,0:T(8,128)(2,1)}, bf16[960,256]{1,0:T(8,128)(2,1)}, u32[]{:S(2)}, u32[]{:S(2)}) collective-permute-start(bf16[960,256]{1,0:T(8,128)(2,1)} %dynamic-slice_bitcast_fusion.20), channel_id=1, source_target_pairs={{0,16},{16,0},{1,17},{17,1},{2,18},{18,2},{3,19},{19,3},{4,20},{20... | collective-permute-start | bytes 1474568 | tf_op jit(solution)/shard_map/ppermute | solution.py:38
  34.3 272.4 %all-gather.4.cloned.1.call-start = ((), (), s32[]{:S(2)}) async-start(), calls=%async_computation | async-start | bytes 16220160 | tf_op jit(solution)/shard_map/all_gather | solution.py:526
  76.1 8.1 %collective-permute-start.6 = (bf16[120,1024]{1,0:T(8,128)(2,1)S(1)}, bf16[120,1024]{1,0:T(8,128)(2,1)S(1)}, u32[]{:S(2)}, u32[]{:S(2)}) collective-permute-start(bf16[120,1024]{1,0:T(8,128)(2,1)S(1)} %get-tuple-element.196), channel_id=1, source_target_pairs={{0,16},{16,0},{1,17},{17,1},{2,18},{18,2},{3,19},{19,3},{4,20},{20... | collective-permute-start | bytes 737288 | tf_op jit(solution)/shard_map/ppermute | solution.py:38
  77.5 9.9 %collective-permute-start.4 = (bf16[120,1024]{1,0:T(8,128)(2,1)S(1)}, bf16[120,1024]{1,0:T(8,128)(2,1)S(1)}, u32[]{:S(2)}, u32[]{:S(2)}) collective-permute-start(bf16[120,1024]{1,0:T(8,128)(2,1)S(1)} %get-tuple-element.195), channel_id=1, source_target_pairs={{0,2},{1,3},{2,0},{3,1},{4,6},{5,7},{6,4},{7,5},{8,10},{9,11},{10,... | collective-permute-start | bytes 737288 | tf_op jit(solution)/shard_map/ppermute | solution.py:34
  85.0 13.3 %collective-permute-start.7 = (bf16[120,2048]{1,0:T(8,128)(2,1)}, bf16[120,2048]{1,0:T(8,128)(2,1)S(1)}, u32[]{:S(2)}, u32[]{:S(2)}) collective-permute-start(bf16[120,2048]{1,0:T(8,128)(2,1)} %pad_maximum_fusion.4), channel_id=1, source_target_pairs={{0,2},{1,3},{2,0},{3,1},{4,6},{5,7},{6,4},{7,5},{8,10},{9,11},{10,... | collective-permute-start | bytes 1474568 | tf_op jit(solution)/shard_map/ppermute | solution.py:34
  87.5 12.4 %collective-permute-start.5 = (bf16[120,2048]{1,0:T(8,128)(2,1)S(1)}, bf16[120,2048]{1,0:T(8,128)(2,1)}, u32[]{:S(2)}, u32[]{:S(2)}) collective-permute-start(bf16[120,2048]{1,0:T(8,128)(2,1)S(1)} %pad_maximum_fusion.3), channel_id=1, source_target_pairs={{0,16},{16,0},{1,17},{17,1},{2,18},{18,2},{3,19},{19,3},{4,20},{20... | collective-permute-start | bytes 1474568 | tf_op jit(solution)/shard_map/ppermute | solution.py:38
  113.9 346.3 %all-reduce.4.cloned.1.call-start = ((), (), s32[]{:S(2)}) async-start(), calls=%async_computation.2 | async-start | bytes 8388608 | tf_op jit(solution)/shard_map/psum | solution.py:615
  114.4 15.5 %collective-permute-start.9 = (bf16[120,2048]{1,0:T(8,128)(2,1)}, bf16[120,2048]{1,0:T(8,128)(2,1)S(1)}, u32[]{:S(2)}, u32[]{:S(2)}) collective-permute-start(bf16[120,2048]{1,0:T(8,128)(2,1)} %multiply_convert_fusion), channel_id=1, source_target_pairs={{0,16},{16,0},{1,17},{17,1},{2,18},{18,2},{3,19},{19,3},{4,20},{20... | collective-permute-start | bytes 1474568 | tf_op jit(solution)/shard_map/ppermute | solution.py:38
  123.8 16.2 %collective-permute-start.11 = (bf16[120,2048]{1,0:T(8,128)(2,1)S(1)}, bf16[120,2048]{1,0:T(8,128)(2,1)S(1)}, u32[]{:S(2)}, u32[]{:S(2)}) collective-permute-start(bf16[120,2048]{1,0:T(8,128)(2,1)S(1)} %copy-done.3), channel_id=1, source_target_pairs={{0,2},{1,3},{2,0},{3,1},{4,6},{5,7},{6,4},{7,5},{8,10},{9,11},{10,... | collective-permute-start | bytes 1474568 | tf_op jit(solution)/shard_map/ppermute | solution.py:34
  125.3 16.9 %collective-permute-start.8 = (bf16[120,2048]{1,0:T(8,128)(2,1)S(1)}, bf16[120,2048]{1,0:T(8,128)(2,1)S(1)}, u32[]{:S(2)}, u32[]{:S(2)}) collective-permute-start(bf16[120,2048]{1,0:T(8,128)(2,1)S(1)} %copy-done.3), channel_id=1, source_target_pairs={{0,1},{1,0},{2,3},{3,2},{4,5},{5,4},{6,7},{7,6},{8,9},{9,8},{10,11... | collective-permute-start | bytes 1474568 | tf_op jit(solution)/shard_map/ppermute | solution.py:30
  129.9 17.8 %collective-permute-start.10 = (bf16[120,2048]{1,0:T(8,128)(2,1)S(1)}, bf16[120,2048]{1,0:T(8,128)(2,1)S(1)}, u32[]{:S(2)}, u32[]{:S(2)}) collective-permute-start(bf16[120,2048]{1,0:T(8,128)(2,1)S(1)} %collective-permute-done.9), channel_id=1, source_target_pairs={{0,1},{1,0},{2,3},{3,2},{4,5},{5,4},{6,7},{7,6},{8,9},{9,8},{10,11... | collective-permute-start | bytes 1474568 | tf_op jit(solution)/shard_map/ppermute | solution.py:30
  176.2 13.1 %collective-permute-start.19 = (bf16[120,1024]{1,0:T(8,128)(2,1)S(1)}, bf16[120,1024]{1,0:T(8,128)(2,1)S(1)}, u32[]{:S(2)}, u32[]{:S(2)}) collective-permute-start(bf16[120,1024]{1,0:T(8,128)(2,1)S(1)} %get-tuple-element.193), channel_id=1, source_target_pairs={{0,2},{1,3},{2,0},{3,1},{4,6},{5,7},{6,4},{7,5},{8,10},{9,11},{10,... | collective-permute-start | bytes 737288 | tf_op jit(solution)/shard_map/ppermute | solution.py:34
  177.9 13.5 %collective-permute-start.18 = (bf16[120,1024]{1,0:T(8,128)(2,1)S(1)}, bf16[120,1024]{1,0:T(8,128)(2,1)S(1)}, u32[]{:S(2)}, u32[]{:S(2)}) collective-permute-start(bf16[120,1024]{1,0:T(8,128)(2,1)S(1)} %get-tuple-element.194), channel_id=1, source_target_pairs={{0,16},{16,0},{1,17},{17,1},{2,18},{18,2},{3,19},{19,3},{4,20},{20... | collective-permute-start | bytes 737288 | tf_op jit(solution)/shard_map/ppermute | solution.py:38
  191.5 24.1 %collective-permute-start.22 = (bf16[120,2048]{1,0:T(8,128)(2,1)S(1)}, bf16[120,2048]{1,0:T(8,128)(2,1)S(1)}, u32[]{:S(2)}, u32[]{:S(2)}) collective-permute-start(bf16[120,2048]{1,0:T(8,128)(2,1)S(1)} %pad_maximum_fusion.6), channel_id=1, source_target_pairs={{0,2},{1,3},{2,0},{3,1},{4,6},{5,7},{6,4},{7,5},{8,10},{9,11},{10,... | collective-permute-start | bytes 1474568 | tf_op jit(solution)/shard_map/ppermute | solution.py:34
  191.7 24.1 %collective-permute-start.21 = (bf16[120,2048]{1,0:T(8,128)(2,1)S(1)}, bf16[120,2048]{1,0:T(8,128)(2,1)S(1)}, u32[]{:S(2)}, u32[]{:S(2)}) collective-permute-start(bf16[120,2048]{1,0:T(8,128)(2,1)S(1)} %pad_maximum_fusion.5), channel_id=1, source_target_pairs={{0,16},{16,0},{1,17},{17,1},{2,18},{18,2},{3,19},{19,3},{4,20},{20... | collective-permute-start | bytes 1474568 | tf_op jit(solution)/shard_map/ppermute | solution.py:38
  219.3 15.1 %collective-permute-start.24 = (bf16[120,2048]{1,0:T(8,128)(2,1)S(1)}, bf16[120,2048]{1,0:T(8,128)(2,1)S(1)}, u32[]{:S(2)}, u32[]{:S(2)}) collective-permute-start(bf16[120,2048]{1,0:T(8,128)(2,1)S(1)} %get-tuple-element.156), channel_id=1, source_target_pairs={{0,16},{16,0},{1,17},{17,1},{2,18},{18,2},{3,19},{19,3},{4,20},{20... | collective-permute-start | bytes 1474568 | tf_op jit(solution)/shard_map/ppermute | solution.py:38
  221.1 17.7 %collective-permute-start.26 = (bf16[120,2048]{1,0:T(8,128)(2,1)S(1)}, bf16[120,2048]{1,0:T(8,128)(2,1)S(1)}, u32[]{:S(2)}, u32[]{:S(2)}) collective-permute-start(bf16[120,2048]{1,0:T(8,128)(2,1)S(1)} %get-tuple-element.156), channel_id=1, source_target_pairs={{0,2},{1,3},{2,0},{3,1},{4,6},{5,7},{6,4},{7,5},{8,10},{9,11},{10,... | collective-permute-start | bytes 1474568 | tf_op jit(solution)/shard_map/ppermute | solution.py:34
  222.8 17.3 %collective-permute-start.23 = (bf16[120,2048]{1,0:T(8,128)(2,1)S(1)}, bf16[120,2048]{1,0:T(8,128)(2,1)S(1)}, u32[]{:S(2)}, u32[]{:S(2)}) collective-permute-start(bf16[120,2048]{1,0:T(8,128)(2,1)S(1)} %get-tuple-element.156), channel_id=1, source_target_pairs={{0,1},{1,0},{2,3},{3,2},{4,5},{5,4},{6,7},{7,6},{8,9},{9,8},{10,11... | collective-permute-start | bytes 1474568 | tf_op jit(solution)/shard_map/ppermute | solution.py:30
  234.4 12.3 %collective-permute-start.25 = (bf16[120,2048]{1,0:T(8,128)(2,1)S(1)}, bf16[120,2048]{1,0:T(8,128)(2,1)S(1)}, u32[]{:S(2)}, u32[]{:S(2)}) collective-permute-start(bf16[120,2048]{1,0:T(8,128)(2,1)S(1)} %collective-permute-done.24), channel_id=1, source_target_pairs={{0,1},{1,0},{2,3},{3,2},{4,5},{5,4},{6,7},{7,6},{8,9},{9,8},{10,11... | collective-permute-start | bytes 1474568 | tf_op jit(solution)/shard_map/ppermute | solution.py:30
  237.4 28.6 %collective-permute-start.20 = (bf16[4,960,256]{2,1,0:T(8,128)(2,1)}, bf16[4,960,256]{2,1,0:T(8,128)(2,1)S(1)}, u32[]{:S(2)}, u32[]{:S(2)}) collective-permute-start(bf16[4,960,256]{2,1,0:T(8,128)(2,1)} %dynamic-slice_bitcast_fusion.1), channel_id=1, source_target_pairs={{0,1},{1,0},{2,3},{3,2},{4,5},{5,4},{6,7},{7,6},{8,9},{9,8},{10,11... | collective-permute-start | bytes 5898248 | tf_op jit(solution)/shard_map/ppermute | solution.py:30
  238.1 7.9 %collective-permute-start.28 = (bf16[120,1024]{1,0:T(8,128)(2,1)S(1)}, bf16[120,1024]{1,0:T(8,128)(2,1)S(1)}, u32[]{:S(2)}, u32[]{:S(2)}) collective-permute-start(bf16[120,1024]{1,0:T(8,128)(2,1)S(1)} %slice.162), channel_id=1, source_target_pairs={{0,2},{1,3},{2,0},{3,1},{4,6},{5,7},{6,4},{7,5},{8,10},{9,11},{10,... | collective-permute-start | bytes 737288 | tf_op jit(solution)/shard_map/ppermute | solution.py:34
  238.7 7.9 %collective-permute-start.30 = (bf16[120,1024]{1,0:T(8,128)(2,1)S(1)}, bf16[120,1024]{1,0:T(8,128)(2,1)S(1)}, u32[]{:S(2)}, u32[]{:S(2)}) collective-permute-start(bf16[120,1024]{1,0:T(8,128)(2,1)S(1)} %slice.163), channel_id=1, source_target_pairs={{0,16},{16,0},{1,17},{17,1},{2,18},{18,2},{3,19},{19,3},{4,20},{20... | collective-permute-start | bytes 737288 | tf_op jit(solution)/shard_map/ppermute | solution.py:38
  248.3 30.0 %collective-permute-start.32 = (bf16[1,240,2048]{2,1,0:T(8,128)(2,1)}, bf16[1,240,2048]{2,1,0:T(8,128)(2,1)}, u32[]{:S(2)}, u32[]{:S(2)}) collective-permute-start(bf16[1,240,2048]{2,1,0:T(8,128)(2,1)} %get-tuple-element.106.refs_2_), channel_id=1, source_target_pairs={{0,2},{1,3},{2,0},{3,1},{4,6},{5,7},{6,4},{7,5},{8,10},{9,11},{10,... | collective-permute-start | bytes 2949128 | tf_op jit(solution)/shard_map/ppermute | solution.py:34
  263.0 14.2 %collective-permute-start.36 = (bf16[960,256]{1,0:T(8,128)(2,1)}, bf16[960,256]{1,0:T(8,128)(2,1)}, u32[]{:S(2)}, u32[]{:S(2)}) collective-permute-start(bf16[960,256]{1,0:T(8,128)(2,1)} %broadcast_select_fusion.3), channel_id=1, source_target_pairs={{0,16},{16,0},{1,17},{17,1},{2,18},{18,2},{3,19},{19,3},{4,20},{20... | collective-permute-start | bytes 1474568 | tf_op jit(solution)/shard_map/ppermute | solution.py:38
  265.8 42.0 %collective-permute-start.40 = (bf16[1,240,2048]{2,1,0:T(8,128)(2,1)}, bf16[1,240,2048]{2,1,0:T(8,128)(2,1)}, u32[]{:S(2)}, u32[]{:S(2)}) collective-permute-start(bf16[1,240,2048]{2,1,0:T(8,128)(2,1)} %get-tuple-element.106.refs_2_), channel_id=1, source_target_pairs={{0,1},{1,0},{2,3},{3,2},{4,5},{5,4},{6,7},{7,6},{8,9},{9,8},{10,11... | collective-permute-start | bytes 2949128 | tf_op jit(solution)/shard_map/ppermute | solution.py:30
  265.9 24.5 %collective-permute-start.34 = (bf16[1,240,2048]{2,1,0:T(8,128)(2,1)}, bf16[1,240,2048]{2,1,0:T(8,128)(2,1)}, u32[]{:S(2)}, u32[]{:S(2)}) collective-permute-start(bf16[1,240,2048]{2,1,0:T(8,128)(2,1)} %get-tuple-element.111), channel_id=1, source_target_pairs={{0,4},{4,0},{8,12},{12,8},{1,5},{5,1},{9,13},{13,9},{2,6},{6,2},{1... | collective-permute-start | bytes 2949128 | tf_op jit(solution)/shard_map/ppermute | solution.py:552
  267.2 35.4 %collective-permute-start.39 = (bf16[1,240,2048]{2,1,0:T(8,128)(2,1)}, bf16[1,240,2048]{2,1,0:T(8,128)(2,1)}, u32[]{:S(2)}, u32[]{:S(2)}) collective-permute-start(bf16[1,240,2048]{2,1,0:T(8,128)(2,1)} %get-tuple-element.121.refs_1_), channel_id=1, source_target_pairs={{0,1},{1,0},{2,3},{3,2},{4,5},{5,4},{6,7},{7,6},{8,9},{9,8},{10,11... | collective-permute-start | bytes 2949128 | tf_op jit(solution)/shard_map/ppermute | solution.py:30
  278.3 23.6 %collective-permute-start.35 = (bf16[1,240,2048]{2,1,0:T(8,128)(2,1)S(1)}, bf16[1,240,2048]{2,1,0:T(8,128)(2,1)}, u32[]{:S(2)}, u32[]{:S(2)}) collective-permute-start(bf16[1,240,2048]{2,1,0:T(8,128)(2,1)S(1)} %copy-done.6), channel_id=1, source_target_pairs={{0,2},{1,3},{2,0},{3,1},{4,6},{5,7},{6,4},{7,5},{8,10},{9,11},{10,... | collective-permute-start | bytes 2949128 | tf_op jit(solution)/shard_map/ppermute | solution.py:34
  279.0 12.5 %collective-permute-start.33 = (bf16[960,256]{1,0:T(8,128)(2,1)S(1)}, bf16[960,256]{1,0:T(8,128)(2,1)S(1)}, u32[]{:S(2)}, u32[]{:S(2)}) collective-permute-start(bf16[960,256]{1,0:T(8,128)(2,1)S(1)} %broadcast_select_fusion.7), channel_id=1, source_target_pairs={{0,16},{16,0},{1,17},{17,1},{2,18},{18,2},{3,19},{19,3},{4,20},{20... | collective-permute-start | bytes 1474568 | tf_op jit(solution)/shard_map/ppermute | solution.py:38
  290.3 17.8 %collective-permute-start.41 = (bf16[1,240,2048]{2,1,0:T(8,128)(2,1)S(1)}, bf16[1,240,2048]{2,1,0:T(8,128)(2,1)}, u32[]{:S(2)}, u32[]{:S(2)}) collective-permute-start(bf16[1,240,2048]{2,1,0:T(8,128)(2,1)S(1)} %copy-done.6), channel_id=1, source_target_pairs={{0,1},{1,0},{2,3},{3,2},{4,5},{5,4},{6,7},{7,6},{8,9},{9,8},{10,11... | collective-permute-start | bytes 2949128 | tf_op jit(solution)/shard_map/ppermute | solution.py:30
  302.1 11.3 %collective-permute-start.42 = (bf16[1,240,2048]{2,1,0:T(8,128)(2,1)}, bf16[1,240,2048]{2,1,0:T(8,128)(2,1)}, u32[]{:S(2)}, u32[]{:S(2)}) collective-permute-start(bf16[1,240,2048]{2,1,0:T(8,128)(2,1)} %collective-permute-done.34.refs_4_), channel_id=1, source_target_pairs={{0,1},{1,0},{2,3},{3,2},{4,5},{5,4},{6,7},{7,6},{8,9},{9,8},{10,11... | collective-permute-start | bytes 2949128 | tf_op jit(solution)/shard_map/ppermute | solution.py:30
  302.1 11.2 %collective-permute-start.43 = (bf16[1,240,2048]{2,1,0:T(8,128)(2,1)}, bf16[1,240,2048]{2,1,0:T(8,128)(2,1)}, u32[]{:S(2)}, u32[]{:S(2)}) collective-permute-start(bf16[1,240,2048]{2,1,0:T(8,128)(2,1)} %collective-permute-done.32.refs_5_), channel_id=1, source_target_pairs={{0,1},{1,0},{2,3},{3,2},{4,5},{5,4},{6,7},{7,6},{8,9},{9,8},{10,11... | collective-permute-start | bytes 2949128 | tf_op jit(solution)/shard_map/ppermute | solution.py:30
  302.6 10.7 %collective-permute-start.44 = (bf16[1,240,2048]{2,1,0:T(8,128)(2,1)}, bf16[1,240,2048]{2,1,0:T(8,128)(2,1)}, u32[]{:S(2)}, u32[]{:S(2)}) collective-permute-start(bf16[1,240,2048]{2,1,0:T(8,128)(2,1)} %collective-permute-done.35.refs_6_), channel_id=1, source_target_pairs={{0,1},{1,0},{2,3},{3,2},{4,5},{5,4},{6,7},{7,6},{8,9},{9,8},{10,11... | collective-permute-start | bytes 2949128 | tf_op jit(solution)/shard_map/ppermute | solution.py:30
  307.8 91.4 %collective-permute-start.38 = (bf16[960,128]{1,0:T(8,128)(2,1)S(1)}, bf16[960,128]{1,0:T(8,128)(2,1)S(1)}, u32[]{:S(2)}, u32[]{:S(2)}) collective-permute-start(bf16[960,128]{1,0:T(8,128)(2,1)S(1)} %get-tuple-element.191), channel_id=1, source_target_pairs={{0,2},{1,3},{2,0},{3,1},{4,6},{5,7},{6,4},{7,5},{8,10},{9,11},{10,... | collective-permute-start | bytes 737288 | tf_op jit(solution)/shard_map/ppermute | solution.py:34
  308.1 91.1 %collective-permute-start.37 = (bf16[960,128]{1,0:T(8,128)(2,1)S(1)}, bf16[960,128]{1,0:T(8,128)(2,1)S(1)}, u32[]{:S(2)}, u32[]{:S(2)}) collective-permute-start(bf16[960,128]{1,0:T(8,128)(2,1)S(1)} %get-tuple-element.192), channel_id=1, source_target_pairs={{0,16},{16,0},{1,17},{17,1},{2,18},{18,2},{3,19},{19,3},{4,20},{20... | collective-permute-start | bytes 737288 | tf_op jit(solution)/shard_map/ppermute | solution.py:38
  418.8 20.6 %collective-permute-start.47 = (bf16[4,960,256]{2,1,0:T(8,128)(2,1)}, bf16[4,960,256]{2,1,0:T(8,128)(2,1)S(1)}, u32[]{:S(2)}, u32[]{:S(2)}) collective-permute-start(bf16[4,960,256]{2,1,0:T(8,128)(2,1)} %dynamic-slice_bitcast_fusion), channel_id=1, source_target_pairs={{0,1},{1,0},{2,3},{3,2},{4,5},{5,4},{6,7},{7,6},{8,9},{9,8},{10,11... | collective-permute-start | bytes 5898248 | tf_op jit(solution)/shard_map/ppermute | solution.py:30
  419.8 13.8 %collective-permute-start.46 = (bf16[960,256]{1,0:T(8,128)(2,1)}, bf16[960,256]{1,0:T(8,128)(2,1)S(1)}, u32[]{:S(2)}, u32[]{:S(2)}) collective-permute-start(bf16[960,256]{1,0:T(8,128)(2,1)} %pad_maximum_fusion.8), channel_id=1, source_target_pairs={{0,2},{1,3},{2,0},{3,1},{4,6},{5,7},{6,4},{7,5},{8,10},{9,11},{10,... | collective-permute-start | bytes 1474568 | tf_op jit(solution)/shard_map/ppermute | solution.py:34
  422.5 13.6 %collective-permute-start.45 = (bf16[960,256]{1,0:T(8,128)(2,1)}, bf16[960,256]{1,0:T(8,128)(2,1)S(1)}, u32[]{:S(2)}, u32[]{:S(2)}) collective-permute-start(bf16[960,256]{1,0:T(8,128)(2,1)} %pad_maximum_fusion.7), channel_id=1, source_target_pairs={{0,16},{16,0},{1,17},{17,1},{2,18},{18,2},{3,19},{19,3},{4,20},{20... | collective-permute-start | bytes 1474568 | tf_op jit(solution)/shard_map/ppermute | solution.py:38
  441.6 8.7 %collective-permute-start.49 = (bf16[960,128]{1,0:T(8,128)(2,1)S(1)}, bf16[960,128]{1,0:T(8,128)(2,1)S(1)}, u32[]{:S(2)}, u32[]{:S(2)}) collective-permute-start(bf16[960,128]{1,0:T(8,128)(2,1)S(1)} %get-tuple-element.189), channel_id=1, source_target_pairs={{0,2},{1,3},{2,0},{3,1},{4,6},{5,7},{6,4},{7,5},{8,10},{9,11},{10,... | collective-permute-start | bytes 737288 | tf_op jit(solution)/shard_map/ppermute | solution.py:34
  442.0 8.3 %collective-permute-start.48 = (bf16[960,128]{1,0:T(8,128)(2,1)S(1)}, bf16[960,128]{1,0:T(8,128)(2,1)S(1)}, u32[]{:S(2)}, u32[]{:S(2)}) collective-permute-start(bf16[960,128]{1,0:T(8,128)(2,1)S(1)} %get-tuple-element.190), channel_id=1, source_target_pairs={{0,16},{16,0},{1,17},{17,1},{2,18},{18,2},{3,19},{19,3},{4,20},{20... | collective-permute-start | bytes 737288 | tf_op jit(solution)/shard_map/ppermute | solution.py:38
  460.2 11.8 %collective-permute-start.58 = (f32[4,2048]{1,0:T(4,128)S(1)}, f32[4,2048]{1,0:T(4,128)S(1)}, u32[]{:S(2)}, u32[]{:S(2)}) collective-permute-start(f32[4,2048]{1,0:T(4,128)S(1)} %add_add_fusion.1), channel_id=1, source_target_pairs={{0,12},{4,8},{8,4},{12,0},{1,13},{5,9},{9,5},{13,1},{2,14},{6,10},... | collective-permute-start | bytes 98312 | tf_op jit(solution)/shard_map/ppermute | solution.py:459
  461.4 10.7 %collective-permute-start.57 = (f32[4,2048]{1,0:T(4,128)S(1)}, f32[4,2048]{1,0:T(4,128)S(1)}, u32[]{:S(2)}, u32[]{:S(2)}) collective-permute-start(f32[4,2048]{1,0:T(4,128)S(1)} %add_add_fusion.1), channel_id=1, source_target_pairs={{0,8},{4,12},{8,0},{12,4},{1,9},{5,13},{9,1},{13,5},{2,10},{6,14},... | collective-permute-start | bytes 98312 | tf_op jit(solution)/shard_map/ppermute | solution.py:459
  461.8 10.3 %collective-permute-start.56 = (f32[4,2048]{1,0:T(4,128)S(1)}, f32[4,2048]{1,0:T(4,128)S(1)}, u32[]{:S(2)}, u32[]{:S(2)}) collective-permute-start(f32[4,2048]{1,0:T(4,128)S(1)} %add_add_fusion.1), channel_id=1, source_target_pairs={{0,4},{4,0},{8,12},{12,8},{1,5},{5,1},{9,13},{13,9},{2,6},{6,2},{1... | collective-permute-start | bytes 98312 | tf_op jit(solution)/shard_map/ppermute | solution.py:459
  465.0 12.2 %collective-permute-start.55 = (bf16[960,256]{1,0:T(8,128)(2,1)S(1)}, bf16[960,256]{1,0:T(8,128)(2,1)S(1)}, u32[]{:S(2)}, u32[]{:S(2)}) collective-permute-start(bf16[960,256]{1,0:T(8,128)(2,1)S(1)} %pad_maximum_fusion.10), channel_id=1, source_target_pairs={{0,2},{1,3},{2,0},{3,1},{4,6},{5,7},{6,4},{7,5},{8,10},{9,11},{10,... | collective-permute-start | bytes 1474568 | tf_op jit(solution)/shard_map/ppermute | solution.py:34
  466.6 11.9 %collective-permute-start.54 = (bf16[960,256]{1,0:T(8,128)(2,1)S(1)}, bf16[960,256]{1,0:T(8,128)(2,1)S(1)}, u32[]{:S(2)}, u32[]{:S(2)}) collective-permute-start(bf16[960,256]{1,0:T(8,128)(2,1)S(1)} %pad_maximum_fusion.9), channel_id=1, source_target_pairs={{0,16},{16,0},{1,17},{17,1},{2,18},{18,2},{3,19},{19,3},{4,20},{20... | collective-permute-start | bytes 1474568 | tf_op jit(solution)/shard_map/ppermute | solution.py:38
  (47 other events, 383.8 us)
Sparse Core Ops, SparseCore 0:
  34.5 79.3 all-gather.5
  116.8 132.0 all-gather.3
  306.9 153.2 all-reduce.3
